TPU v7x, 128 devices: a whole 4x4x4 slice. The times are simulated.
128 devices in a mesh: expert: 32 (over z, x, y_lo), dp: 4 (over y_hi, core).
Axes of the slice: x: 4, y: 4 (y_hi: 2, y_lo: 2; y = y_hi * 2 + y_lo), z: 4, core: 2. Of those that a mesh axis runs over, the one named last changes fastest.
Arguments:
- tokens: bfloat16 [4096, 5120], P('expert', 'dp'), may hold values from -6 to 6
- cotangent: bfloat16 [4096, 5120], P('expert', 'dp'), may hold values from -6 to 6
- expert_ids: int32 [4096, 6], P('expert'), may hold values from 0 to 159, all different within a row
- route_probs: float32 [4096, 6], P('expert'), may hold values from 0.1 to 1
- w_gate: bfloat16 [32, 5120, 1536], P('expert', None, 'dp'), may hold values from -0.078125 to 0.078125
- w_up: bfloat16 [32, 5120, 1536], P('expert', None, 'dp'), may hold values from -0.078125 to 0.078125
- w_down: bfloat16 [32, 1536, 5120], P('expert', 'dp'), may hold values from -0.15625 to 0.15625
Outputs:
- mixed: bfloat16 [4096, 5120], P('expert', 'dp')
- grad_tokens: bfloat16 [4096, 5120], P('expert', 'dp')
- grad_probs: float32 [4096, 6], P('expert')
- grad_gate: bfloat16 [32, 5120, 1536], P('expert', None, 'dp')
- grad_up: bfloat16 [32, 5120, 1536], P('expert', None, 'dp')
- grad_down: bfloat16 [32, 1536, 5120], P('expert', 'dp')
All inputs are finite; a program needn't handle non-finite values.
Results may differ from a plain program's by a relative error of at most 0.0058.
Values may be sent and summed in bfloat16 or wider, within the bound.
No kernel may reach another device: no remote copies, remote signals or barrier semaphores. Data moves between devices by JAX's collectives and lax.ppermute only.
A program may use at most 192 MiB of HBM per device.

v0:
```python
import jax
import jax.numpy as jnp
from jax import lax
from jax.sharding import PartitionSpec as P

CAP = 12


def expert_pass(rows_in, rows_grad, gate_w, up_w, down_w):
    gate_pre = jnp.dot(rows_in, gate_w, preferred_element_type=jnp.float32)
    up_proj = jnp.dot(rows_in, up_w, preferred_element_type=jnp.float32)
    sigma = jax.nn.sigmoid(gate_pre)
    active = gate_pre * sigma
    hidden = (active * up_proj).astype(jnp.bfloat16)
    result = jnp.dot(hidden, down_w, preferred_element_type=jnp.float32)
    d_hidden = lax.dot_general(
        rows_grad, down_w, (((1,), (1,)), ((), ())), preferred_element_type=jnp.float32
    )
    d_gate = (d_hidden * up_proj * sigma * (1.0 + gate_pre * (1.0 - sigma))).astype(jnp.bfloat16)
    d_up = (d_hidden * active).astype(jnp.bfloat16)
    g_down = lax.dot_general(
        hidden, rows_grad, (((0,), (0,)), ((), ())), preferred_element_type=jnp.float32
    ).astype(jnp.bfloat16)
    g_gate = lax.dot_general(
        rows_in, d_gate, (((0,), (0,)), ((), ())), preferred_element_type=jnp.float32
    ).astype(jnp.bfloat16)
    g_up = lax.dot_general(
        rows_in, d_up, (((0,), (0,)), ((), ())), preferred_element_type=jnp.float32
    ).astype(jnp.bfloat16)
    backward = lax.dot_general(
        d_gate, gate_w, (((1,), (1,)), ((), ())), preferred_element_type=jnp.float32
    )
    backward = backward + lax.dot_general(
        d_up, up_w, (((1,), (1,)), ((), ())), preferred_element_type=jnp.float32
    )
    return (result, backward, g_gate, g_up, g_down)


def slot_rows(source_rows, grad_rows, slot_token, slot_prob, experts, capacity):
    columns = source_rows.shape[1]
    src_pad = jnp.concatenate([source_rows, jnp.zeros((1, columns), source_rows.dtype)], axis=0)
    grad_pad = jnp.concatenate([grad_rows, jnp.zeros((1, columns), grad_rows.dtype)], axis=0)
    picked = src_pad[slot_token].reshape(experts, capacity, columns)
    scaled = (slot_prob[:, None] * grad_pad[slot_token].astype(jnp.float32)).astype(jnp.bfloat16)
    return (picked, scaled.reshape(experts, capacity, columns))


def pick_rows(stacked, slot_of):
    columns = stacked.shape[-1]
    padded = jnp.concatenate(
        [stacked.reshape(-1, columns), jnp.zeros((1, columns), jnp.float32)], axis=0
    )
    return padded[slot_of]


def body(tokens, cotangent, expert_ids, route_probs, w_gate, w_up, w_down):
    experts = lax.axis_size("expert")
    tok_rows = expert_ids.shape[0]
    topk = expert_ids.shape[1]
    capacity = CAP
    entries = tok_rows * topk
    flat = expert_ids.reshape(-1)
    onehot = (flat[:, None] == jnp.arange(experts, dtype=jnp.int32)[None, :]).astype(jnp.int32)
    before = jnp.cumsum(onehot, axis=0) - onehot
    place = jnp.sum(onehot * before, axis=1)
    live = (flat < experts) & (place < capacity)
    empty_slot = experts * capacity
    target = jnp.where(live, flat * capacity + place, empty_slot)
    slot_entry = (
        jnp.full((empty_slot + 1,), entries, jnp.int32)
        .at[target]
        .set(jnp.arange(entries, dtype=jnp.int32))[:-1]
    )
    slot_token = slot_entry // topk
    prob_pad = jnp.concatenate([route_probs.reshape(-1), jnp.zeros((1,), jnp.float32)], axis=0)
    slot_prob = prob_pad[slot_entry]
    whole_tokens, whole_cot = (
        lax.all_gather(tokens, "dp", axis=1, tiled=True),
        lax.all_gather(cotangent, "dp", axis=1, tiled=True),
    )
    send_in, send_grad = slot_rows(
        whole_tokens, whole_cot, slot_token, slot_prob, experts, capacity
    )
    recv_in, recv_grad = (
        lax.all_to_all(send_in, "expert", split_axis=0, concat_axis=0, tiled=True),
        lax.all_to_all(send_grad, "expert", split_axis=0, concat_axis=0, tiled=True),
    )
    width = recv_in.shape[2]
    result, backward, g_gate, g_up, g_down = expert_pass(
        recv_in.reshape(-1, width), recv_grad.reshape(-1, width), w_gate[0], w_up[0], w_down[0]
    )
    result3 = result.reshape(experts, capacity, width)
    backward3 = backward.reshape(experts, capacity, width)
    slot_of = jnp.where(live, target, empty_slot)
    owner_result, owner_back = (
        lax.psum_scatter(result3, "dp", scatter_dimension=2, tiled=True),
        lax.psum_scatter(backward3, "dp", scatter_dimension=2, tiled=True),
    )
    home_result, home_back = (
        lax.all_to_all(owner_result, "expert", split_axis=0, concat_axis=0, tiled=True),
        lax.all_to_all(owner_back, "expert", split_axis=0, concat_axis=0, tiled=True),
    )
    entry_slice = pick_rows(home_result, slot_of)
    narrow = entry_slice.shape[1]
    back_slice = jnp.sum(pick_rows(home_back, slot_of).reshape(tok_rows, topk, narrow), axis=1)
    narrow = entry_slice.shape[1]
    entry_three = entry_slice.reshape(tok_rows, topk, narrow)
    mixed = jnp.sum(route_probs[:, :, None] * entry_three, axis=1).astype(jnp.bfloat16)
    inner_part = jnp.sum(cotangent.astype(jnp.float32)[:, None, :] * entry_three, axis=2)
    grad_probs = lax.psum(inner_part, "dp")
    grad_tokens = back_slice.astype(jnp.bfloat16)
    return (mixed, grad_tokens, grad_probs, g_gate[None], g_up[None], g_down[None])


def solution(mesh):
    return jax.shard_map(
        body,
        mesh=mesh,
        in_specs=(
            P("expert", "dp"),
            P("expert", "dp"),
            P("expert", None),
            P("expert", None),
            P("expert", None, "dp"),
            P("expert", None, "dp"),
            P("expert", "dp", None),
        ),
        out_specs=(
            P("expert", "dp"),
            P("expert", "dp"),
            P("expert", None),
            P("expert", None, "dp"),
            P("expert", None, "dp"),
            P("expert", "dp", None),
        ),
        check_vma=False,
    )
```

profile of v0, /device:TPU:0, one launch (start us, length us, event | category | flops | bytes accessed | tf_op | source)
XLA Modules:
  0.0 527.1 jit_solution(11416133389755261633)
XLA Ops:
  7.2 0.7 all-gather.3.cloned.1.call-update
  7.9 0.8 copy.26
  8.7 0.1 eq.29
  8.8 0.1 eq.25
  9.0 1.7 reduce-window.6
  10.7 0.3 slice_reduce_fusion
  11.0 0.7 broadcast_multiply_fusion
  11.7 0.1 copy.29
  11.8 0.1 mul.75
  12.0 0.7 broadcast_compare_fusion
  12.7 0.1 copy.25
  12.8 0.2 lt.64
  13.0 0.1 fusion.18
  13.1 3.4 scatter_custom_fusion
  16.5 17.9 %all-gather.3.cloned.1.call-done = bf16[128,5120]{1,0:T(8,128)(2,1)} async-done(((bf16[128,1280]{1,0:T(8,128)(2,1)}), bf16[128,5120]{1,0:T(8,128)(2,1)}) %all-gather.3.cloned.1.call-update) | async-done | bytes 1310736 | tf_op jit(solution)/shard_map/all_gather | solution.py:78
  34.4 1.4 concatenate.15
  35.9 4.6 gather_fusion
  40.5 6.9 %reshape.153 = bf16[32,12,5120]{2,1,0:T(8,128)(2,1)} reshape(bf16[384,5120]{1,0:T(8,128)(2,1)} %gather_fusion) | data formatting | bytes 7864320 | tf_op jit(solution)/shard_map/reshape | solution.py:43
  47.5 7.5 %all-to-all-start = ((bf16[32,12,5120]{2,1,0:T(8,128)(2,1)}), bf16[32,12,5120]{2,1,0:T(8,128)(2,1)}, u32[]{:S(2)}, u32[]{:S(2)}) async-start(bf16[32,12,5120]{2,1,0:T(8,128)(2,1)} %reshape.153), calls=%async_computation | async-start | bytes 10485760 | tf_op jit(solution)/shard_map/all_to_all | solution.py:85
  55.0 0.7 all-gather.5.cloned.1.call-update
  55.7 0.1 copy.24
  55.8 0.1 reshape.157
  56.0 1.9 gather_fusion.2
  58.0 37.8 %all-gather.5.cloned.1.call-done = bf16[128,5120]{1,0:T(8,128)(2,1)} async-done(((bf16[128,1280]{1,0:T(8,128)(2,1)}), bf16[128,5120]{1,0:T(8,128)(2,1)}) %all-gather.5.cloned.1.call-update) | async-done | bytes 1310736 | tf_op jit(solution)/shard_map/all_gather | solution.py:79
  95.8 1.4 concatenate.18
  97.3 4.6 gather_fusion.3
  101.9 7.6 %reshape.162 = f32[32,12,5120]{2,1,0:T(8,128)} reshape(bf16[384,5120]{1,0:T(8,128)(2,1)} %gather_fusion.3) | data formatting | bytes 11796480 | tf_op jit(solution)/shard_map/convert_element_type | solution.py:44
  109.6 7.8 %multiply_convert_fusion = bf16[32,12,5120]{2,1,0:T(8,128)(2,1)} fusion(f32[32,12,5120]{2,1,0:T(8,128)} %reshape.162, f32[32,12]{1,0:T(8,128)S(1)} %mul.79), kind=kLoop, calls=%fused_computation.6 | loop fusion | flops 3932160 | bytes 11798016 | tf_op jit(solution)/shard_map/convert_element_type | solution.py:44
  117.4 11.3 %all-to-all-done = bf16[32,12,5120]{2,1,0:T(8,128)(2,1)} async-done(((bf16[32,12,5120]{2,1,0:T(8,128)(2,1)}), bf16[32,12,5120]{2,1,0:T(8,128)(2,1)}, u32[]{:S(2)}, u32[]{:S(2)}) %all-to-all-start) | async-done | bytes 3932192 | tf_op jit(solution)/shard_map/all_to_all | solution.py:85
  128.7 26.4 %all-to-all-start.2 = ((bf16[32,12,5120]{2,1,0:T(8,128)(2,1)}), bf16[32,12,5120]{2,1,0:T(8,128)(2,1)}, u32[]{:S(2)}, u32[]{:S(2)}) async-start(bf16[32,12,5120]{2,1,0:T(8,128)(2,1)} %multiply_convert_fusion), calls=%async_computation.3 | async-start | bytes 10485760 | tf_op jit(solution)/shard_map/all_to_all | solution.py:86
  155.1 0.2 reduce-scatter.5.cloned.1.call-start
  155.3 7.0 %reshape.154 = bf16[384,5120]{1,0:T(8,128)(2,1)} reshape(bf16[32,12,5120]{2,1,0:T(8,128)(2,1)} %all-to-all-done) | data formatting | bytes 7864320 | tf_op jit(solution)/shard_map/reshape | solution.py:90
  162.3 5.6 %fusion.12 = f32[384,384]{1,0:T(8,128)S(1)} fusion(bf16[384,5120]{1,0:T(8,128)(2,1)} %reshape.154, bf16[1,5120,384]{2,1,0:T(8,128)(2,1)} %param.11), kind=kOutput, calls=%fused_computation.25 | convolution fusion | flops 1509949440 | bytes 8454144 | tf_op jit(solution)/shard_map/dot_general | solution.py:10
  168.0 2.2 fusion.8
  170.2 57.1 %all-to-all-done.2 = bf16[32,12,5120]{2,1,0:T(8,128)(2,1)} async-done(((bf16[32,12,5120]{2,1,0:T(8,128)(2,1)}), bf16[32,12,5120]{2,1,0:T(8,128)(2,1)}, u32[]{:S(2)}, u32[]{:S(2)}) %all-to-all-start.2) | async-done | bytes 3932192 | tf_op jit(solution)/shard_map/all_to_all | solution.py:86
  227.3 7.0 %reshape.158 = bf16[384,5120]{1,0:T(8,128)(2,1)} reshape(bf16[32,12,5120]{2,1,0:T(8,128)(2,1)} %all-to-all-done.2) | data formatting | bytes 7864320 | tf_op jit(solution)/shard_map/reshape | solution.py:90
  234.4 5.8 %multiply_convert_fusion.1 = (bf16[384,384]{1,0:T(8,128)(2,1)S(1)}, bf16[384,384]{1,0:T(8,128)(2,1)S(1)}, bf16[384,384]{1,0:T(8,128)(2,1)S(1)}) fusion(f32[384,384]{1,0:T(8,128)S(1)} %fusion.12, f32[384,384]{1,0:T(8,128)S(1)} %fusion.8, bf16[384,5120]{1,0:T(8,128)(2,1)} %reshape.158, bf16[1,384,5120]{2,1,0:T(8,128)(2,1)} %param.13), kind=kOutput, calls=%fused_computation.27 | convolution fusion | flops 1512161280 | bytes 9928704 | tf_op jit(solution)/shard_map/dot_general | solution.py:16
  240.2 2.2 fusion.10
  242.5 0.1 copy-done.1
  242.6 5.5 %convolution_add_fusion = f32[384,5120]{1,0:T(8,128)} fusion(f32[384,5120]{1,0:T(8,128)S(1)} %fusion.10, bf16[384,384]{1,0:T(8,128)(2,1)S(1)} %get-tuple-element.16, bf16[1,5120,384]{2,1,0:T(8,128)(2,1)S(1)} %copy-done.1), kind=kOutput, calls=%fused_computation.7 | convolution fusion | flops 1511915520 | bytes 19955712 | tf_op jit(solution)/shard_map/dot_general | solution.py:33
  248.1 9.2 %reshape.159 = f32[32,12,5120]{2,1,0:T(8,128)} reshape(f32[384,5120]{1,0:T(8,128)} %convolution_add_fusion) | data formatting | bytes 15728640 | tf_op jit(solution)/shard_map/reshape | solution.py:93
  257.4 7.5 %fusion.3 = f32[32,12,5120]{2,0,1:T(8,128)} fusion(bf16[1,384,5120]{2,1,0:T(8,128)(2,1)} %param.13, bf16[32,12,384]{2,1,0:T(8,128)(2,1)S(1)} %dot_general.31), kind=kOutput, calls=%fused_computation.16 | convolution fusion | flops 1509949440 | bytes 12091392 | tf_op jit(solution)/shard_map/dot_general | solution.py:15
  264.9 88.4 %reduce-scatter.5.cloned.1.call-done = f32[32,12,1280]{2,1,0:T(8,128)} async-done(((f32[32,12,5120]{2,1,0:T(8,128)}), f32[32,12,1280]{2,1,0:T(8,128)}) %reduce-scatter.5.cloned.1.call-update) | async-done | bytes 1966096 | tf_op jit(solution)/shard_map/reduce_scatter | solution.py:97
  353.3 7.5 %all-to-all-start.3 = ((f32[32,12,1280]{2,1,0:T(8,128)}), f32[32,12,1280]{2,1,0:T(8,128)S(1)}, u32[]{:S(2)}, u32[]{:S(2)}) async-start(f32[32,12,1280]{2,1,0:T(8,128)} %reduce-scatter.5.cloned.1.call-done), calls=%async_computation.5 | async-start | bytes 5242880 | tf_op jit(solution)/shard_map/all_to_all | solution.py:101
  360.8 77.5 %reduce-scatter.3.cloned.1.call-done = f32[32,12,1280]{2,0,1:T(8,128)} async-done(((f32[32,12,5120]{2,0,1:T(8,128)}), f32[32,12,1280]{2,0,1:T(8,128)}) %reduce-scatter.3.cloned.1.call-update) | async-done | bytes 1966096 | tf_op jit(solution)/shard_map/reduce_scatter | solution.py:96
  438.3 4.2 copy.31
  442.5 7.9 %all-to-all-start.1 = ((f32[32,12,1280]{2,1,0:T(8,128)}), f32[32,12,1280]{2,1,0:T(8,128)}, u32[]{:S(2)}, u32[]{:S(2)}) async-start(f32[32,12,1280]{2,1,0:T(8,128)} %copy.31), calls=%async_computation.2 | async-start | bytes 5242880 | tf_op jit(solution)/shard_map/all_to_all | solution.py:100
  450.4 1.0 convert_element_type.55
  451.5 6.5 %fusion.2 = bf16[1,384,5120]{2,1,0:T(8,128)(2,1)} fusion(bf16[384,384]{1,0:T(8,128)(2,1)} %copy-done.5, bf16[384,5120]{1,0:T(8,128)(2,1)} %reshape.158), kind=kOutput, calls=%fused_computation.13 | convolution fusion | flops 1511915520 | bytes 8159232 | tf_op jit(solution)/shard_map/dot_general | solution.py:21
  458.0 4.2 fusion
  462.2 4.1 fusion.1
  466.3 1.4 reshape.160
  467.7 1.7 concatenate.19
  469.4 4.1 gather_fusion.4
  473.5 5.1 reshape.161
  478.5 4.8 reduce_sum.41
  483.3 3.5 all-to-all-done.1
  486.8 2.8 reshape.155
  489.6 1.7 concatenate.16
  491.3 4.1 gather_fusion.1
  495.4 5.1 reshape.156
  500.4 4.8 multiply_reduce_fusion
  505.2 14.6 %psum.7 = f32[128,6]{1,0:T(8,128)S(1)} all-reduce(f32[128,6]{1,0:T(8,128)S(1)} %get-tuple-element.12), channel_id=1, replica_groups=mesh['expert'=32,'dp'=4] {'dp'}, use_global_device_ids=true, to_apply=%region_9.10 | all-reduce | flops 768 | bytes 6144 | tf_op jit(solution)/shard_map/psum | solution.py:110
  519.9 0.7 copy.33
  (38 shorter events, 0.5 us)
Async XLA Ops:
  7.2 27.3 %all-gather.3.cloned.1.call-start = ((), (), s32[]{:S(2)}) async-start(), calls=%async_computation.6 | async-start | bytes 1638400 | tf_op jit(solution)/shard_map/all_gather | solution.py:78
  47.5 8.3 %copy-start.10 = (f32[128,6]{0,1:T(8,128)S(1)}, f32[128,6]{0,1:T(8,128)}, u32[]{:S(2)}) copy-start(f32[128,6]{0,1:T(8,128)} %param.10) | copy-start | bytes 9220
  47.5 81.3 %all-to-all-start = ((bf16[32,12,5120]{2,1,0:T(8,128)(2,1)}), bf16[32,12,5120]{2,1,0:T(8,128)(2,1)}, u32[]{:S(2)}, u32[]{:S(2)}) async-start(bf16[32,12,5120]{2,1,0:T(8,128)(2,1)} %reshape.153), calls=%async_computation | async-start | bytes 10485760 | tf_op jit(solution)/shard_map/all_to_all | solution.py:85
  55.0 40.9 %all-gather.5.cloned.1.call-start = ((), (), s32[]{:S(2)}) async-start(), calls=%async_computation.8 | async-start | bytes 1638400 | tf_op jit(solution)/shard_map/all_gather | solution.py:79
  128.7 98.6 %all-to-all-start.2 = ((bf16[32,12,5120]{2,1,0:T(8,128)(2,1)}), bf16[32,12,5120]{2,1,0:T(8,128)(2,1)}, u32[]{:S(2)}, u32[]{:S(2)}) async-start(bf16[32,12,5120]{2,1,0:T(8,128)(2,1)} %multiply_convert_fusion), calls=%async_computation.3 | async-start | bytes 10485760 | tf_op jit(solution)/shard_map/all_to_all | solution.py:86
  155.1 198.2 %reduce-scatter.5.cloned.1.call-start = ((), (), s32[]{:S(2)}) async-start(), calls=%async_computation.9 | async-start | bytes 13107200 | tf_op jit(solution)/shard_map/reduce_scatter | solution.py:97
  162.3 5.6 %copy-start = (bf16[1,5120,384]{2,1,0:T(8,128)(2,1)S(1)}, bf16[1,5120,384]{2,1,0:T(8,128)(2,1)}, u32[]{:S(2)}) copy-start(bf16[1,5120,384]{2,1,0:T(8,128)(2,1)} %param.12) | copy-start | bytes 11796484
  162.3 5.6 %copy-start.3 = (bf16[384,5120]{1,0:T(8,128)(2,1)S(1)}, bf16[384,5120]{1,0:T(8,128)(2,1)}, u32[]{:S(2)}) copy-start(bf16[384,5120]{1,0:T(8,128)(2,1)} %reshape.154) | copy-start | bytes 11796484
  234.4 5.8 %copy-start.2 = (bf16[1,5120,384]{2,1,0:T(8,128)(2,1)S(1)}, bf16[1,5120,384]{2,1,0:T(8,128)(2,1)}, u32[]{:S(2)}) copy-start(bf16[1,5120,384]{2,1,0:T(8,128)(2,1)} %param.11) | copy-start | bytes 11796484
  240.2 2.3 copy-start.8
  240.2 2.3 copy-start.6
  240.2 17.2 %copy-start.5 = (bf16[384,384]{1,0:T(8,128)(2,1)}, bf16[384,384]{1,0:T(8,128)(2,1)S(1)}, u32[]{:S(2)}) copy-start(bf16[384,384]{1,0:T(8,128)(2,1)S(1)} %get-tuple-element.18) | copy-start | bytes 884740
  240.2 2.4 copy-start.1
  257.3 181.0 %reduce-scatter.3.cloned.1.call-start = ((), (), s32[]{:S(2)}) async-start(), calls=%async_computation.7 | async-start | bytes 9830400 | tf_op jit(solution)/shard_map/reduce_scatter | solution.py:96
  353.3 89.2 %all-to-all-start.3 = ((f32[32,12,1280]{2,1,0:T(8,128)}), f32[32,12,1280]{2,1,0:T(8,128)S(1)}, u32[]{:S(2)}, u32[]{:S(2)}) async-start(f32[32,12,1280]{2,1,0:T(8,128)} %reduce-scatter.5.cloned.1.call-done), calls=%async_computation.5 | async-start | bytes 5242880 | tf_op jit(solution)/shard_map/all_to_all | solution.py:101
  442.5 44.3 %all-to-all-start.1 = ((f32[32,12,1280]{2,1,0:T(8,128)}), f32[32,12,1280]{2,1,0:T(8,128)}, u32[]{:S(2)}, u32[]{:S(2)}) async-start(f32[32,12,1280]{2,1,0:T(8,128)} %copy.31), calls=%async_computation.2 | async-start | bytes 5242880 | tf_op jit(solution)/shard_map/all_to_all | solution.py:100
  451.5 6.5 %copy-start.4 = (bf16[384,5120]{1,0:T(8,128)(2,1)S(1)}, bf16[384,5120]{1,0:T(8,128)(2,1)}, u32[]{:S(2)}) copy-start(bf16[384,5120]{1,0:T(8,128)(2,1)} %reshape.154) | copy-start | bytes 11796484
  451.5 6.5 %copy-start.9 = (bf16[384,384]{1,0:T(8,128)(2,1)S(1)}, bf16[384,384]{1,0:T(8,128)(2,1)}, u32[]{:S(2)}) copy-start(bf16[384,384]{1,0:T(8,128)(2,1)} %copy-done.8) | copy-start | bytes 884740
  458.0 4.2 copy-start.7
Sparse Core Ops, SparseCore 0:
  9.7 24.6 all-gather.2
  57.5 38.3 all-gather.4
  257.4 95.8 reduce-scatter.4
  355.8 82.4 reduce-scatter.2
where the time goes:
time: 529 us; the launch traced here: 527 us
  waiting for transfers between devices  295 us (56%)
  local copies, waits for them, and re-layouts  88.4 us (17%)
  starting transfers between devices  49.6 us (9%)
  matrix products  43.6 us (8%)
  other arithmetic  21.8 us (4%)
  blocking collectives  14.6 us (3%)
  between operations  14.1 us (3%)
    reduce_scatter x1, waiting for transfers between devices, body(): lax.psum_scatter(backward3, 'dp', scatter_dimension=2, tiled=True)  88.4 us
    reduce_scatter x1, waiting for transfers between devices, body(): lax.psum_scatter(result3, 'dp', scatter_dimension=2, tiled=True)  77.5 us
    all_to_all x1, waiting for transfers between devices, body(): lax.all_to_all(send_grad, 'expert', split_axis=0, concat_axis=0, tiled=True)  57.1 us
    all_gather x1, waiting for transfers between devices, body(): lax.all_gather(cotangent, 'dp', axis=1, tiled=True)  37.8 us
    all_to_all x1, starting transfers between devices, body(): lax.all_to_all(send_grad, 'expert', split_axis=0, concat_axis=0, tiled=True)  26.4 us
    all_gather x1, waiting for transfers between devices, body(): lax.all_gather(tokens, 'dp', axis=1, tiled=True)  17.9 us
    psum x1, blocking collectives, body(): grad_probs = lax.psum(inner_part, 'dp')  14.6 us
    all_to_all x1, waiting for transfers between devices, body(): lax.all_to_all(send_in, 'expert', split_axis=0, concat_axis=0, tiled=True)  11.3 us
  transfers between devices with their start and end apart: 8, of which 7 were waited for; matrix products, arithmetic and copies ran while one was open for 17% of the time, Pallas kernels for 0%

commit v1 on v0

v1 whole, which is shorter than its diff:
```python
import functools

import jax
import jax.numpy as jnp
from jax import lax
from jax.experimental import pallas as pl
from jax.experimental.pallas import tpu as pltpu
from jax.sharding import Mesh, PartitionSpec as P

BF = jnp.bfloat16
F32 = jnp.float32

EXPERTS = 32
BLOCK = 128
TOPK = 6
COLS = 1280
HALF = 640
HID = 384
ROWS = 384
MAIN = 256
REST = 128
WIDE = COLS + HALF
D = 4 * COLS
VMEM = 40 * 1024 * 1024


def _dot(a, b):
    return jnp.dot(a, b, preferred_element_type=F32)


def _dot_nt(a, b):
    return lax.dot_general(a, b, (((1,), (1,)), ((), ())), preferred_element_type=F32)


def _dot_tn(a, b):
    return lax.dot_general(a, b, (((0,), (0,)), ((), ())), preferred_element_type=F32)


def _iota(shape, dim):
    return lax.broadcasted_iota(jnp.int32, shape, dim)


def _routing(ids_t, probs_t):
    expert = _iota((EXPERTS, BLOCK), 0)
    chosen = jnp.zeros((EXPERTS, BLOCK), F32)
    weight = jnp.zeros((EXPERTS, BLOCK), F32)
    for k in range(TOPK):
        hit = ids_t[k : k + 1, :] == expert
        chosen = jnp.where(hit, 1.0, chosen)
        weight = jnp.where(hit, probs_t[k : k + 1, :], weight)
    earlier = (_iota((BLOCK, BLOCK), 0) < _iota((BLOCK, BLOCK), 1)).astype(F32).astype(BF)
    before = _dot(chosen.astype(BF), earlier)
    code = jnp.where(chosen > 0.5, before, -1.0)
    row = _iota((MAIN, EXPERTS), 0)
    spread = ((row // 8) == _iota((MAIN, EXPERTS), 1)).astype(F32).astype(BF)
    place = _dot(spread, code.astype(BF))
    j = _iota((MAIN, BLOCK), 0)
    main = jnp.where(place == (j % 8).astype(F32), 1.0, 0.0)
    rest = jnp.where(place == (8 + j % 4).astype(F32), 1.0, 0.0)
    hi = weight.astype(BF)
    left = weight - hi.astype(F32)
    mid = left.astype(BF)
    low = (left - mid.astype(F32)).astype(BF)
    full = _dot(spread, hi) + _dot(spread, mid) + _dot(spread, low)
    return main, rest, full


def _lower_half(shape):
    return (_iota(shape, 0) % 8) < 4


def _send(main, rest, source):
    first = _lower_half((MAIN, BLOCK))
    p0 = jnp.where(first, rest, 0.0).astype(BF)
    p1 = jnp.where(first, 0.0, rest).astype(BF)
    a = _dot(main.astype(BF), source)
    b = _dot(p0, source[:, :HALF]) + _dot(p1, source[:, HALF:])
    return a, b


def _pack_rows_kernel(ids_ref, probs_ref, tok_ref, out_ref):
    main, rest, _ = _routing(ids_ref[...], probs_ref[...])
    a, b = _send(main, rest, tok_ref[...])
    a, b = a.astype(BF), b.astype(BF)
    for y in range(2):
        out_ref[y, :, :COLS] = a
        out_ref[y, :, COLS:] = b


def _pack_grads_kernel(ids_ref, probs_ref, cot_ref, out_ref, pick_ref, weight_ref):
    main, rest, full = _routing(ids_ref[...], probs_ref[...])
    a, b = _send(main, rest, cot_ref[...])
    wm, wr = main * full, rest * full
    a = (a * jnp.sum(wm, axis=1, keepdims=True)).astype(BF)
    b = (b * jnp.sum(wr, axis=1, keepdims=True)).astype(BF)
    for y in range(2):
        out_ref[y, :, :COLS] = a
        out_ref[y, :, COLS:] = b
    pick_ref[:MAIN, :] = main.astype(BF)
    pick_ref[MAIN:, :] = rest.astype(BF)
    weight_ref[:MAIN, :] = wm
    weight_ref[MAIN:, :] = wr


def _fold(h):
    q = _iota((REST, MAIN), 0)
    return (_iota((REST, MAIN), 1) == (q // 4) * 8 + 4 * h + q % 4).astype(F32).astype(BF)


def _fold_t(h):
    q = _iota((MAIN, REST), 1)
    return (_iota((MAIN, REST), 0) == (q // 4) * 8 + 4 * h + q % 4).astype(F32).astype(BF)


def _unpack(r_ref, x_ref):
    rest = r_ref[0, :, COLS:]
    x_ref[:MAIN, :] = r_ref[0, :, :COLS]
    x_ref[MAIN:, :HALF] = _dot(_fold(0), rest).astype(BF)
    x_ref[MAIN:, HALF:] = _dot(_fold(1), rest).astype(BF)


def _pack(value, out_ref):
    rest = value[MAIN:, :]
    out_ref[0, :, :COLS] = value[:MAIN, :]
    out_ref[0, :, COLS:] = (_dot(_fold_t(0), rest[:, :HALF]) + _dot(_fold_t(1), rest[:, HALF:])).astype(BF)


def _forward_kernel(core_ref, own_ref, other_ref, wg_ref, wu_ref, x_ref, g_ref, u_ref, h_ref):
    step = pl.program_id(0)

    @pl.when(step < 2)
    def _():
        _unpack(own_ref, x_ref)

    @pl.when(step >= 2)
    def _():
        _unpack(other_ref, x_ref)

    x = x_ref[...]
    g = _dot(x, wg_ref[...])
    u = _dot(x, wu_ref[...])

    @pl.when(step == 0)
    def _():
        g_ref[...] = g
        u_ref[...] = u

    @pl.when(step > 0)
    def _():
        g_ref[...] += g
        u_ref[...] += u

    @pl.when(step == 3)
    def _():
        gate = g_ref[...]
        h_ref[...] = (gate * jax.nn.sigmoid(gate) * u_ref[...]).astype(BF)


def _backward_kernel(core_ref, own_ref, other_ref, wd_ref, g_ref, u_ref, e_ref, d_ref, a_ref):
    step = pl.program_id(0)

    @pl.when(step < 2)
    def _():
        _unpack(own_ref, e_ref)

    @pl.when(step >= 2)
    def _():
        _unpack(other_ref, e_ref)

    a = _dot_nt(e_ref[...], wd_ref[...])

    @pl.when(step == 0)
    def _():
        a_ref[...] = a

    @pl.when(step > 0)
    def _():
        a_ref[...] += a

    @pl.when(step == 3)
    def _():
        total, gate = a_ref[...], g_ref[...]
        s = jax.nn.sigmoid(gate)
        d_ref[:, :HID] = (total * u_ref[...] * s * (1.0 + gate * (1.0 - s))).astype(BF)
        d_ref[:, HID:] = (total * (gate * s)).astype(BF)


def _result_kernel(core_ref, h_ref, hp_ref, wd_ref, wdp_ref, out_ref):
    value = _dot(h_ref[...], wd_ref[...]) + _dot(hp_ref[...], wdp_ref[...])
    _pack(value.astype(BF), out_ref)


def _back_kernel(core_ref, d_ref, dp_ref, wg_ref, wu_ref, wgp_ref, wup_ref, out_ref):
    value = _dot_nt(d_ref[:, :HID], wg_ref[...]) + _dot_nt(d_ref[:, HID:], wu_ref[...])
    value += _dot_nt(dp_ref[:, :HID], wgp_ref[...]) + _dot_nt(dp_ref[:, HID:], wup_ref[...])
    _pack(value.astype(BF), out_ref)


def _home(pick, r_ref):
    main = pick[:MAIN, :]
    first = _lower_half((MAIN, BLOCK))
    rest = pick[MAIN:, :].astype(F32)
    halves = (jnp.where(first, rest, 0.0).astype(BF), jnp.where(first, 0.0, rest).astype(BF))
    out = []
    for h in range(2):
        total = jnp.zeros((BLOCK, HALF), F32)
        for y in range(2):
            total += _dot_tn(main, r_ref[y, :, h * HALF : (h + 1) * HALF])
            total += _dot_tn(halves[h], r_ref[y, :, COLS:])
        out.append(total)
    return out


def _mixed_kernel(ids_ref, pick_ref, weight_ref, cot_ref, r_ref, mixed_ref, gp_ref):
    w = weight_ref[...]
    hi = w.astype(BF)
    lo = (w - hi.astype(F32)).astype(BF)
    top, bottom = _home(hi, r_ref), _home(lo, r_ref)
    for h in range(2):
        mixed_ref[:, h * HALF : (h + 1) * HALF] = (top[h] + bottom[h]).astype(BF)
    cot = cot_ref[...]
    first = _lower_half((MAIN, BLOCK))
    inner = jnp.zeros((MAIN, BLOCK), F32)
    inner_rest = jnp.zeros((MAIN, BLOCK), F32)
    for y in range(2):
        inner += _dot_nt(r_ref[y, :, :COLS], cot)
        rest = r_ref[y, :, COLS:]
        inner_rest += jnp.where(first, _dot_nt(rest, cot[:, :HALF]), _dot_nt(rest, cot[:, HALF:]))
    pick = pick_ref[...].astype(F32)
    both = pick[:MAIN, :] * inner + pick[MAIN:, :] * inner_rest
    each = jnp.sum(both.reshape(EXPERTS, 8, BLOCK), axis=1)
    expert = _iota((EXPERTS, BLOCK), 0)
    ids = ids_ref[...]
    for k in range(TOPK):
        gp_ref[k : k + 1, :] = jnp.sum(jnp.where(ids[k : k + 1, :] == expert, each, 0.0), axis=0, keepdims=True)
    gp_ref[TOPK:, :] = jnp.zeros((8 - TOPK, BLOCK), F32)


def _grad_tokens_kernel(pick_ref, r_ref, out_ref):
    halves = _home(pick_ref[...], r_ref)
    for h in range(2):
        out_ref[:, h * HALF : (h + 1) * HALF] = halves[h].astype(BF)


def _params():
    return pltpu.CompilerParams(vmem_limit_bytes=VMEM)


def _cost(flops, moved):
    return pl.CostEstimate(flops=int(flops), bytes_accessed=int(moved), transcendentals=0)


def _shape(shape, dtype):
    return jax.ShapeDtypeStruct(shape, dtype)


def _src(step):
    return step // 2


def _group(step, core):
    return (step % 2) * 2 + jnp.where(step < 2, core, 1 - core)


def _received():
    own = pl.BlockSpec((1, MAIN, WIDE), lambda i, c: (jnp.minimum(i, 1), 0, 0))
    other = pl.BlockSpec((1, MAIN, WIDE), lambda i, c: (jnp.maximum(i - 2, 0), 0, 0))
    return own, other


def _fixed(*shape):
    return pl.BlockSpec(shape, lambda i, c: (0,) * len(shape))


def _forward(core, own, other, w_gate, w_up):
    weight = pl.BlockSpec((COLS, HID), lambda i, c: (_group(i, c[0]), 0))
    return pl.pallas_call(
        _forward_kernel,
        grid_spec=pltpu.PrefetchScalarGridSpec(
            num_scalar_prefetch=1,
            grid=(4,),
            in_specs=[*_received(), weight, weight],
            out_specs=[
                pl.BlockSpec((ROWS, COLS), lambda i, c: (0, _group(i, c[0]))),
                _fixed(ROWS, HID),
                _fixed(ROWS, HID),
                _fixed(ROWS, HID),
            ],
        ),
        out_shape=[
            _shape((ROWS, D), BF),
            _shape((ROWS, HID), F32),
            _shape((ROWS, HID), F32),
            _shape((ROWS, HID), BF),
        ],
        compiler_params=_params(),
        cost_estimate=_cost(4 * ROWS * D * HID, 17e6),
        name="forward",
    )(core, own, other, w_gate, w_up)


def _backward(core, own, other, w_down, gate, up):
    return pl.pallas_call(
        _backward_kernel,
        grid_spec=pltpu.PrefetchScalarGridSpec(
            num_scalar_prefetch=1,
            grid=(4,),
            in_specs=[
                *_received(),
                pl.BlockSpec((HID, COLS), lambda i, c: (0, _group(i, c[0]))),
                _fixed(ROWS, HID),
                _fixed(ROWS, HID),
            ],
            out_specs=[
                pl.BlockSpec((ROWS, COLS), lambda i, c: (0, _group(i, c[0]))),
                _fixed(ROWS, 2 * HID),
            ],
            scratch_shapes=[pltpu.VMEM((ROWS, HID), F32)],
        ),
        out_shape=[_shape((ROWS, D), BF), _shape((ROWS, 2 * HID), BF)],
        compiler_params=_params(),
        cost_estimate=_cost(2 * ROWS * D * HID, 14e6),
        name="backward",
    )(core, own, other, w_down, gate, up)


def _result(core, hidden, hidden_p, w_down, w_down_p):
    weight = pl.BlockSpec((HID, COLS), lambda i, c: (0, 2 * i + c[0]))
    return pl.pallas_call(
        _result_kernel,
        grid_spec=pltpu.PrefetchScalarGridSpec(
            num_scalar_prefetch=1,
            grid=(2,),
            in_specs=[_fixed(ROWS, HID), _fixed(ROWS, HID), weight, weight],
            out_specs=pl.BlockSpec((1, MAIN, WIDE), lambda i, c: (i, 0, 0)),
        ),
        out_shape=_shape((2, MAIN, WIDE), BF),
        compiler_params=_params(),
        cost_estimate=_cost(2 * ROWS * D * HID, 7e6),
        name="result",
    )(core, hidden, hidden_p, w_down, w_down_p)


def _back(core, grads, grads_p, w_gate, w_up, w_gate_p, w_up_p):
    weight = pl.BlockSpec((COLS, HID), lambda i, c: (2 * i + c[0], 0))
    return pl.pallas_call(
        _back_kernel,
        grid_spec=pltpu.PrefetchScalarGridSpec(
            num_scalar_prefetch=1,
            grid=(2,),
            in_specs=[_fixed(ROWS, 2 * HID), _fixed(ROWS, 2 * HID), weight, weight, weight, weight],
            out_specs=pl.BlockSpec((1, MAIN, WIDE), lambda i, c: (i, 0, 0)),
        ),
        out_shape=_shape((2, MAIN, WIDE), BF),
        compiler_params=_params(),
        cost_estimate=_cost(4 * ROWS * D * HID, 11e6),
        name="back",
    )(core, grads, grads_p, w_gate, w_up, w_gate_p, w_up_p)


def _local(kernel, out_shape, flops, moved, name, *args):
    return pl.pallas_call(
        kernel, out_shape=out_shape, compiler_params=_params(), cost_estimate=_cost(flops, moved), name=name
    )(*args)


def _exchange(packed):
    chunks = packed.reshape(2 * EXPERTS, 8, WIDE)
    got = lax.all_to_all(chunks, ("yhi", "expert"), split_axis=0, concat_axis=0, tiled=True)
    return got.reshape(2, MAIN, WIDE)


def _swap(value, axis="core"):
    return lax.ppermute(value, axis, [(0, 1), (1, 0)])


def body(tokens, cotangent, expert_ids, route_probs, w_gate, w_up, w_down):
    core = lax.axis_index("core").astype(jnp.int32).reshape(1)
    wg, wu, wd = w_gate[0], w_up[0], w_down[0]
    ids_t, probs_t = expert_ids.T, route_probs.T

    send_x = _local(_pack_rows_kernel, _shape((2, MAIN, WIDE), BF), 2e8, 3e6, "pack_rows", ids_t, probs_t, tokens)
    recv_x = _exchange(send_x)
    send_e, pick, weight = _local(
        _pack_grads_kernel,
        [_shape((2, MAIN, WIDE), BF), _shape((2 * MAIN, BLOCK), BF), _shape((2 * MAIN, BLOCK), F32)],
        2e8,
        3e6,
        "pack_grads",
        ids_t,
        probs_t,
        cotangent,
    )
    wd_p, wg_p, wu_p = _swap(wd), _swap(wg), _swap(wu)
    recv_e = _exchange(send_e)

    x, gate, up, hidden = _forward(core, recv_x, _swap(recv_x), wg, wu)
    send_o = _result(core, hidden, _swap(hidden), wd, wd_p)
    recv_o = _exchange(send_o)

    e, grads = _backward(core, recv_e, _swap(recv_e), wd, gate, up)
    send_b = _back(core, grads, _swap(grads), wg, wu, wg_p, wu_p)
    recv_b = _exchange(send_b)

    g_down = _dot_tn(hidden, e).astype(BF)
    g_gate = _dot_tn(x, grads[:, :HID]).astype(BF)
    g_up = _dot_tn(x, grads[:, HID:]).astype(BF)

    mixed, inner = _local(
        _mixed_kernel,
        [_shape((BLOCK, COLS), BF), _shape((8, BLOCK), F32)],
        4e8,
        3e6,
        "mixed",
        ids_t,
        pick,
        weight,
        cotangent,
        recv_o,
    )
    inner = inner + _swap(inner)
    inner = inner + _swap(inner, "yhi")
    grad_probs = inner[:TOPK].T

    grad_tokens = _local(_grad_tokens_kernel, _shape((BLOCK, COLS), BF), 2e8, 3e6, "grad_tokens", pick, recv_b)
    return mixed, grad_tokens, grad_probs, g_gate[None], g_up[None], g_down[None]


def solution(mesh):
    fine = Mesh(mesh.devices.reshape(EXPERTS, 2, 2), ("expert", "yhi", "core"))
    dp = ("yhi", "core")
    return jax.shard_map(
        body,
        mesh=fine,
        in_specs=(
            P("expert", dp),
            P("expert", dp),
            P("expert", None),
            P("expert", None),
            P("expert", None, dp),
            P("expert", None, dp),
            P("expert", dp, None),
        ),
        out_specs=(
            P("expert", dp),
            P("expert", dp),
            P("expert", None),
            P("expert", None, dp),
            P("expert", None, dp),
            P("expert", dp, None),
        ),
        check_vma=False,
    )
```

time: 529 us -> 170 us (0.32)
  waiting for transfers between devices: 295 us -> 63.2 us
  local copies, waits for them, and re-layouts: 88.4 us -> 21.3 us
  Pallas kernels: 0 us -> 33.6 us
  matrix products: 43.6 us -> 15.1 us
  other arithmetic: 21.8 us -> 0.01 us
  starting transfers between devices: 49.6 us -> 34.8 us
  blocking collectives: 14.6 us -> 0 us
  between operations: 14.1 us -> 0.9 us
    reduce_scatter x2 -> x0, waiting for transfers between devices: 166 us -> none  [the longest x1 88.4 us: body(): lax.psum_scatter(backward3, 'dp', scatter_dimension=2, tiled=True)]
    all_gather x2 -> x0, waiting for transfers between devices: 55.7 us -> none  [the longest x1 37.8 us: body(): lax.all_gather(cotangent, 'dp', axis=1, tiled=True)]
    reshape x9 -> x0, local copies, waits for them, and re-layouts: 44.6 us -> none  [the longest x1 9.16 us: body(): backward3 = backward.reshape(experts, capacity, width)]
    pallas_call x0 -> x8, Pallas kernels: none -> 33.6 us  [the longest x1 8.64 us: _forward(): pl.pallas_call(_forward_kernel, grid_spec=pltpu.PrefetchScalarGridSpec(nu...]
    dot_general x9 -> x3, matrix products: 43.6 us -> 15.1 us  [_dot_tn(): lax.dot_general(a, b, (((0,), (0,)), ((), ())), preferred_element_type=F32)]
    gather x5 -> x0, local copies, waits for them, and re-layouts: 19.4 us -> none  [the longest x2 8.19 us: pick_rows(): return padded[slot_of]]
    unnamed x25 -> x54, local copies, waits for them, and re-layouts: 1.75 us -> 20.7 us
    all_to_all x4, starting transfers between devices: 49.3 us -> 30.3 us  [_exchange(): lax.all_to_all(chunks, ('yhi', 'expert'), split_axis=0, concat_axis=0, ti...]
  transfers between devices with their start and end apart: 8 -> 13, of which waited for: 7 -> 6; matrix products, arithmetic and copies ran while one was open for 17% -> 9% of each run, Pallas kernels for 0% -> 19%
where the time goes in v1:
time: 170 us; the launch traced here: 169 us
  waiting for transfers between devices  63.2 us (37%)
  starting transfers between devices  34.8 us (20%)
  Pallas kernels  33.6 us (20%)
  local copies, waits for them, and re-layouts  21.3 us (13%)
  matrix products  15.1 us (9%)
    all_to_all x4, waiting for transfers between devices, _exchange(): lax.all_to_all(chunks, ('yhi', 'expert'), split_axis=0, concat_axis=0, ti...  60 us
    all_to_all x4, starting transfers between devices, _exchange(): lax.all_to_all(chunks, ('yhi', 'expert'), split_axis=0, concat_axis=0, ti...  30.3 us
    unnamed x54, local copies, waits for them, and re-layouts  20.7 us
    dot_general x3, matrix products, _dot_tn(): lax.dot_general(a, b, (((0,), (0,)), ((), ())), preferred_element_type=F32)  15.1 us
    pallas_call x1, Pallas kernels, _forward(): pl.pallas_call(_forward_kernel, grid_spec=pltpu.PrefetchScalarGridSpec(nu...  8.64 us
    pallas_call x1, Pallas kernels, _back(): pl.pallas_call(_back_kernel, grid_spec=pltpu.PrefetchScalarGridSpec(num_s...  7.09 us
    pallas_call x4, Pallas kernels, _local(): pl.pallas_call(kernel, out_shape=out_shape, compiler_params=_params(), co...  6.7 us
    pallas_call x1, Pallas kernels, _backward(): pl.pallas_call(_backward_kernel, grid_spec=pltpu.PrefetchScalarGridSpec(n...  6.41 us
  transfers between devices with their start and end apart: 13, of which 6 were waited for; matrix products, arithmetic and copies ran while one was open for 9% of the time, Pallas kernels for 19%

profile of v1, /device:TPU:0, one launch (start us, length us, event | category | flops | bytes accessed | tf_op | source)
XLA Modules:
  0.0 169.0 jit_solution(13724227160065582142)
XLA Ops:
  0.6 1.0 copy-done.17
  1.6 0.7 copy-done.22
  2.3 0.7 copy-done.24
  3.0 0.7 pack_rows.1
  3.7 0.0 copy-start.8
  3.7 1.3 copy-done.8
  5.0 11.5 %all-to-all-start = ((bf16[64,8,1920]{2,1,0:T(8,128)(2,1)}), bf16[64,8,1920]{2,1,0:T(8,128)(2,1)S(1)}, u32[]{:S(2)}, u32[]{:S(2)}) async-start(bf16[64,8,1920]{2,1,0:T(8,128)(2,1)} %bitcast.41), calls=%async_computation | async-start | bytes 3932160 | tf_op jit(solution)/shard_map/all_to_all | solution.py:369
  16.5 0.1 collective-permute-start.2
  16.6 0.8 pack_grads.1
  17.4 0.0 copy-start.12
  17.4 1.3 copy-done.12
  18.7 0.7 copy-done.15
  19.3 0.7 copy-done.20
  20.0 24.3 %all-to-all-done = bf16[64,8,1920]{2,1,0:T(8,128)(2,1)S(1)} async-done(((bf16[64,8,1920]{2,1,0:T(8,128)(2,1)}), bf16[64,8,1920]{2,1,0:T(8,128)(2,1)S(1)}, u32[]{:S(2)}, u32[]{:S(2)}) %all-to-all-start) | async-done | bytes 1966112 | tf_op jit(solution)/shard_map/all_to_all | solution.py:369
  44.3 1.3 copy-done.5
  45.6 6.0 %all-to-all-start.2 = ((bf16[64,8,1920]{2,1,0:T(8,128)(2,1)}), bf16[64,8,1920]{2,1,0:T(8,128)(2,1)S(1)}, u32[]{:S(2)}, u32[]{:S(2)}) async-start(bf16[64,8,1920]{2,1,0:T(8,128)(2,1)} %bitcast.43), calls=%async_computation.2 | async-start | bytes 3932160 | tf_op jit(solution)/shard_map/all_to_all | solution.py:369
  51.6 0.1 collective-permute-start
  51.7 0.5 collective-permute-start.5
  52.2 0.1 collective-permute-start.6
  52.3 25.6 %all-to-all-done.2 = bf16[64,8,1920]{2,1,0:T(8,128)(2,1)S(1)} async-done(((bf16[64,8,1920]{2,1,0:T(8,128)(2,1)}), bf16[64,8,1920]{2,1,0:T(8,128)(2,1)S(1)}, u32[]{:S(2)}, u32[]{:S(2)}) %all-to-all-start.2) | async-done | bytes 1966112 | tf_op jit(solution)/shard_map/all_to_all | solution.py:369
  77.9 0.0 collective-permute-start.3
  77.9 0.0 collective-permute-done.other_ref
  78.0 2.1 %copy-done = bf16[1,5120,384]{2,1,0:T(8,128)(2,1)S(1)} copy-done((bf16[1,5120,384]{2,1,0:T(8,128)(2,1)S(1)}, bf16[1,5120,384]{2,1,0:T(8,128)(2,1)}, u32[]{:S(2)}) %copy-start) | copy-done | bytes 3932184
  80.1 1.5 copy-done.6
  81.6 8.6 %forward.1 = (bf16[384,5120]{1,0:T(8,128)(2,1)S(1)}, f32[384,384]{1,0:T(8,128)S(1)}, f32[384,384]{1,0:T(8,128)S(1)}, bf16[384,384]{1,0:T(8,128)(2,1)S(1)}) custom-call(s32[1]{0:T(128)} %bitcast.2.core_ref, bf16[2,256,1920]{2,1,0:T(8,128)(2,1)S(1)} %bitcast.38, bf16[2,256,1920]{2,1,0:T(8,128)(2,1)} %collective-permute-done.other_ref, ...), custom_call_target="tpu_custom_call" | custom-call | flops 3019898880 | bytes 17000000 | tf_op jit(solution)/shard_map/forward/pallas_call | solution.py:277
  90.3 0.0 copy-start.25
  90.3 1.9 %copy-done.25 = bf16[384,5120]{1,0:T(8,128)(2,1)} copy-done((bf16[384,5120]{1,0:T(8,128)(2,1)}, bf16[384,5120]{1,0:T(8,128)(2,1)S(1)}, u32[]{:S(2)}) %copy-start.25) | copy-done | bytes 3932184
  92.2 0.5 collective-permute-start.1
  92.7 0.0 collective-permute-done.2.wdp_ref
  92.7 1.2 collective-permute-done.1.hp_ref
  93.9 4.8 %result.1 = bf16[2,256,1920]{2,1,0:T(8,128)(2,1)S(1)} custom-call(s32[1]{0:T(128)} %bitcast.2.core_ref, bf16[384,384]{1,0:T(8,128)(2,1)S(1)} %get-tuple-element.19.h_ref, bf16[384,384]{1,0:T(8,128)(2,1)S(1)} %collective-permute-done.1.hp_ref, bf16[384,5120]{1,0:T(8,128)(2,1)S(1)} %bitcast.33, bf16[384,5120]{1,0:T(8,128)(2,1)} %collective-permute-done.2.wdp_ref), custom_call_target="tpu_custom_call" | custom-call | flops 1509949440 | bytes 7000000 | tf_op jit(solution)/shard_map/result/pallas_call | solution.py:329
  98.7 0.0 copy-start.7
  98.7 1.3 copy-done.7
  100.0 6.7 %all-to-all-start.1 = ((bf16[64,8,1920]{2,1,0:T(8,128)(2,1)}), bf16[64,8,1920]{2,1,0:T(8,128)(2,1)}, u32[]{:S(2)}, u32[]{:S(2)}) async-start(bf16[64,8,1920]{2,1,0:T(8,128)(2,1)} %bitcast.40), calls=%async_computation.1 | async-start | bytes 3932160 | tf_op jit(solution)/shard_map/all_to_all | solution.py:369
  106.7 0.0 collective-permute-done.3.other_ref
  106.7 0.0 copy-start.4
  106.7 2.1 %copy-done.4 = bf16[1,384,5120]{2,1,0:T(8,128)(2,1)S(1)} copy-done((bf16[1,384,5120]{2,1,0:T(8,128)(2,1)S(1)}, bf16[1,384,5120]{2,1,0:T(8,128)(2,1)}, u32[]{:S(2)}) %copy-start.4) | copy-done | bytes 3932184
  108.8 1.1 copy-done.14
  109.9 6.4 %backward.1 = (bf16[384,5120]{1,0:T(8,128)(2,1)S(1)}, bf16[384,768]{1,0:T(8,128)(2,1)S(1)}) custom-call(s32[1]{0:T(128)} %bitcast.2.core_ref, bf16[2,256,1920]{2,1,0:T(8,128)(2,1)S(1)} %bitcast.36, bf16[2,256,1920]{2,1,0:T(8,128)(2,1)} %collective-permute-done.3.other_ref, bf16[384,5120]{1,0:T(8,128)(2,1)S(1)} %bitcast.34, ...), custom_call_target="tpu_custom_call" | custom-call | flops 1509949440 | bytes 14000000 | tf_op jit(solution)/shard_map/backward/pallas_call | solution.py:303
  116.3 1.9 %copy-done.10 = bf16[384,5120]{1,0:T(8,128)(2,1)} copy-done((bf16[384,5120]{1,0:T(8,128)(2,1)}, bf16[384,5120]{1,0:T(8,128)(2,1)S(1)}, u32[]{:S(2)}) %copy-start.10) | copy-done | bytes 3932184
  118.2 0.1 collective-permute-start.4
  118.3 0.0 collective-permute-done.5.wgp_ref
  118.3 0.0 collective-permute-done.6.wup_ref
  118.3 1.9 %collective-permute-done.4.dp_ref = bf16[384,768]{1,0:T(8,128)(2,1)S(1)} collective-permute-done((bf16[384,768]{1,0:T(8,128)(2,1)S(1)}, bf16[384,768]{1,0:T(8,128)(2,1)S(1)}, u32[]{:S(2)}, u32[]{:S(2)}) %collective-permute-start.4) | collective-permute-done | bytes 589856 | tf_op jit(solution)/shard_map/ppermute | solution.py:374
  120.2 0.0 copy-done.2
  120.2 7.1 %back.1 = bf16[2,256,1920]{2,1,0:T(8,128)(2,1)S(1)} custom-call(s32[1]{0:T(128)} %bitcast.2.core_ref, bf16[384,768]{1,0:T(8,128)(2,1)S(1)} %get-tuple-element.24.d_ref, bf16[384,768]{1,0:T(8,128)(2,1)S(1)} %collective-permute-done.4.dp_ref, bf16[5120,384]{1,0:T(8,128)(2,1)S(1)} %bitcast.28, bf16[5120,384]{1,0:T(8,128)(2,1)S(1)} %bitcast.31, ...), custom_call_target="tpu_custom_call" | custom-call | flops 3019898880 | bytes 11000000 | tf_op jit(solution)/shard_map/back/pallas_call | solution.py:346
  127.3 1.3 copy-done.9
  128.6 6.3 %all-to-all-done.1 = bf16[64,8,1920]{2,1,0:T(8,128)(2,1)} async-done(((bf16[64,8,1920]{2,1,0:T(8,128)(2,1)}), bf16[64,8,1920]{2,1,0:T(8,128)(2,1)}, u32[]{:S(2)}, u32[]{:S(2)}) %all-to-all-start.1) | async-done | bytes 1966112 | tf_op jit(solution)/shard_map/all_to_all | solution.py:369
  134.9 6.0 %all-to-all-start.3 = ((bf16[64,8,1920]{2,1,0:T(8,128)(2,1)}), bf16[64,8,1920]{2,1,0:T(8,128)(2,1)S(1)}, u32[]{:S(2)}, u32[]{:S(2)}) async-start(bf16[64,8,1920]{2,1,0:T(8,128)(2,1)} %bitcast.42), calls=%async_computation.3 | async-start | bytes 3932160 | tf_op jit(solution)/shard_map/all_to_all | solution.py:369
  141.0 0.0 copy-start.16
  141.0 0.0 copy-start.19
  141.0 0.0 copy-start.21
  141.0 0.0 copy-start.26
  141.0 6.8 %fusion.1 = bf16[1,5120,384]{2,1,0:T(8,128)(2,1)} fusion(bf16[384,5120]{1,0:T(8,128)(2,1)} %copy-done.25, bf16[384,768]{1,0:T(8,128)(2,1)S(1)} %get-tuple-element.24.d_ref), kind=kOutput, calls=%fused_computation.4 | convolution fusion | flops 1511915520 | bytes 8159232 | tf_op jit(solution)/shard_map/dot_general | solution.py:36
  147.8 3.8 %mixed.1 = (bf16[128,1280]{1,0:T(8,128)(2,1)}, f32[8,128]{1,0:T(8,128)S(1)}) custom-call(s32[6,128]{1,0:T(8,128)S(1)} %bitcast.46, bf16[512,128]{1,0:T(8,128)(2,1)S(1)} %copy-done.16, f32[512,128]{1,0:T(8,128)S(1)} %copy-done.21, bf16[128,1280]{1,0:T(8,128)(2,1)S(1)} %copy-done.19, bf16[2,256,1920]{2,1,0:T(8,128)(2,1)} %bitcast.9.r_ref), custom_call_target="tpu_custom_call" | custom-call | flops 400000000 | bytes 3000000 | tf_op jit(solution)/shard_map/mixed/pallas_call | solution.py:362
  151.6 0.0 collective-permute-start.7
  151.7 4.1 %fusion = bf16[1,5120,384]{2,1,0:T(8,128)(2,1)} fusion(bf16[384,5120]{1,0:T(8,128)(2,1)S(1)} %copy-done.26, bf16[384,768]{1,0:T(8,128)(2,1)S(1)} %get-tuple-element.24.d_ref), kind=kOutput, calls=%fused_computation.3 | convolution fusion | flops 1511915520 | bytes 8159232 | tf_op jit(solution)/shard_map/dot_general | solution.py:36
  155.8 0.0 collective-permute-done.7
  155.8 3.2 %collective-permute-start.8 = (f32[8,128]{1,0:T(8,128)S(1)}, f32[8,128]{1,0:T(8,128)S(1)}, u32[]{:S(2)}, u32[]{:S(2)}) collective-permute-start(f32[8,128]{1,0:T(8,128)S(1)} %add.6), channel_id=1, source_target_pairs={{0,2},{2,0},{1,3},{3,1},{4,6},{6,4},{5,7},{7,5},{8,10},{10,8},{9,1... | collective-permute-start | bytes 12296 | tf_op jit(solution)/shard_map/ppermute | solution.py:374
  159.0 4.2 %fusion.2 = bf16[1,384,5120]{2,1,0:T(8,128)(2,1)} fusion(bf16[384,384]{1,0:T(8,128)(2,1)S(1)} %get-tuple-element.19.h_ref, bf16[384,5120]{1,0:T(8,128)(2,1)S(1)} %copy-done.11), kind=kOutput, calls=%fused_computation.5 | convolution fusion | flops 1511915520 | bytes 8159232 | tf_op jit(solution)/shard_map/dot_general | solution.py:36
  163.2 0.0 collective-permute-done.8
  163.2 0.6 slice_bitcast_fusion
  163.8 3.8 %all-to-all-done.3 = bf16[64,8,1920]{2,1,0:T(8,128)(2,1)S(1)} async-done(((bf16[64,8,1920]{2,1,0:T(8,128)(2,1)}), bf16[64,8,1920]{2,1,0:T(8,128)(2,1)S(1)}, u32[]{:S(2)}, u32[]{:S(2)}) %all-to-all-start.3) | async-done | bytes 1966112 | tf_op jit(solution)/shard_map/all_to_all | solution.py:369
  167.6 1.3 grad_tokens.1
  (30 shorter events, 0.1 us)
Async XLA Ops:
  0.6 1.0 copy-start.17
  1.6 0.7 copy-start.22
  2.3 0.7 copy-start.24
  3.0 13.6 %copy-start.18 = (bf16[128,1280]{1,0:T(8,128)(2,1)S(1)}, bf16[128,1280]{1,0:T(8,128)(2,1)}, u32[]{:S(2)}) copy-start(bf16[128,1280]{1,0:T(8,128)(2,1)} %cot_ref.3) | copy-start | bytes 983044
  3.0 13.6 %copy-start.23 = (s32[128,6]{0,1:T(8,128)S(1)}, s32[128,6]{0,1:T(8,128)}, u32[]{:S(2)}) copy-start(s32[128,6]{0,1:T(8,128)} %param.9) | copy-start | bytes 9220
  3.7 1.3 copy-start.8
  5.0 39.3 %all-to-all-start = ((bf16[64,8,1920]{2,1,0:T(8,128)(2,1)}), bf16[64,8,1920]{2,1,0:T(8,128)(2,1)S(1)}, u32[]{:S(2)}, u32[]{:S(2)}) async-start(bf16[64,8,1920]{2,1,0:T(8,128)(2,1)} %bitcast.41), calls=%async_computation | async-start | bytes 3932160 | tf_op jit(solution)/shard_map/all_to_all | solution.py:369
  16.5 76.2 %collective-permute-start.2 = (bf16[384,5120]{1,0:T(8,128)(2,1)}, bf16[384,5120]{1,0:T(8,128)(2,1)}, u32[]{:S(2)}, u32[]{:S(2)}) collective-permute-start(bf16[384,5120]{1,0:T(8,128)(2,1)} %bitcast.32), channel_id=1, source_target_pairs={{0,1},{1,0},{2,3},{3,2},{4,5},{5,4},{6,7},{7,6},{8,9},{9,8},{10,11... | collective-permute-start | bytes 11796488 | tf_op jit(solution)/shard_map/ppermute | solution.py:374
  17.4 1.3 copy-start.12
  18.7 0.7 copy-start.15
  19.3 0.7 copy-start.20
  44.3 1.3 copy-start.5
  45.6 32.4 %all-to-all-start.2 = ((bf16[64,8,1920]{2,1,0:T(8,128)(2,1)}), bf16[64,8,1920]{2,1,0:T(8,128)(2,1)S(1)}, u32[]{:S(2)}, u32[]{:S(2)}) async-start(bf16[64,8,1920]{2,1,0:T(8,128)(2,1)} %bitcast.43), calls=%async_computation.2 | async-start | bytes 3932160 | tf_op jit(solution)/shard_map/all_to_all | solution.py:369
  51.6 26.3 %collective-permute-start = (bf16[2,256,1920]{2,1,0:T(8,128)(2,1)}, bf16[2,256,1920]{2,1,0:T(8,128)(2,1)}, u32[]{:S(2)}, u32[]{:S(2)}) collective-permute-start(bf16[2,256,1920]{2,1,0:T(8,128)(2,1)} %bitcast.37), channel_id=1, source_target_pairs={{0,1},{1,0},{2,3},{3,2},{4,5},{5,4},{6,7},{7,6},{8,9},{9,8},{10,11... | collective-permute-start | bytes 5898248 | tf_op jit(solution)/shard_map/ppermute | solution.py:374
  51.7 66.6 %collective-permute-start.5 = (bf16[5120,384]{1,0:T(8,128)(2,1)}, bf16[5120,384]{1,0:T(8,128)(2,1)}, u32[]{:S(2)}, u32[]{:S(2)}) collective-permute-start(bf16[5120,384]{1,0:T(8,128)(2,1)} %bitcast.26), channel_id=1, source_target_pairs={{0,1},{1,0},{2,3},{3,2},{4,5},{5,4},{6,7},{7,6},{8,9},{9,8},{10,11... | collective-permute-start | bytes 11796488 | tf_op jit(solution)/shard_map/ppermute | solution.py:374
  52.2 66.1 %collective-permute-start.6 = (bf16[5120,384]{1,0:T(8,128)(2,1)}, bf16[5120,384]{1,0:T(8,128)(2,1)}, u32[]{:S(2)}, u32[]{:S(2)}) collective-permute-start(bf16[5120,384]{1,0:T(8,128)(2,1)} %bitcast.29), channel_id=1, source_target_pairs={{0,1},{1,0},{2,3},{3,2},{4,5},{5,4},{6,7},{7,6},{8,9},{9,8},{10,11... | collective-permute-start | bytes 11796488 | tf_op jit(solution)/shard_map/ppermute | solution.py:374
  77.9 28.8 %collective-permute-start.3 = (bf16[2,256,1920]{2,1,0:T(8,128)(2,1)S(1)}, bf16[2,256,1920]{2,1,0:T(8,128)(2,1)}, u32[]{:S(2)}, u32[]{:S(2)}) collective-permute-start(bf16[2,256,1920]{2,1,0:T(8,128)(2,1)S(1)} %bitcast.35), channel_id=1, source_target_pairs={{0,1},{1,0},{2,3},{3,2},{4,5},{5,4},{6,7},{7,6},{8,9},{9,8},{10,11... | collective-permute-start | bytes 5898248 | tf_op jit(solution)/shard_map/ppermute | solution.py:374
  77.9 2.1 %copy-start = (bf16[1,5120,384]{2,1,0:T(8,128)(2,1)S(1)}, bf16[1,5120,384]{2,1,0:T(8,128)(2,1)}, u32[]{:S(2)}) copy-start(bf16[1,5120,384]{2,1,0:T(8,128)(2,1)} %param.11) | copy-start | bytes 11796484
  80.1 1.5 copy-start.6
  81.6 12.3 %copy-start.3 = (bf16[1,384,5120]{2,1,0:T(8,128)(2,1)S(1)}, bf16[1,384,5120]{2,1,0:T(8,128)(2,1)}, u32[]{:S(2)}) copy-start(bf16[1,384,5120]{2,1,0:T(8,128)(2,1)} %param.13) | copy-start | bytes 11796484
  90.3 1.9 %copy-start.25 = (bf16[384,5120]{1,0:T(8,128)(2,1)}, bf16[384,5120]{1,0:T(8,128)(2,1)S(1)}, u32[]{:S(2)}) copy-start(bf16[384,5120]{1,0:T(8,128)(2,1)S(1)} %get-tuple-element.26) | copy-start | bytes 11796484
  92.2 6.5 %copy-start.13 = (f32[384,384]{1,0:T(8,128)}, f32[384,384]{1,0:T(8,128)S(1)}, u32[]{:S(2)}) copy-start(f32[384,384]{1,0:T(8,128)S(1)} %get-tuple-element.23.u_ref) | copy-start | bytes 1769476
  92.2 1.7 %collective-permute-start.1 = (bf16[384,384]{1,0:T(8,128)(2,1)S(1)}, bf16[384,384]{1,0:T(8,128)(2,1)S(1)}, u32[]{:S(2)}, u32[]{:S(2)}) collective-permute-start(bf16[384,384]{1,0:T(8,128)(2,1)S(1)} %get-tuple-element.19.h_ref), channel_id=1, source_target_pairs={{0,1},{1,0},{2,3},{3,2},{4,5},{5,4},{6,7},{7,6},{8,9},{9,8},{10,11... | collective-permute-start | bytes 884744 | tf_op jit(solution)/shard_map/ppermute | solution.py:374
  98.7 1.3 copy-start.7
  100.0 35.0 %all-to-all-start.1 = ((bf16[64,8,1920]{2,1,0:T(8,128)(2,1)}), bf16[64,8,1920]{2,1,0:T(8,128)(2,1)}, u32[]{:S(2)}, u32[]{:S(2)}) async-start(bf16[64,8,1920]{2,1,0:T(8,128)(2,1)} %bitcast.40), calls=%async_computation.1 | async-start | bytes 3932160 | tf_op jit(solution)/shard_map/all_to_all | solution.py:369
  106.7 2.1 %copy-start.4 = (bf16[1,384,5120]{2,1,0:T(8,128)(2,1)S(1)}, bf16[1,384,5120]{2,1,0:T(8,128)(2,1)}, u32[]{:S(2)}) copy-start(bf16[1,384,5120]{2,1,0:T(8,128)(2,1)} %param.13) | copy-start | bytes 11796484
  108.8 1.1 copy-start.14
  109.9 10.3 %copy-start.1 = (bf16[1,5120,384]{2,1,0:T(8,128)(2,1)S(1)}, bf16[1,5120,384]{2,1,0:T(8,128)(2,1)}, u32[]{:S(2)}) copy-start(bf16[1,5120,384]{2,1,0:T(8,128)(2,1)} %param.11) | copy-start | bytes 11796484
  109.9 10.3 %copy-start.2 = (bf16[1,5120,384]{2,1,0:T(8,128)(2,1)S(1)}, bf16[1,5120,384]{2,1,0:T(8,128)(2,1)}, u32[]{:S(2)}) copy-start(bf16[1,5120,384]{2,1,0:T(8,128)(2,1)} %param.12) | copy-start | bytes 11796484
  116.3 1.9 %copy-start.10 = (bf16[384,5120]{1,0:T(8,128)(2,1)}, bf16[384,5120]{1,0:T(8,128)(2,1)S(1)}, u32[]{:S(2)}) copy-start(bf16[384,5120]{1,0:T(8,128)(2,1)S(1)} %get-tuple-element.27) | copy-start | bytes 11796484
  118.2 2.0 %collective-permute-start.4 = (bf16[384,768]{1,0:T(8,128)(2,1)S(1)}, bf16[384,768]{1,0:T(8,128)(2,1)S(1)}, u32[]{:S(2)}, u32[]{:S(2)}) collective-permute-start(bf16[384,768]{1,0:T(8,128)(2,1)S(1)} %get-tuple-element.24.d_ref), channel_id=1, source_target_pairs={{0,1},{1,0},{2,3},{3,2},{4,5},{5,4},{6,7},{7,6},{8,9},{9,8},{10,11... | collective-permute-start | bytes 1769480 | tf_op jit(solution)/shard_map/ppermute | solution.py:374
  127.3 1.3 copy-start.9
  134.9 32.7 %all-to-all-start.3 = ((bf16[64,8,1920]{2,1,0:T(8,128)(2,1)}), bf16[64,8,1920]{2,1,0:T(8,128)(2,1)S(1)}, u32[]{:S(2)}, u32[]{:S(2)}) async-start(bf16[64,8,1920]{2,1,0:T(8,128)(2,1)} %bitcast.42), calls=%async_computation.3 | async-start | bytes 3932160 | tf_op jit(solution)/shard_map/all_to_all | solution.py:369
  141.0 6.8 %copy-start.16 = (bf16[512,128]{1,0:T(8,128)(2,1)S(1)}, bf16[512,128]{1,0:T(8,128)(2,1)}, u32[]{:S(2)}) copy-start(bf16[512,128]{1,0:T(8,128)(2,1)} %copy-done.15) | copy-start | bytes 393220
  141.0 6.8 %copy-start.19 = (bf16[128,1280]{1,0:T(8,128)(2,1)S(1)}, bf16[128,1280]{1,0:T(8,128)(2,1)}, u32[]{:S(2)}) copy-start(bf16[128,1280]{1,0:T(8,128)(2,1)} %cot_ref.3) | copy-start | bytes 983044
  141.0 6.8 %copy-start.21 = (f32[512,128]{1,0:T(8,128)S(1)}, f32[512,128]{1,0:T(8,128)}, u32[]{:S(2)}) copy-start(f32[512,128]{1,0:T(8,128)} %copy-done.20) | copy-start | bytes 786436
  141.0 10.7 %copy-start.26 = (bf16[384,5120]{1,0:T(8,128)(2,1)S(1)}, bf16[384,5120]{1,0:T(8,128)(2,1)}, u32[]{:S(2)}) copy-start(bf16[384,5120]{1,0:T(8,128)(2,1)} %copy-done.25) | copy-start | bytes 11796484
  151.6 7.3 %copy-start.11 = (bf16[384,5120]{1,0:T(8,128)(2,1)S(1)}, bf16[384,5120]{1,0:T(8,128)(2,1)}, u32[]{:S(2)}) copy-start(bf16[384,5120]{1,0:T(8,128)(2,1)} %copy-done.10) | copy-start | bytes 11796484
  151.6 4.2 %collective-permute-start.7 = (f32[8,128]{1,0:T(8,128)S(1)}, f32[8,128]{1,0:T(8,128)S(1)}, u32[]{:S(2)}, u32[]{:S(2)}) collective-permute-start(f32[8,128]{1,0:T(8,128)S(1)} %get-tuple-element.25), channel_id=1, source_target_pairs={{0,1},{1,0},{2,3},{3,2},{4,5},{5,4},{6,7},{7,6},{8,9},{9,8},{10,11... | collective-permute-start | bytes 12296 | tf_op jit(solution)/shard_map/ppermute | solution.py:374
  155.8 7.3 %collective-permute-start.8 = (f32[8,128]{1,0:T(8,128)S(1)}, f32[8,128]{1,0:T(8,128)S(1)}, u32[]{:S(2)}, u32[]{:S(2)}) collective-permute-start(f32[8,128]{1,0:T(8,128)S(1)} %add.6), channel_id=1, source_target_pairs={{0,2},{2,0},{1,3},{3,1},{4,6},{6,4},{5,7},{7,5},{8,10},{10,8},{9,1... | collective-permute-start | bytes 12296 | tf_op jit(solution)/shard_map/ppermute | solution.py:374

commit v2 on v1

--- a/solution.py
+++ b/solution.py
@@ -233,10 +233,10 @@
     ids = ids_ref[...]
     for k in range(TOPK):
         gp_ref[k : k + 1, :] = jnp.sum(jnp.where(ids[k : k + 1, :] == expert, each, 0.0), axis=0, keepdims=True)
-    gp_ref[TOPK:, :] = jnp.zeros((8 - TOPK, BLOCK), F32)
-
-
-def _grad_tokens_kernel(pick_ref, r_ref, out_ref):
+
+
+def _grad_tokens_kernel(pick_ref, r_ref, inner_ref, far_ref, out_ref, gp_ref):
+    gp_ref[...] = inner_ref[...] + far_ref[...]
     halves = _home(pick_ref[...], r_ref)
     for h in range(2):
         out_ref[:, h * HALF : (h + 1) * HALF] = halves[h].astype(BF)
@@ -254,8 +254,8 @@
     return jax.ShapeDtypeStruct(shape, dtype)
 
 
-def _src(step):
-    return step // 2
+def _hbm(value):
+    return pltpu.with_memory_space_constraint(value, pltpu.HBM)
 
 
 def _group(step, core):
@@ -288,7 +288,7 @@
             ],
         ),
         out_shape=[
-            _shape((ROWS, D), BF),
+            pltpu.HBM((ROWS, D), BF),
             _shape((ROWS, HID), F32),
             _shape((ROWS, HID), F32),
             _shape((ROWS, HID), BF),
@@ -296,7 +296,7 @@
         compiler_params=_params(),
         cost_estimate=_cost(4 * ROWS * D * HID, 17e6),
         name="forward",
-    )(core, own, other, w_gate, w_up)
+    )(core, _hbm(own), _hbm(other), _hbm(w_gate), _hbm(w_up))
 
 
 def _backward(core, own, other, w_down, gate, up):
@@ -317,11 +317,11 @@
             ],
             scratch_shapes=[pltpu.VMEM((ROWS, HID), F32)],
         ),
-        out_shape=[_shape((ROWS, D), BF), _shape((ROWS, 2 * HID), BF)],
+        out_shape=[pltpu.HBM((ROWS, D), BF), _shape((ROWS, 2 * HID), BF)],
         compiler_params=_params(),
         cost_estimate=_cost(2 * ROWS * D * HID, 14e6),
         name="backward",
-    )(core, own, other, w_down, gate, up)
+    )(core, _hbm(own), _hbm(other), _hbm(w_down), gate, up)
 
 
 def _result(core, hidden, hidden_p, w_down, w_down_p):
@@ -334,11 +334,11 @@
             in_specs=[_fixed(ROWS, HID), _fixed(ROWS, HID), weight, weight],
             out_specs=pl.BlockSpec((1, MAIN, WIDE), lambda i, c: (i, 0, 0)),
         ),
-        out_shape=_shape((2, MAIN, WIDE), BF),
+        out_shape=pltpu.HBM((2, MAIN, WIDE), BF),
         compiler_params=_params(),
         cost_estimate=_cost(2 * ROWS * D * HID, 7e6),
         name="result",
-    )(core, hidden, hidden_p, w_down, w_down_p)
+    )(core, hidden, hidden_p, _hbm(w_down), _hbm(w_down_p))
 
 
 def _back(core, grads, grads_p, w_gate, w_up, w_gate_p, w_up_p):
@@ -351,11 +351,11 @@
             in_specs=[_fixed(ROWS, 2 * HID), _fixed(ROWS, 2 * HID), weight, weight, weight, weight],
             out_specs=pl.BlockSpec((1, MAIN, WIDE), lambda i, c: (i, 0, 0)),
         ),
-        out_shape=_shape((2, MAIN, WIDE), BF),
+        out_shape=pltpu.HBM((2, MAIN, WIDE), BF),
         compiler_params=_params(),
         cost_estimate=_cost(4 * ROWS * D * HID, 11e6),
         name="back",
-    )(core, grads, grads_p, w_gate, w_up, w_gate_p, w_up_p)
+    )(core, grads, grads_p, _hbm(w_gate), _hbm(w_up), _hbm(w_gate_p), _hbm(w_up_p))
 
 
 def _local(kernel, out_shape, flops, moved, name, *args):
@@ -379,23 +379,25 @@
     wg, wu, wd = w_gate[0], w_up[0], w_down[0]
     ids_t, probs_t = expert_ids.T, route_probs.T
 
-    send_x = _local(_pack_rows_kernel, _shape((2, MAIN, WIDE), BF), 2e8, 3e6, "pack_rows", ids_t, probs_t, tokens)
+    send_x = _local(_pack_rows_kernel, pltpu.HBM((2, MAIN, WIDE), BF), 2e8, 3e6, "pack_rows", _hbm(ids_t), _hbm(probs_t), _hbm(tokens))
     recv_x = _exchange(send_x)
     send_e, pick, weight = _local(
         _pack_grads_kernel,
-        [_shape((2, MAIN, WIDE), BF), _shape((2 * MAIN, BLOCK), BF), _shape((2 * MAIN, BLOCK), F32)],
+        [pltpu.HBM((2, MAIN, WIDE), BF), _shape((2 * MAIN, BLOCK), BF), _shape((2 * MAIN, BLOCK), F32)],
         2e8,
         3e6,
         "pack_grads",
-        ids_t,
-        probs_t,
-        cotangent,
+        _hbm(ids_t),
+        _hbm(probs_t),
+        _hbm(cotangent),
     )
     wd_p, wg_p, wu_p = _swap(wd), _swap(wg), _swap(wu)
+    recv_x, send_e = lax.optimization_barrier((recv_x, send_e))
     recv_e = _exchange(send_e)
 
     x, gate, up, hidden = _forward(core, recv_x, _swap(recv_x), wg, wu)
     send_o = _result(core, hidden, _swap(hidden), wd, wd_p)
+    recv_e, send_o = lax.optimization_barrier((recv_e, send_o))
     recv_o = _exchange(send_o)
 
     e, grads = _backward(core, recv_e, _swap(recv_e), wd, gate, up)
@@ -408,7 +410,7 @@
 
     mixed, inner = _local(
         _mixed_kernel,
-        [_shape((BLOCK, COLS), BF), _shape((8, BLOCK), F32)],
+        [_shape((BLOCK, COLS), BF), _shape((TOPK, BLOCK), F32)],
         4e8,
         3e6,
         "mixed",
@@ -416,14 +418,23 @@
         pick,
         weight,
         cotangent,
-        recv_o,
+        _hbm(recv_o),
     )
     inner = inner + _swap(inner)
-    inner = inner + _swap(inner, "yhi")
-    grad_probs = inner[:TOPK].T
-
-    grad_tokens = _local(_grad_tokens_kernel, _shape((BLOCK, COLS), BF), 2e8, 3e6, "grad_tokens", pick, recv_b)
-    return mixed, grad_tokens, grad_probs, g_gate[None], g_up[None], g_down[None]
+    far = _swap(inner, "yhi")
+    recv_b, g_gate, g_up, g_down = lax.optimization_barrier((recv_b, g_gate, g_up, g_down))
+    grad_tokens, grad_probs = _local(
+        _grad_tokens_kernel,
+        [_shape((BLOCK, COLS), BF), _shape((TOPK, BLOCK), F32)],
+        2e8,
+        3e6,
+        "grad_tokens",
+        pick,
+        recv_b,
+        inner,
+        far,
+    )
+    return mixed, grad_tokens, grad_probs.T, g_gate[None], g_up[None], g_down[None]
 
 
 def solution(mesh):

time: 170 us -> 147 us (0.86)
  local copies, waits for them, and re-layouts: 21.3 us -> 1.67 us
  waiting for transfers between devices: 63.2 us -> 50.2 us
  Pallas kernels: 33.6 us -> 44.3 us
    unnamed x54 -> x14, local copies, waits for them, and re-layouts: 20.7 us -> 1.67 us
    all_to_all x4, waiting for transfers between devices: 60 us -> 45.5 us  [_exchange(): lax.all_to_all(chunks, ('yhi', 'expert'), split_axis=0, concat_axis=0, ti...]
    pallas_call x4, Pallas kernels: 6.7 us -> 11.3 us  [_local(): pl.pallas_call(kernel, out_shape=out_shape, compiler_params=_params(), co...]
    pallas_call x1, Pallas kernels: 6.41 us -> 8.23 us  [_backward(): pl.pallas_call(_backward_kernel, grid_spec=pltpu.PrefetchScalarGridSpec(n...]
  transfers between devices with their start and end apart: 13 -> 13, of which waited for: 6 -> 7; matrix products, arithmetic and copies ran while one was open for 9% -> 10% of each run, Pallas kernels for 19% -> 27%
where the time goes in v2:
time: 147 us
  waiting for transfers between devices  50.2 us (34%)
  Pallas kernels  44.3 us (30%)
  starting transfers between devices  34.6 us (24%)
  matrix products  15.1 us (10%)
  local copies, waits for them, and re-layouts  1.67 us (1%)
    all_to_all x4, waiting for transfers between devices, _exchange(): lax.all_to_all(chunks, ('yhi', 'expert'), split_axis=0, concat_axis=0, ti...  45.5 us
    all_to_all x4, starting transfers between devices, _exchange(): lax.all_to_all(chunks, ('yhi', 'expert'), split_axis=0, concat_axis=0, ti...  30.3 us
    dot_general x3, matrix products, _dot_tn(): lax.dot_general(a, b, (((0,), (0,)), ((), ())), preferred_element_type=F32)  15.1 us
    pallas_call x4, Pallas kernels, _local(): pl.pallas_call(kernel, out_shape=out_shape, compiler_params=_params(), co...  11.3 us
    pallas_call x1, Pallas kernels, _forward(): pl.pallas_call(_forward_kernel, grid_spec=pltpu.PrefetchScalarGridSpec(nu...  10.3 us
    pallas_call x1, Pallas kernels, _back(): pl.pallas_call(_back_kernel, grid_spec=pltpu.PrefetchScalarGridSpec(num_s...  8.62 us
    pallas_call x1, Pallas kernels, _backward(): pl.pallas_call(_backward_kernel, grid_spec=pltpu.PrefetchScalarGridSpec(n...  8.23 us
    pallas_call x1, Pallas kernels, _result(): pl.pallas_call(_result_kernel, grid_spec=pltpu.PrefetchScalarGridSpec(num...  5.93 us
  transfers between devices with their start and end apart: 13, of which 7 were waited for; matrix products, arithmetic and copies ran while one was open for 10% of the time, Pallas kernels for 27%

profile of v2, /device:TPU:0, one launch (start us, length us, event | category | flops | bytes accessed | tf_op | source)
XLA Modules:
  0.0 146.6 jit_solution(17070548967840705937)
XLA Ops:
  0.6 3.0 %pack_rows.1 = bf16[2,256,1920]{2,1,0:T(8,128)(2,1)} custom-call(s32[6,128]{1,0:T(8,128)} %bitcast.23, f32[6,128]{1,0:T(8,128)} %bitcast.42, bf16[128,1280]{1,0:T(8,128)(2,1)} %tok_ref.1), custom_call_target="tpu_custom_call" | custom-call | flops 200000000 | bytes 3000000 | tf_op jit(solution)/shard_map/pack_rows/pallas_call | solution.py:362
  3.6 11.5 %all-to-all-start = ((bf16[64,8,1920]{2,1,0:T(8,128)(2,1)}), bf16[64,8,1920]{2,1,0:T(8,128)(2,1)S(1)}, u32[]{:S(2)}, u32[]{:S(2)}) async-start(bf16[64,8,1920]{2,1,0:T(8,128)(2,1)} %bitcast.38), calls=%async_computation | async-start | bytes 3932160 | tf_op jit(solution)/shard_map/all_to_all | solution.py:369
  15.2 0.1 collective-permute-start.2
  15.3 3.1 %pack_grads.1 = (bf16[2,256,1920]{2,1,0:T(8,128)(2,1)}, bf16[512,128]{1,0:T(8,128)(2,1)S(1)}, f32[512,128]{1,0:T(8,128)S(1)}) custom-call(s32[6,128]{1,0:T(8,128)} %bitcast.24, f32[6,128]{1,0:T(8,128)} %bitcast.43, bf16[128,1280]{1,0:T(8,128)(2,1)} %cot_ref.3), custom_call_target="tpu_custom_call" | custom-call | flops 200000000 | bytes 3000000 | tf_op jit(solution)/shard_map/pack_grads/pallas_call | solution.py:362
  18.3 0.0 copy-start.1
  18.3 0.7 copy-done.1
  19.0 23.9 %all-to-all-done = bf16[64,8,1920]{2,1,0:T(8,128)(2,1)S(1)} async-done(((bf16[64,8,1920]{2,1,0:T(8,128)(2,1)}), bf16[64,8,1920]{2,1,0:T(8,128)(2,1)S(1)}, u32[]{:S(2)}, u32[]{:S(2)}) %all-to-all-start) | async-done | bytes 1966112 | tf_op jit(solution)/shard_map/all_to_all | solution.py:369
  42.9 0.0 copy-start.4
  43.0 0.0 collective-permute-start
  43.0 6.3 %all-to-all-start.1 = ((bf16[64,8,1920]{2,1,0:T(8,128)(2,1)}), bf16[64,8,1920]{2,1,0:T(8,128)(2,1)}, u32[]{:S(2)}, u32[]{:S(2)}) async-start(bf16[64,8,1920]{2,1,0:T(8,128)(2,1)} %bitcast.41), calls=%async_computation.1 | async-start | bytes 3932160 | tf_op jit(solution)/shard_map/all_to_all | solution.py:369
  49.2 0.3 collective-permute-start.5
  49.5 0.3 collective-permute-start.6
  49.8 0.0 collective-permute-done.other_ref
  49.8 0.0 copy-done.4
  49.8 10.3 %forward.1 = (bf16[384,5120]{1,0:T(8,128)(2,1)}, f32[384,384]{1,0:T(8,128)S(1)}, f32[384,384]{1,0:T(8,128)S(1)}, bf16[384,384]{1,0:T(8,128)(2,1)S(1)}) custom-call(s32[1]{0:T(128)} %bitcast.6.core_ref, bf16[2,256,1920]{2,1,0:T(8,128)(2,1)} %bitcast.36, bf16[2,256,1920]{2,1,0:T(8,128)(2,1)} %collective-permute-done.other_ref, bf16[5120,384]{1,0:T(8,128)(2,1)} %bitcast.27, ...), custom_call_target="tpu_custom_call" | custom-call | flops 3019898880 | bytes 17000000 | tf_op jit(solution)/shard_map/forward/pallas_call | solution.py:277
  60.1 0.2 collective-permute-start.1
  60.3 0.0 collective-permute-done.2.wdp_ref
  60.3 1.8 %collective-permute-done.1.hp_ref = bf16[384,384]{1,0:T(8,128)(2,1)S(1)} collective-permute-done((bf16[384,384]{1,0:T(8,128)(2,1)S(1)}, bf16[384,384]{1,0:T(8,128)(2,1)S(1)}, u32[]{:S(2)}, u32[]{:S(2)}) %collective-permute-start.1) | collective-permute-done | bytes 294944 | tf_op jit(solution)/shard_map/ppermute | solution.py:374
  62.1 5.9 %result.1 = bf16[2,256,1920]{2,1,0:T(8,128)(2,1)} custom-call(s32[1]{0:T(128)} %bitcast.6.core_ref, bf16[384,384]{1,0:T(8,128)(2,1)S(1)} %get-tuple-element.32.h_ref, bf16[384,384]{1,0:T(8,128)(2,1)S(1)} %collective-permute-done.1.hp_ref, bf16[384,5120]{1,0:T(8,128)(2,1)} %bitcast.33, bf16[384,5120]{1,0:T(8,128)(2,1)} %collective-permute-done.2.wdp_ref), custom_call_target="tpu_custom_call" | custom-call | flops 1509949440 | bytes 7000000 | tf_op jit(solution)/shard_map/result/pallas_call | solution.py:329
  68.1 9.5 %all-to-all-done.1 = bf16[64,8,1920]{2,1,0:T(8,128)(2,1)} async-done(((bf16[64,8,1920]{2,1,0:T(8,128)(2,1)}), bf16[64,8,1920]{2,1,0:T(8,128)(2,1)}, u32[]{:S(2)}, u32[]{:S(2)}) %all-to-all-start.1) | async-done | bytes 1966112 | tf_op jit(solution)/shard_map/all_to_all | solution.py:369
  77.6 0.0 collective-permute-start.3
  77.6 6.4 %all-to-all-start.2 = ((bf16[64,8,1920]{2,1,0:T(8,128)(2,1)}), bf16[64,8,1920]{2,1,0:T(8,128)(2,1)}, u32[]{:S(2)}, u32[]{:S(2)}) async-start(bf16[64,8,1920]{2,1,0:T(8,128)(2,1)} %bitcast.37), calls=%async_computation.2 | async-start | bytes 3932160 | tf_op jit(solution)/shard_map/all_to_all | solution.py:369
  83.9 0.0 collective-permute-done.3.other_ref
  83.9 8.2 %backward.1 = (bf16[384,5120]{1,0:T(8,128)(2,1)}, bf16[384,768]{1,0:T(8,128)(2,1)S(1)}) custom-call(s32[1]{0:T(128)} %bitcast.6.core_ref, bf16[2,256,1920]{2,1,0:T(8,128)(2,1)} %bitcast.5.own_ref, bf16[2,256,1920]{2,1,0:T(8,128)(2,1)} %collective-permute-done.3.other_ref, bf16[384,5120]{1,0:T(8,128)(2,1)} %bitcast.34, ...), custom_call_target="tpu_custom_call" | custom-call | flops 1509949440 | bytes 14000000 | tf_op jit(solution)/shard_map/backward/pallas_call | solution.py:303
  92.2 0.3 collective-permute-start.4
  92.4 0.0 collective-permute-done.5.wgp_ref
  92.4 0.0 collective-permute-done.6.wup_ref
  92.4 1.7 %collective-permute-done.4.dp_ref = bf16[384,768]{1,0:T(8,128)(2,1)S(1)} collective-permute-done((bf16[384,768]{1,0:T(8,128)(2,1)S(1)}, bf16[384,768]{1,0:T(8,128)(2,1)S(1)}, u32[]{:S(2)}, u32[]{:S(2)}) %collective-permute-start.4) | collective-permute-done | bytes 589856 | tf_op jit(solution)/shard_map/ppermute | solution.py:374
  94.2 8.6 %back.1 = bf16[2,256,1920]{2,1,0:T(8,128)(2,1)} custom-call(s32[1]{0:T(128)} %bitcast.6.core_ref, bf16[384,768]{1,0:T(8,128)(2,1)S(1)} %get-tuple-element.38.d_ref, bf16[384,768]{1,0:T(8,128)(2,1)S(1)} %collective-permute-done.4.dp_ref, bf16[5120,384]{1,0:T(8,128)(2,1)} %bitcast.28, bf16[5120,384]{1,0:T(8,128)(2,1)} %bitcast.31, ...), custom_call_target="tpu_custom_call" | custom-call | flops 3019898880 | bytes 11000000 | tf_op jit(solution)/shard_map/back/pallas_call | solution.py:346
  102.8 0.0 copy-start
  102.8 0.0 copy-start.3
  102.8 9.5 %all-to-all-done.2 = bf16[64,8,1920]{2,1,0:T(8,128)(2,1)} async-done(((bf16[64,8,1920]{2,1,0:T(8,128)(2,1)}), bf16[64,8,1920]{2,1,0:T(8,128)(2,1)}, u32[]{:S(2)}, u32[]{:S(2)}) %all-to-all-start.2) | async-done | bytes 1966112 | tf_op jit(solution)/shard_map/all_to_all | solution.py:369
  112.3 6.1 %all-to-all-start.3 = ((bf16[64,8,1920]{2,1,0:T(8,128)(2,1)}), bf16[64,8,1920]{2,1,0:T(8,128)(2,1)S(1)}, u32[]{:S(2)}, u32[]{:S(2)}) async-start(bf16[64,8,1920]{2,1,0:T(8,128)(2,1)} %bitcast.39), calls=%async_computation.3 | async-start | bytes 3932160 | tf_op jit(solution)/shard_map/all_to_all | solution.py:369
  118.4 0.0 copy-done
  118.4 0.0 copy-done.3
  118.4 0.0 copy-start.2
  118.5 0.9 copy-done.2
  119.4 3.8 %mixed.1 = (bf16[128,1280]{1,0:T(8,128)(2,1)}, f32[6,128]{1,0:T(8,128)S(1)}) custom-call(s32[6,128]{1,0:T(8,128)S(1)} %bitcast.25, bf16[512,128]{1,0:T(8,128)(2,1)S(1)} %get-tuple-element.27.pick_ref, f32[512,128]{1,0:T(8,128)S(1)} %copy-done.2, bf16[128,1280]{1,0:T(8,128)(2,1)S(1)} %copy-done, bf16[2,256,1920]{2,1,0:T(8,128)(2,1)} %bitcast.11.r_ref), custom_call_target="tpu_custom_call" | custom-call | flops 400000000 | bytes 3000000 | tf_op jit(solution)/shard_map/mixed/pallas_call | solution.py:362
  123.2 0.0 collective-permute-start.7
  123.2 1.2 collective-permute-done.7
  124.4 3.2 %collective-permute-start.8 = (f32[6,128]{1,0:T(8,128)S(1)}, f32[6,128]{1,0:T(8,128)S(1)}, u32[]{:S(2)}, u32[]{:S(2)}) collective-permute-start(f32[6,128]{1,0:T(8,128)S(1)} %add.3.inner_ref), channel_id=1, source_target_pairs={{0,2},{2,0},{1,3},{3,1},{4,6},{6,4},{5,7},{7,5},{8,10},{10,8},{9,1... | collective-permute-start | bytes 9224 | tf_op jit(solution)/shard_map/ppermute | solution.py:374
  127.6 0.0 copy-start.6
  127.6 6.8 %convolution_convert_fusion.2 = bf16[5120,384]{1,0:T(8,128)(2,1)} fusion(bf16[384,5120]{1,0:T(8,128)(2,1)} %get-tuple-element.39, bf16[384,768]{1,0:T(8,128)(2,1)S(1)} %get-tuple-element.38.d_ref), kind=kOutput, calls=%fused_computation.2 | convolution fusion | flops 1511915520 | bytes 8159232 | tf_op jit(solution)/shard_map/dot_general | solution.py:36
  134.4 0.0 copy-done.6
  134.4 0.0 copy-start.5
  134.4 4.1 %convolution_convert_fusion.1 = bf16[5120,384]{1,0:T(8,128)(2,1)} fusion(bf16[384,5120]{1,0:T(8,128)(2,1)S(1)} %copy-done.6, bf16[384,768]{1,0:T(8,128)(2,1)S(1)} %get-tuple-element.38.d_ref), kind=kOutput, calls=%fused_computation.1 | convolution fusion | flops 1511915520 | bytes 8159232 | tf_op jit(solution)/shard_map/dot_general | solution.py:36
  138.5 0.0 copy-done.5
  138.5 4.2 %convolution_convert_fusion = bf16[384,5120]{1,0:T(8,128)(2,1)} fusion(bf16[384,384]{1,0:T(8,128)(2,1)S(1)} %get-tuple-element.32.h_ref, bf16[384,5120]{1,0:T(8,128)(2,1)S(1)} %copy-done.5), kind=kOutput, calls=%fused_computation | convolution fusion | flops 1511915520 | bytes 8159232 | tf_op jit(solution)/shard_map/dot_general | solution.py:36
  142.7 2.6 %all-to-all-done.3 = bf16[64,8,1920]{2,1,0:T(8,128)(2,1)S(1)} async-done(((bf16[64,8,1920]{2,1,0:T(8,128)(2,1)}), bf16[64,8,1920]{2,1,0:T(8,128)(2,1)S(1)}, u32[]{:S(2)}, u32[]{:S(2)}) %all-to-all-start.3) | async-done | bytes 1966112 | tf_op jit(solution)/shard_map/all_to_all | solution.py:369
  145.2 0.0 collective-permute-done.8.far_ref
  145.2 1.3 grad_tokens.1
  (1 shorter events, 0.0 us)
Async XLA Ops:
  3.6 39.3 %all-to-all-start = ((bf16[64,8,1920]{2,1,0:T(8,128)(2,1)}), bf16[64,8,1920]{2,1,0:T(8,128)(2,1)S(1)}, u32[]{:S(2)}, u32[]{:S(2)}) async-start(bf16[64,8,1920]{2,1,0:T(8,128)(2,1)} %bitcast.38), calls=%async_computation | async-start | bytes 3932160 | tf_op jit(solution)/shard_map/all_to_all | solution.py:369
  15.2 45.2 %collective-permute-start.2 = (bf16[384,5120]{1,0:T(8,128)(2,1)}, bf16[384,5120]{1,0:T(8,128)(2,1)}, u32[]{:S(2)}, u32[]{:S(2)}) collective-permute-start(bf16[384,5120]{1,0:T(8,128)(2,1)} %bitcast.32), channel_id=1, source_target_pairs={{0,1},{1,0},{2,3},{3,2},{4,5},{5,4},{6,7},{7,6},{8,9},{9,8},{10,11... | collective-permute-start | bytes 11796488 | tf_op jit(solution)/shard_map/ppermute | solution.py:374
  18.3 0.7 copy-start.1
  42.9 6.9 %copy-start.4 = (bf16[64,8,1920]{2,1,0:T(8,128)(2,1)}, bf16[64,8,1920]{2,1,0:T(8,128)(2,1)S(1)}, u32[]{:S(2)}) copy-start(bf16[64,8,1920]{2,1,0:T(8,128)(2,1)S(1)} %all-to-all-done) | copy-start | bytes 5898244
  43.0 6.9 %collective-permute-start = (bf16[2,256,1920]{2,1,0:T(8,128)(2,1)S(1)}, bf16[2,256,1920]{2,1,0:T(8,128)(2,1)}, u32[]{:S(2)}, u32[]{:S(2)}) collective-permute-start(bf16[2,256,1920]{2,1,0:T(8,128)(2,1)S(1)} %bitcast.35), channel_id=1, source_target_pairs={{0,1},{1,0},{2,3},{3,2},{4,5},{5,4},{6,7},{7,6},{8,9},{9,8},{10,11... | collective-permute-start | bytes 5898248 | tf_op jit(solution)/shard_map/ppermute | solution.py:374
  43.0 34.6 %all-to-all-start.1 = ((bf16[64,8,1920]{2,1,0:T(8,128)(2,1)}), bf16[64,8,1920]{2,1,0:T(8,128)(2,1)}, u32[]{:S(2)}, u32[]{:S(2)}) async-start(bf16[64,8,1920]{2,1,0:T(8,128)(2,1)} %bitcast.41), calls=%async_computation.1 | async-start | bytes 3932160 | tf_op jit(solution)/shard_map/all_to_all | solution.py:369
  49.2 43.2 %collective-permute-start.5 = (bf16[5120,384]{1,0:T(8,128)(2,1)}, bf16[5120,384]{1,0:T(8,128)(2,1)}, u32[]{:S(2)}, u32[]{:S(2)}) collective-permute-start(bf16[5120,384]{1,0:T(8,128)(2,1)} %bitcast.26), channel_id=1, source_target_pairs={{0,1},{1,0},{2,3},{3,2},{4,5},{5,4},{6,7},{7,6},{8,9},{9,8},{10,11... | collective-permute-start | bytes 11796488 | tf_op jit(solution)/shard_map/ppermute | solution.py:374
  49.5 42.9 %collective-permute-start.6 = (bf16[5120,384]{1,0:T(8,128)(2,1)}, bf16[5120,384]{1,0:T(8,128)(2,1)}, u32[]{:S(2)}, u32[]{:S(2)}) collective-permute-start(bf16[5120,384]{1,0:T(8,128)(2,1)} %bitcast.29), channel_id=1, source_target_pairs={{0,1},{1,0},{2,3},{3,2},{4,5},{5,4},{6,7},{7,6},{8,9},{9,8},{10,11... | collective-permute-start | bytes 11796488 | tf_op jit(solution)/shard_map/ppermute | solution.py:374
  60.1 2.0 %collective-permute-start.1 = (bf16[384,384]{1,0:T(8,128)(2,1)S(1)}, bf16[384,384]{1,0:T(8,128)(2,1)S(1)}, u32[]{:S(2)}, u32[]{:S(2)}) collective-permute-start(bf16[384,384]{1,0:T(8,128)(2,1)S(1)} %get-tuple-element.32.h_ref), channel_id=1, source_target_pairs={{0,1},{1,0},{2,3},{3,2},{4,5},{5,4},{6,7},{7,6},{8,9},{9,8},{10,11... | collective-permute-start | bytes 884744 | tf_op jit(solution)/shard_map/ppermute | solution.py:374
  77.6 6.4 %collective-permute-start.3 = (bf16[2,256,1920]{2,1,0:T(8,128)(2,1)}, bf16[2,256,1920]{2,1,0:T(8,128)(2,1)}, u32[]{:S(2)}, u32[]{:S(2)}) collective-permute-start(bf16[2,256,1920]{2,1,0:T(8,128)(2,1)} %bitcast.5.own_ref), channel_id=1, source_target_pairs={{0,1},{1,0},{2,3},{3,2},{4,5},{5,4},{6,7},{7,6},{8,9},{9,8},{10,11... | collective-permute-start | bytes 5898248 | tf_op jit(solution)/shard_map/ppermute | solution.py:374
  77.6 34.7 %all-to-all-start.2 = ((bf16[64,8,1920]{2,1,0:T(8,128)(2,1)}), bf16[64,8,1920]{2,1,0:T(8,128)(2,1)}, u32[]{:S(2)}, u32[]{:S(2)}) async-start(bf16[64,8,1920]{2,1,0:T(8,128)(2,1)} %bitcast.37), calls=%async_computation.2 | async-start | bytes 3932160 | tf_op jit(solution)/shard_map/all_to_all | solution.py:369
  92.2 2.0 %collective-permute-start.4 = (bf16[384,768]{1,0:T(8,128)(2,1)S(1)}, bf16[384,768]{1,0:T(8,128)(2,1)S(1)}, u32[]{:S(2)}, u32[]{:S(2)}) collective-permute-start(bf16[384,768]{1,0:T(8,128)(2,1)S(1)} %get-tuple-element.38.d_ref), channel_id=1, source_target_pairs={{0,1},{1,0},{2,3},{3,2},{4,5},{5,4},{6,7},{7,6},{8,9},{9,8},{10,11... | collective-permute-start | bytes 1769480 | tf_op jit(solution)/shard_map/ppermute | solution.py:374
  102.8 15.6 %copy-start = (bf16[128,1280]{1,0:T(8,128)(2,1)S(1)}, bf16[128,1280]{1,0:T(8,128)(2,1)}, u32[]{:S(2)}) copy-start(bf16[128,1280]{1,0:T(8,128)(2,1)} %cot_ref.3) | copy-start | bytes 983044
  102.8 15.6 %copy-start.3 = (s32[128,6]{0,1:T(8,128)S(1)}, s32[128,6]{0,1:T(8,128)}, u32[]{:S(2)}) copy-start(s32[128,6]{0,1:T(8,128)} %param.9) | copy-start | bytes 9220
  112.3 33.0 %all-to-all-start.3 = ((bf16[64,8,1920]{2,1,0:T(8,128)(2,1)}), bf16[64,8,1920]{2,1,0:T(8,128)(2,1)S(1)}, u32[]{:S(2)}, u32[]{:S(2)}) async-start(bf16[64,8,1920]{2,1,0:T(8,128)(2,1)} %bitcast.39), calls=%async_computation.3 | async-start | bytes 3932160 | tf_op jit(solution)/shard_map/all_to_all | solution.py:369
  118.4 1.0 copy-start.2
  123.2 1.2 collective-permute-start.7
  124.4 20.8 %collective-permute-start.8 = (f32[6,128]{1,0:T(8,128)S(1)}, f32[6,128]{1,0:T(8,128)S(1)}, u32[]{:S(2)}, u32[]{:S(2)}) collective-permute-start(f32[6,128]{1,0:T(8,128)S(1)} %add.3.inner_ref), channel_id=1, source_target_pairs={{0,2},{2,0},{1,3},{3,1},{4,6},{6,4},{5,7},{7,5},{8,10},{10,8},{9,1... | collective-permute-start | bytes 9224 | tf_op jit(solution)/shard_map/ppermute | solution.py:374
  127.6 6.8 %copy-start.6 = (bf16[384,5120]{1,0:T(8,128)(2,1)S(1)}, bf16[384,5120]{1,0:T(8,128)(2,1)}, u32[]{:S(2)}) copy-start(bf16[384,5120]{1,0:T(8,128)(2,1)} %get-tuple-element.39) | copy-start | bytes 11796484
  134.4 4.1 %copy-start.5 = (bf16[384,5120]{1,0:T(8,128)(2,1)S(1)}, bf16[384,5120]{1,0:T(8,128)(2,1)}, u32[]{:S(2)}) copy-start(bf16[384,5120]{1,0:T(8,128)(2,1)} %get-tuple-element.40) | copy-start | bytes 11796484

commit v3 on v2

--- a/solution.py
+++ b/solution.py
@@ -22,6 +22,8 @@
 WIDE = COLS + HALF
 D = 4 * COLS
 VMEM = 40 * 1024 * 1024
+EARLY = 16
+LATE = 1 / 128
 
 
 def _dot(a, b):
@@ -125,61 +127,65 @@
     out_ref[0, :, COLS:] = (_dot(_fold_t(0), rest[:, :HALF]) + _dot(_fold_t(1), rest[:, HALF:])).astype(BF)
 
 
-def _forward_kernel(core_ref, own_ref, other_ref, wg_ref, wu_ref, x_ref, g_ref, u_ref, h_ref):
-    step = pl.program_id(0)
-
-    @pl.when(step < 2)
-    def _():
-        _unpack(own_ref, x_ref)
-
-    @pl.when(step >= 2)
-    def _():
-        _unpack(other_ref, x_ref)
-
-    x = x_ref[...]
-    g = _dot(x, wg_ref[...])
-    u = _dot(x, wu_ref[...])
-
-    @pl.when(step == 0)
+def _forward_own_kernel(core_ref, r_ref, wg_ref, wu_ref, x_ref, g_ref, u_ref):
+    _unpack(r_ref, x_ref)
+    g = _dot(x_ref[...], wg_ref[...])
+    u = _dot(x_ref[...], wu_ref[...])
+
+    @pl.when(pl.program_id(0) == 0)
     def _():
         g_ref[...] = g
         u_ref[...] = u
 
-    @pl.when(step > 0)
+    @pl.when(pl.program_id(0) > 0)
     def _():
         g_ref[...] += g
         u_ref[...] += u
 
-    @pl.when(step == 3)
-    def _():
-        gate = g_ref[...]
-        h_ref[...] = (gate * jax.nn.sigmoid(gate) * u_ref[...]).astype(BF)
-
-
-def _backward_kernel(core_ref, own_ref, other_ref, wd_ref, g_ref, u_ref, e_ref, d_ref, a_ref):
-    step = pl.program_id(0)
-
-    @pl.when(step < 2)
-    def _():
-        _unpack(own_ref, e_ref)
-
-    @pl.when(step >= 2)
-    def _():
-        _unpack(other_ref, e_ref)
-
+
+def _forward_other_kernel(core_ref, r_ref, wg_ref, wu_ref, g0_ref, u0_ref, x0_ref, x_ref, g_ref, u_ref, h_ref):
+    _unpack(r_ref, x_ref)
+    g = _dot(x_ref[...], wg_ref[...])
+    u = _dot(x_ref[...], wu_ref[...])
+
+    @pl.when(pl.program_id(0) == 0)
+    def _():
+        g_ref[...] = g0_ref[...] + g
+        u_ref[...] = u0_ref[...] + u
+
+    @pl.when(pl.program_id(0) > 0)
+    def _():
+        gate = g_ref[...] + g
+        up = u_ref[...] + u
+        g_ref[...] = gate
+        u_ref[...] = up
+        h_ref[...] = (gate * jax.nn.sigmoid(gate) * up).astype(BF)
+
+
+def _backward_own_kernel(core_ref, r_ref, wd_ref, e_ref, a_ref):
+    _unpack(r_ref, e_ref)
     a = _dot_nt(e_ref[...], wd_ref[...])
 
-    @pl.when(step == 0)
+    @pl.when(pl.program_id(0) == 0)
     def _():
         a_ref[...] = a
 
-    @pl.when(step > 0)
+    @pl.when(pl.program_id(0) > 0)
     def _():
         a_ref[...] += a
 
-    @pl.when(step == 3)
-    def _():
-        total, gate = a_ref[...], g_ref[...]
+
+def _backward_other_kernel(core_ref, r_ref, wd_ref, a0_ref, g_ref, u_ref, e0_ref, e_ref, d_ref, a_ref):
+    _unpack(r_ref, e_ref)
+    a = _dot_nt(e_ref[...], wd_ref[...])
+
+    @pl.when(pl.program_id(0) == 0)
+    def _():
+        a_ref[...] = a0_ref[...] + a
+
+    @pl.when(pl.program_id(0) > 0)
+    def _():
+        total, gate = a_ref[...] + a, g_ref[...]
         s = jax.nn.sigmoid(gate)
         d_ref[:, :HID] = (total * u_ref[...] * s * (1.0 + gate * (1.0 - s))).astype(BF)
         d_ref[:, HID:] = (total * (gate * s)).astype(BF)
@@ -258,70 +264,101 @@
     return pltpu.with_memory_space_constraint(value, pltpu.HBM)
 
 
-def _group(step, core):
-    return (step % 2) * 2 + jnp.where(step < 2, core, 1 - core)
-
-
-def _received():
-    own = pl.BlockSpec((1, MAIN, WIDE), lambda i, c: (jnp.minimum(i, 1), 0, 0))
-    other = pl.BlockSpec((1, MAIN, WIDE), lambda i, c: (jnp.maximum(i - 2, 0), 0, 0))
-    return own, other
-
-
 def _fixed(*shape):
     return pl.BlockSpec(shape, lambda i, c: (0,) * len(shape))
 
 
-def _forward(core, own, other, w_gate, w_up):
-    weight = pl.BlockSpec((COLS, HID), lambda i, c: (_group(i, c[0]), 0))
+def _half_pass(kernel, other, weights, state, out, scratch, flops, moved, name, aliases={}):
+    def group(i, c):
+        return 2 * i + (1 - c[0] if other else c[0])
+
+    block = {
+        "row": pl.BlockSpec((COLS, HID), lambda i, c: (group(i, c), 0)),
+        "column": pl.BlockSpec((HID, COLS), lambda i, c: (0, group(i, c))),
+        "received": pl.BlockSpec((1, MAIN, WIDE), lambda i, c: (i, 0, 0)),
+        "slots": pl.BlockSpec((ROWS, COLS), lambda i, c: (0, group(i, c))),
+        "whole": pl.BlockSpec(memory_space=pl.ANY),
+        "hidden": _fixed(ROWS, HID),
+        "both": _fixed(ROWS, 2 * HID),
+    }
     return pl.pallas_call(
-        _forward_kernel,
+        kernel,
         grid_spec=pltpu.PrefetchScalarGridSpec(
             num_scalar_prefetch=1,
-            grid=(4,),
-            in_specs=[*_received(), weight, weight],
-            out_specs=[
-                pl.BlockSpec((ROWS, COLS), lambda i, c: (0, _group(i, c[0]))),
-                _fixed(ROWS, HID),
-                _fixed(ROWS, HID),
-                _fixed(ROWS, HID),
-            ],
+            grid=(2,),
+            in_specs=[block["received"]] + [block[k] for k in weights + state],
+            out_specs=[block[k] for k, _ in out],
+            scratch_shapes=scratch,
         ),
-        out_shape=[
-            pltpu.HBM((ROWS, D), BF),
-            _shape((ROWS, HID), F32),
-            _shape((ROWS, HID), F32),
-            _shape((ROWS, HID), BF),
+        out_shape=[t for _, t in out],
+        input_output_aliases=aliases,
+        compiler_params=_params(),
+        cost_estimate=_cost(flops, moved),
+        name=name,
+    )
+
+
+def _forward_own(core, own, w_gate, w_up):
+    return _half_pass(
+        _forward_own_kernel,
+        False,
+        ["row", "row"],
+        [],
+        [("slots", pltpu.HBM((ROWS, D), BF)), ("hidden", _shape((ROWS, HID), F32)), ("hidden", _shape((ROWS, HID), F32))],
+        [],
+        EARLY * 2 * ROWS * D * HID,
+        EARLY * 9e6,
+        "forward_own",
+    )(core, _hbm(own), _hbm(w_gate), _hbm(w_up))
+
+
+def _forward_other(core, other, w_gate, w_up, gate, up, x):
+    return _half_pass(
+        _forward_other_kernel,
+        True,
+        ["row", "row"],
+        ["hidden", "hidden", "whole"],
+        [
+            ("slots", pltpu.HBM((ROWS, D), BF)),
+            ("hidden", _shape((ROWS, HID), F32)),
+            ("hidden", _shape((ROWS, HID), F32)),
+            ("hidden", _shape((ROWS, HID), BF)),
         ],
-        compiler_params=_params(),
-        cost_estimate=_cost(4 * ROWS * D * HID, 17e6),
-        name="forward",
-    )(core, _hbm(own), _hbm(other), _hbm(w_gate), _hbm(w_up))
-
-
-def _backward(core, own, other, w_down, gate, up):
-    return pl.pallas_call(
-        _backward_kernel,
-        grid_spec=pltpu.PrefetchScalarGridSpec(
-            num_scalar_prefetch=1,
-            grid=(4,),
-            in_specs=[
-                *_received(),
-                pl.BlockSpec((HID, COLS), lambda i, c: (0, _group(i, c[0]))),
-                _fixed(ROWS, HID),
-                _fixed(ROWS, HID),
-            ],
-            out_specs=[
-                pl.BlockSpec((ROWS, COLS), lambda i, c: (0, _group(i, c[0]))),
-                _fixed(ROWS, 2 * HID),
-            ],
-            scratch_shapes=[pltpu.VMEM((ROWS, HID), F32)],
-        ),
-        out_shape=[pltpu.HBM((ROWS, D), BF), _shape((ROWS, 2 * HID), BF)],
-        compiler_params=_params(),
-        cost_estimate=_cost(2 * ROWS * D * HID, 14e6),
-        name="backward",
-    )(core, _hbm(own), _hbm(other), _hbm(w_down), gate, up)
+        [],
+        LATE * 2 * ROWS * D * HID,
+        LATE * 9e6,
+        "forward_other",
+        {6: 0},
+    )(core, _hbm(other), _hbm(w_gate), _hbm(w_up), gate, up, _hbm(x))
+
+
+def _backward_own(core, own, w_down):
+    return _half_pass(
+        _backward_own_kernel,
+        False,
+        ["column"],
+        [],
+        [("slots", pltpu.HBM((ROWS, D), BF)), ("hidden", _shape((ROWS, HID), F32))],
+        [],
+        EARLY * 2 * ROWS * D * HID,
+        EARLY * 9e6,
+        "backward_own",
+    )(core, _hbm(own), _hbm(w_down))
+
+
+def _backward_other(core, other, w_down, partial, gate, up, e):
+    return _half_pass(
+        _backward_other_kernel,
+        True,
+        ["column"],
+        ["hidden", "hidden", "hidden", "whole"],
+        [("slots", pltpu.HBM((ROWS, D), BF)), ("both", _shape((ROWS, 2 * HID), BF))],
+        [pltpu.VMEM((ROWS, HID), F32)],
+        LATE * ROWS * D * HID,
+        LATE * 6e6,
+        "backward_other",
+        {6: 0},
+    )(core, _hbm(other), _hbm(w_down), partial, gate, up, _hbm(e))
 
 
 def _result(core, hidden, hidden_p, w_down, w_down_p):
@@ -336,7 +373,7 @@
         ),
         out_shape=pltpu.HBM((2, MAIN, WIDE), BF),
         compiler_params=_params(),
-        cost_estimate=_cost(2 * ROWS * D * HID, 7e6),
+        cost_estimate=_cost(LATE * 2 * ROWS * D * HID, LATE * 7e6),
         name="result",
     )(core, hidden, hidden_p, _hbm(w_down), _hbm(w_down_p))
 
@@ -353,7 +390,7 @@
         ),
         out_shape=pltpu.HBM((2, MAIN, WIDE), BF),
         compiler_params=_params(),
-        cost_estimate=_cost(4 * ROWS * D * HID, 11e6),
+        cost_estimate=_cost(LATE * 4 * ROWS * D * HID, LATE * 11e6),
         name="back",
     )(core, grads, grads_p, _hbm(w_gate), _hbm(w_up), _hbm(w_gate_p), _hbm(w_up_p))
 
@@ -395,12 +432,14 @@
     recv_x, send_e = lax.optimization_barrier((recv_x, send_e))
     recv_e = _exchange(send_e)
 
-    x, gate, up, hidden = _forward(core, recv_x, _swap(recv_x), wg, wu)
+    x, gate, up = _forward_own(core, recv_x, wg, wu)
+    x, gate, up, hidden = _forward_other(core, _swap(recv_x), wg, wu, gate, up, x)
     send_o = _result(core, hidden, _swap(hidden), wd, wd_p)
     recv_e, send_o = lax.optimization_barrier((recv_e, send_o))
     recv_o = _exchange(send_o)
 
-    e, grads = _backward(core, recv_e, _swap(recv_e), wd, gate, up)
+    e, partial = _backward_own(core, recv_e, wd)
+    e, grads = _backward_other(core, _swap(recv_e), wd, partial, gate, up, e)
     send_b = _back(core, grads, _swap(grads), wg, wu, wg_p, wu_p)
     recv_b = _exchange(send_b)
 
@@ -414,10 +453,10 @@
         4e8,
         3e6,
         "mixed",
-        ids_t,
-        pick,
-        weight,
-        cotangent,
+        _hbm(ids_t),
+        _hbm(pick),
+        _hbm(weight),
+        _hbm(cotangent),
         _hbm(recv_o),
     )
     inner = inner + _swap(inner)

time: 147 us -> 144 us (0.980)
  waiting for transfers between devices: 50.2 us -> 41.8 us
  local copies, waits for them, and re-layouts: 1.67 us -> 3.89 us
    all_to_all x4, waiting for transfers between devices: 45.5 us -> 37.8 us  [_exchange(): lax.all_to_all(chunks, ('yhi', 'expert'), split_axis=0, concat_axis=0, ti...]
    unnamed x14 -> x16, local copies, waits for them, and re-layouts: 1.67 us -> 3.89 us
    pallas_call x2 -> x4, Pallas kernels: 18.5 us -> 20.1 us  [the longest x1 5.69 us: _forward_other(): _half_pass(_forward_other_kernel, True, ['row', 'row'], ['hidden', 'hidde...]
  transfers between devices with their start and end apart: 13 -> 13, of which waited for: 7 -> 7; matrix products, arithmetic and copies ran while one was open for 10% -> 11% of each run, Pallas kernels for 27% -> 29%
where the time goes in v3:
time: 144 us; the launch traced here: 143 us
  Pallas kernels  45.7 us (32%)
  waiting for transfers between devices  41.8 us (29%)
  starting transfers between devices  36 us (25%)
  matrix products  15.1 us (10%)
  local copies, waits for them, and re-layouts  3.89 us (3%)
    all_to_all x4, waiting for transfers between devices, _exchange(): lax.all_to_all(chunks, ('yhi', 'expert'), split_axis=0, concat_axis=0, ti...  37.8 us
    all_to_all x4, starting transfers between devices, _exchange(): lax.all_to_all(chunks, ('yhi', 'expert'), split_axis=0, concat_axis=0, ti...  30.9 us
    dot_general x3, matrix products, _dot_tn(): lax.dot_general(a, b, (((0,), (0,)), ((), ())), preferred_element_type=F32)  15.1 us
    pallas_call x4, Pallas kernels, _local(): pl.pallas_call(kernel, out_shape=out_shape, compiler_params=_params(), co...  11 us
    pallas_call x1, Pallas kernels, _back(): pl.pallas_call(_back_kernel, grid_spec=pltpu.PrefetchScalarGridSpec(num_s...  8.66 us
    pallas_call x1, Pallas kernels, _result(): pl.pallas_call(_result_kernel, grid_spec=pltpu.PrefetchScalarGridSpec(num...  5.93 us
    pallas_call x1, Pallas kernels, _forward_other(): _half_pass(_forward_other_kernel, True, ['row', 'row'], ['hidden', 'hidde...  5.69 us
    pallas_call x1, Pallas kernels, _forward_own(): _half_pass(_forward_own_kernel, False, ['row', 'row'], [], [('slots', plt...  5.61 us
  transfers between devices with their start and end apart: 13, of which 7 were waited for; matrix products, arithmetic and copies ran while one was open for 11% of the time, Pallas kernels for 29%

profile of v3, /device:TPU:0, one launch (start us, length us, event | category | flops | bytes accessed | tf_op | source)
XLA Modules:
  0.0 143.2 jit_solution(9380910516811877663)
XLA Ops:
  0.6 3.0 %pack_rows.1 = bf16[2,256,1920]{2,1,0:T(8,128)(2,1)} custom-call(s32[6,128]{1,0:T(8,128)} %bitcast.42, f32[6,128]{1,0:T(8,128)} %bitcast.45, bf16[128,1280]{1,0:T(8,128)(2,1)} %tok_ref.1), custom_call_target="tpu_custom_call" | custom-call | flops 200000000 | bytes 3000000 | tf_op jit(solution)/shard_map/pack_rows/pallas_call | solution.py:399
  3.6 11.5 %all-to-all-start = ((bf16[64,8,1920]{2,1,0:T(8,128)(2,1)}), bf16[64,8,1920]{2,1,0:T(8,128)(2,1)S(1)}, u32[]{:S(2)}, u32[]{:S(2)}) async-start(bf16[64,8,1920]{2,1,0:T(8,128)(2,1)} %bitcast.36), calls=%async_computation | async-start | bytes 3932160 | tf_op jit(solution)/shard_map/all_to_all | solution.py:406
  15.2 0.1 collective-permute-start.2
  15.3 0.5 collective-permute-start.5
  15.7 0.1 collective-permute-start.6
  15.8 3.1 %pack_grads.1 = (bf16[2,256,1920]{2,1,0:T(8,128)(2,1)}, bf16[512,128]{1,0:T(8,128)(2,1)S(1)}, f32[512,128]{1,0:T(8,128)S(1)}) custom-call(s32[6,128]{1,0:T(8,128)} %bitcast.43, f32[6,128]{1,0:T(8,128)} %bitcast.46, bf16[128,1280]{1,0:T(8,128)(2,1)} %cot_ref.3), custom_call_target="tpu_custom_call" | custom-call | flops 200000000 | bytes 3000000 | tf_op jit(solution)/shard_map/pack_grads/pallas_call | solution.py:399
  18.9 0.0 copy-start
  18.9 0.6 copy-done
  19.5 0.0 copy-start.2
  19.5 0.7 copy-done.2
  20.2 22.7 %all-to-all-done = bf16[64,8,1920]{2,1,0:T(8,128)(2,1)S(1)} async-done(((bf16[64,8,1920]{2,1,0:T(8,128)(2,1)}), bf16[64,8,1920]{2,1,0:T(8,128)(2,1)S(1)}, u32[]{:S(2)}, u32[]{:S(2)}) %all-to-all-start) | async-done | bytes 1966112 | tf_op jit(solution)/shard_map/all_to_all | solution.py:406
  43.0 0.0 copy-start.5
  43.0 6.3 %all-to-all-start.1 = ((bf16[64,8,1920]{2,1,0:T(8,128)(2,1)}), bf16[64,8,1920]{2,1,0:T(8,128)(2,1)}, u32[]{:S(2)}, u32[]{:S(2)}) async-start(bf16[64,8,1920]{2,1,0:T(8,128)(2,1)} %bitcast.39), calls=%async_computation.1 | async-start | bytes 3932160 | tf_op jit(solution)/shard_map/all_to_all | solution.py:406
  49.2 0.1 collective-permute-start
  49.3 0.0 copy-done.5
  49.3 5.6 %forward_own.1 = (bf16[384,5120]{1,0:T(8,128)(2,1)}, f32[384,384]{1,0:T(8,128)S(1)}, f32[384,384]{1,0:T(8,128)S(1)}) custom-call(s32[1]{0:T(128)} %bitcast.6.core_ref, bf16[2,256,1920]{2,1,0:T(8,128)(2,1)} %bitcast.41, bf16[5120,384]{1,0:T(8,128)(2,1)} %bitcast.24, bf16[5120,384]{1,0:T(8,128)(2,1)} %bitcast.28), custom_call_target="tpu_custom_call" | custom-call | flops 24159191040 | bytes 144000000 | tf_op jit(solution)/shard_map/forward_own/pallas_call | solution.py:302
  54.9 0.0 collective-permute-done.r_ref
  54.9 0.0 copy-start.6
  54.9 1.3 copy-done.6
  56.2 5.7 %forward_other.1 = (bf16[384,5120]{1,0:T(8,128)(2,1)}, f32[384,384]{1,0:T(8,128)S(1)}, f32[384,384]{1,0:T(8,128)S(1)}, bf16[384,384]{1,0:T(8,128)(2,1)S(1)}) custom-call(s32[1]{0:T(128)} %bitcast.6.core_ref, bf16[2,256,1920]{2,1,0:T(8,128)(2,1)} %copy-done.6, bf16[5120,384]{1,0:T(8,128)(2,1)} %bitcast.25, ...), custom_call_target="tpu_custom_call", output_to_operand_aliasing={{0}: (6, {})} | custom-call | flops 11796480 | bytes 70312 | tf_op jit(solution)/shard_map/forward_other/pallas_call | solution.py:316
  61.9 0.5 collective-permute-start.1
  62.4 0.0 collective-permute-done.2.wdp_ref
  62.4 1.2 collective-permute-done.1.hp_ref
  63.6 5.9 %result.1 = bf16[2,256,1920]{2,1,0:T(8,128)(2,1)} custom-call(s32[1]{0:T(128)} %bitcast.6.core_ref, bf16[384,384]{1,0:T(8,128)(2,1)S(1)} %get-tuple-element.40.h_ref, bf16[384,384]{1,0:T(8,128)(2,1)S(1)} %collective-permute-done.1.hp_ref, bf16[384,5120]{1,0:T(8,128)(2,1)} %bitcast.32, bf16[384,5120]{1,0:T(8,128)(2,1)} %collective-permute-done.2.wdp_ref), custom_call_target="tpu_custom_call" | custom-call | flops 11796480 | bytes 54687 | tf_op jit(solution)/shard_map/result/pallas_call | solution.py:366
  69.5 5.9 %all-to-all-done.1 = bf16[64,8,1920]{2,1,0:T(8,128)(2,1)} async-done(((bf16[64,8,1920]{2,1,0:T(8,128)(2,1)}), bf16[64,8,1920]{2,1,0:T(8,128)(2,1)}, u32[]{:S(2)}, u32[]{:S(2)}) %all-to-all-start.1) | async-done | bytes 1966112 | tf_op jit(solution)/shard_map/all_to_all | solution.py:406
  75.4 6.8 %all-to-all-start.2 = ((bf16[64,8,1920]{2,1,0:T(8,128)(2,1)}), bf16[64,8,1920]{2,1,0:T(8,128)(2,1)}, u32[]{:S(2)}, u32[]{:S(2)}) async-start(bf16[64,8,1920]{2,1,0:T(8,128)(2,1)} %bitcast.35), calls=%async_computation.2 | async-start | bytes 3932160 | tf_op jit(solution)/shard_map/all_to_all | solution.py:406
  82.2 0.1 collective-permute-start.3
  82.3 4.3 %backward_own.1 = (bf16[384,5120]{1,0:T(8,128)(2,1)}, f32[384,384]{1,0:T(8,128)S(1)}) custom-call(s32[1]{0:T(128)} %bitcast.6.core_ref, bf16[2,256,1920]{2,1,0:T(8,128)(2,1)} %bitcast.5.r_ref, bf16[384,5120]{1,0:T(8,128)(2,1)} %bitcast.33), custom_call_target="tpu_custom_call" | custom-call | flops 24159191040 | bytes 144000000 | tf_op jit(solution)/shard_map/backward_own/pallas_call | solution.py:336
  86.6 0.0 collective-permute-done.3.r_ref
  86.6 0.0 copy-start.7
  86.6 1.3 copy-done.7
  87.8 4.5 %backward_other.1 = (bf16[384,5120]{1,0:T(8,128)(2,1)}, bf16[384,768]{1,0:T(8,128)(2,1)S(1)}) custom-call(s32[1]{0:T(128)} %bitcast.6.core_ref, bf16[2,256,1920]{2,1,0:T(8,128)(2,1)} %copy-done.7, bf16[384,5120]{1,0:T(8,128)(2,1)} %bitcast.34, f32[384,384]{1,0:T(8,128)S(1)} %get-tuple-element.44.a0_ref, ...), custom_call_target="tpu_custom_call", output_to_operand_aliasing={{0}: (6, {})} | custom-call | flops 5898240 | bytes 46875 | tf_op jit(solution)/shard_map/backward_other/pallas_call | solution.py:350
  92.3 0.5 collective-permute-start.4
  92.8 0.0 collective-permute-done.5.wgp_ref
  92.8 0.0 collective-permute-done.6.wup_ref
  92.8 1.6 %collective-permute-done.4.dp_ref = bf16[384,768]{1,0:T(8,128)(2,1)S(1)} collective-permute-done((bf16[384,768]{1,0:T(8,128)(2,1)S(1)}, bf16[384,768]{1,0:T(8,128)(2,1)S(1)}, u32[]{:S(2)}, u32[]{:S(2)}) %collective-permute-start.4) | collective-permute-done | bytes 589856 | tf_op jit(solution)/shard_map/ppermute | solution.py:411
  94.4 8.7 %back.1 = bf16[2,256,1920]{2,1,0:T(8,128)(2,1)} custom-call(s32[1]{0:T(128)} %bitcast.6.core_ref, bf16[384,768]{1,0:T(8,128)(2,1)S(1)} %get-tuple-element.48.d_ref, bf16[384,768]{1,0:T(8,128)(2,1)S(1)} %collective-permute-done.4.dp_ref, bf16[5120,384]{1,0:T(8,128)(2,1)} %bitcast.26, bf16[5120,384]{1,0:T(8,128)(2,1)} %bitcast.30, ...), custom_call_target="tpu_custom_call" | custom-call | flops 23592960 | bytes 85937 | tf_op jit(solution)/shard_map/back/pallas_call | solution.py:383
  103.1 4.9 %all-to-all-done.2 = bf16[64,8,1920]{2,1,0:T(8,128)(2,1)} async-done(((bf16[64,8,1920]{2,1,0:T(8,128)(2,1)}), bf16[64,8,1920]{2,1,0:T(8,128)(2,1)}, u32[]{:S(2)}, u32[]{:S(2)}) %all-to-all-start.2) | async-done | bytes 1966112 | tf_op jit(solution)/shard_map/all_to_all | solution.py:406
  108.0 6.4 %all-to-all-start.3 = ((bf16[64,8,1920]{2,1,0:T(8,128)(2,1)}), bf16[64,8,1920]{2,1,0:T(8,128)(2,1)S(1)}, u32[]{:S(2)}, u32[]{:S(2)}) async-start(bf16[64,8,1920]{2,1,0:T(8,128)(2,1)} %bitcast.37), calls=%async_computation.3 | async-start | bytes 3932160 | tf_op jit(solution)/shard_map/all_to_all | solution.py:406
  114.5 3.6 %mixed.1 = (bf16[128,1280]{1,0:T(8,128)(2,1)}, f32[6,128]{1,0:T(8,128)S(1)}) custom-call(s32[6,128]{1,0:T(8,128)} %bitcast.44, bf16[512,128]{1,0:T(8,128)(2,1)} %copy-done, f32[512,128]{1,0:T(8,128)} %copy-done.2, bf16[128,1280]{1,0:T(8,128)(2,1)} %cot_ref.3, bf16[2,256,1920]{2,1,0:T(8,128)(2,1)} %bitcast.11.r_ref), custom_call_target="tpu_custom_call" | custom-call | flops 400000000 | bytes 3000000 | tf_op jit(solution)/shard_map/mixed/pallas_call | solution.py:399
  118.1 0.1 collective-permute-start.7
  118.2 1.2 collective-permute-done.7
  119.3 3.2 %collective-permute-start.8 = (f32[6,128]{1,0:T(8,128)S(1)}, f32[6,128]{1,0:T(8,128)S(1)}, u32[]{:S(2)}, u32[]{:S(2)}) collective-permute-start(f32[6,128]{1,0:T(8,128)S(1)} %add.3.inner_ref), channel_id=1, source_target_pairs={{0,2},{2,0},{1,3},{3,1},{4,6},{6,4},{5,7},{7,5},{8,10},{10,8},{9,1... | collective-permute-start | bytes 9224 | tf_op jit(solution)/shard_map/ppermute | solution.py:411
  122.5 0.0 copy-start.4
  122.5 6.8 %convolution_convert_fusion.2 = bf16[5120,384]{1,0:T(8,128)(2,1)} fusion(bf16[384,5120]{1,0:T(8,128)(2,1)} %get-tuple-element.49, bf16[384,768]{1,0:T(8,128)(2,1)S(1)} %get-tuple-element.48.d_ref), kind=kOutput, calls=%fused_computation.2 | convolution fusion | flops 1511915520 | bytes 8159232 | tf_op jit(solution)/shard_map/dot_general | solution.py:38
  129.3 0.0 copy-done.4
  129.3 0.0 copy-start.3
  129.3 4.1 %convolution_convert_fusion.1 = bf16[5120,384]{1,0:T(8,128)(2,1)} fusion(bf16[384,5120]{1,0:T(8,128)(2,1)S(1)} %copy-done.4, bf16[384,768]{1,0:T(8,128)(2,1)S(1)} %get-tuple-element.48.d_ref), kind=kOutput, calls=%fused_computation.1 | convolution fusion | flops 1511915520 | bytes 8159232 | tf_op jit(solution)/shard_map/dot_general | solution.py:38
  133.4 0.0 copy-done.3
  133.4 0.0 copy-start.1
  133.4 4.2 %convolution_convert_fusion = bf16[384,5120]{1,0:T(8,128)(2,1)} fusion(bf16[384,384]{1,0:T(8,128)(2,1)S(1)} %get-tuple-element.40.h_ref, bf16[384,5120]{1,0:T(8,128)(2,1)S(1)} %copy-done.3), kind=kOutput, calls=%fused_computation | convolution fusion | flops 1511915520 | bytes 8159232 | tf_op jit(solution)/shard_map/dot_general | solution.py:38
  137.6 4.3 %all-to-all-done.3 = bf16[64,8,1920]{2,1,0:T(8,128)(2,1)S(1)} async-done(((bf16[64,8,1920]{2,1,0:T(8,128)(2,1)}), bf16[64,8,1920]{2,1,0:T(8,128)(2,1)S(1)}, u32[]{:S(2)}, u32[]{:S(2)}) %all-to-all-start.3) | async-done | bytes 1966112 | tf_op jit(solution)/shard_map/all_to_all | solution.py:406
  141.8 0.0 collective-permute-done.8.far_ref
  141.8 0.0 copy-done.1
  141.8 1.4 grad_tokens.1
  (1 shorter events, 0.0 us)
Async XLA Ops:
  3.6 39.3 %all-to-all-start = ((bf16[64,8,1920]{2,1,0:T(8,128)(2,1)}), bf16[64,8,1920]{2,1,0:T(8,128)(2,1)S(1)}, u32[]{:S(2)}, u32[]{:S(2)}) async-start(bf16[64,8,1920]{2,1,0:T(8,128)(2,1)} %bitcast.36), calls=%async_computation | async-start | bytes 3932160 | tf_op jit(solution)/shard_map/all_to_all | solution.py:406
  15.2 47.2 %collective-permute-start.2 = (bf16[384,5120]{1,0:T(8,128)(2,1)}, bf16[384,5120]{1,0:T(8,128)(2,1)}, u32[]{:S(2)}, u32[]{:S(2)}) collective-permute-start(bf16[384,5120]{1,0:T(8,128)(2,1)} %bitcast.31), channel_id=1, source_target_pairs={{0,1},{1,0},{2,3},{3,2},{4,5},{5,4},{6,7},{7,6},{8,9},{9,8},{10,11... | collective-permute-start | bytes 11796488 | tf_op jit(solution)/shard_map/ppermute | solution.py:411
  15.3 77.6 %collective-permute-start.5 = (bf16[5120,384]{1,0:T(8,128)(2,1)}, bf16[5120,384]{1,0:T(8,128)(2,1)}, u32[]{:S(2)}, u32[]{:S(2)}) collective-permute-start(bf16[5120,384]{1,0:T(8,128)(2,1)} %bitcast.23), channel_id=1, source_target_pairs={{0,1},{1,0},{2,3},{3,2},{4,5},{5,4},{6,7},{7,6},{8,9},{9,8},{10,11... | collective-permute-start | bytes 11796488 | tf_op jit(solution)/shard_map/ppermute | solution.py:411
  15.7 77.1 %collective-permute-start.6 = (bf16[5120,384]{1,0:T(8,128)(2,1)}, bf16[5120,384]{1,0:T(8,128)(2,1)}, u32[]{:S(2)}, u32[]{:S(2)}) collective-permute-start(bf16[5120,384]{1,0:T(8,128)(2,1)} %bitcast.27), channel_id=1, source_target_pairs={{0,1},{1,0},{2,3},{3,2},{4,5},{5,4},{6,7},{7,6},{8,9},{9,8},{10,11... | collective-permute-start | bytes 11796488 | tf_op jit(solution)/shard_map/ppermute | solution.py:411
  18.9 0.6 copy-start
  19.5 0.7 copy-start.2
  43.0 6.4 %copy-start.5 = (bf16[64,8,1920]{2,1,0:T(8,128)(2,1)}, bf16[64,8,1920]{2,1,0:T(8,128)(2,1)S(1)}, u32[]{:S(2)}) copy-start(bf16[64,8,1920]{2,1,0:T(8,128)(2,1)S(1)} %all-to-all-done) | copy-start | bytes 5898244
  43.0 32.5 %all-to-all-start.1 = ((bf16[64,8,1920]{2,1,0:T(8,128)(2,1)}), bf16[64,8,1920]{2,1,0:T(8,128)(2,1)}, u32[]{:S(2)}, u32[]{:S(2)}) async-start(bf16[64,8,1920]{2,1,0:T(8,128)(2,1)} %bitcast.39), calls=%async_computation.1 | async-start | bytes 3932160 | tf_op jit(solution)/shard_map/all_to_all | solution.py:406
  49.2 5.7 %collective-permute-start = (bf16[2,256,1920]{2,1,0:T(8,128)(2,1)S(1)}, bf16[2,256,1920]{2,1,0:T(8,128)(2,1)S(1)}, u32[]{:S(2)}, u32[]{:S(2)}) collective-permute-start(bf16[2,256,1920]{2,1,0:T(8,128)(2,1)S(1)} %bitcast.40), channel_id=1, source_target_pairs={{0,1},{1,0},{2,3},{3,2},{4,5},{5,4},{6,7},{7,6},{8,9},{9,8},{10,11... | collective-permute-start | bytes 5898248 | tf_op jit(solution)/shard_map/ppermute | solution.py:411
  54.9 1.3 copy-start.6
  61.9 1.7 %collective-permute-start.1 = (bf16[384,384]{1,0:T(8,128)(2,1)S(1)}, bf16[384,384]{1,0:T(8,128)(2,1)S(1)}, u32[]{:S(2)}, u32[]{:S(2)}) collective-permute-start(bf16[384,384]{1,0:T(8,128)(2,1)S(1)} %get-tuple-element.40.h_ref), channel_id=1, source_target_pairs={{0,1},{1,0},{2,3},{3,2},{4,5},{5,4},{6,7},{7,6},{8,9},{9,8},{10,11... | collective-permute-start | bytes 884744 | tf_op jit(solution)/shard_map/ppermute | solution.py:411
  75.4 32.6 %all-to-all-start.2 = ((bf16[64,8,1920]{2,1,0:T(8,128)(2,1)}), bf16[64,8,1920]{2,1,0:T(8,128)(2,1)}, u32[]{:S(2)}, u32[]{:S(2)}) async-start(bf16[64,8,1920]{2,1,0:T(8,128)(2,1)} %bitcast.35), calls=%async_computation.2 | async-start | bytes 3932160 | tf_op jit(solution)/shard_map/all_to_all | solution.py:406
  82.2 4.4 %collective-permute-start.3 = (bf16[2,256,1920]{2,1,0:T(8,128)(2,1)}, bf16[2,256,1920]{2,1,0:T(8,128)(2,1)S(1)}, u32[]{:S(2)}, u32[]{:S(2)}) collective-permute-start(bf16[2,256,1920]{2,1,0:T(8,128)(2,1)} %bitcast.5.r_ref), channel_id=1, source_target_pairs={{0,1},{1,0},{2,3},{3,2},{4,5},{5,4},{6,7},{7,6},{8,9},{9,8},{10,11... | collective-permute-start | bytes 5898248 | tf_op jit(solution)/shard_map/ppermute | solution.py:411
  86.6 1.3 copy-start.7
  92.3 2.1 %collective-permute-start.4 = (bf16[384,768]{1,0:T(8,128)(2,1)S(1)}, bf16[384,768]{1,0:T(8,128)(2,1)S(1)}, u32[]{:S(2)}, u32[]{:S(2)}) collective-permute-start(bf16[384,768]{1,0:T(8,128)(2,1)S(1)} %get-tuple-element.48.d_ref), channel_id=1, source_target_pairs={{0,1},{1,0},{2,3},{3,2},{4,5},{5,4},{6,7},{7,6},{8,9},{9,8},{10,11... | collective-permute-start | bytes 1769480 | tf_op jit(solution)/shard_map/ppermute | solution.py:411
  108.0 33.8 %all-to-all-start.3 = ((bf16[64,8,1920]{2,1,0:T(8,128)(2,1)}), bf16[64,8,1920]{2,1,0:T(8,128)(2,1)S(1)}, u32[]{:S(2)}, u32[]{:S(2)}) async-start(bf16[64,8,1920]{2,1,0:T(8,128)(2,1)} %bitcast.37), calls=%async_computation.3 | async-start | bytes 3932160 | tf_op jit(solution)/shard_map/all_to_all | solution.py:406
  118.1 1.2 collective-permute-start.7
  119.3 22.5 %collective-permute-start.8 = (f32[6,128]{1,0:T(8,128)S(1)}, f32[6,128]{1,0:T(8,128)S(1)}, u32[]{:S(2)}, u32[]{:S(2)}) collective-permute-start(f32[6,128]{1,0:T(8,128)S(1)} %add.3.inner_ref), channel_id=1, source_target_pairs={{0,2},{2,0},{1,3},{3,1},{4,6},{6,4},{5,7},{7,5},{8,10},{10,8},{9,1... | collective-permute-start | bytes 9224 | tf_op jit(solution)/shard_map/ppermute | solution.py:411
  122.5 6.8 %copy-start.4 = (bf16[384,5120]{1,0:T(8,128)(2,1)S(1)}, bf16[384,5120]{1,0:T(8,128)(2,1)}, u32[]{:S(2)}) copy-start(bf16[384,5120]{1,0:T(8,128)(2,1)} %get-tuple-element.49) | copy-start | bytes 11796484
  129.3 4.1 %copy-start.3 = (bf16[384,5120]{1,0:T(8,128)(2,1)S(1)}, bf16[384,5120]{1,0:T(8,128)(2,1)}, u32[]{:S(2)}) copy-start(bf16[384,5120]{1,0:T(8,128)(2,1)} %get-tuple-element.50) | copy-start | bytes 11796484
  133.4 8.4 %copy-start.1 = (bf16[512,128]{1,0:T(8,128)(2,1)S(1)}, bf16[512,128]{1,0:T(8,128)(2,1)}, u32[]{:S(2)}) copy-start(bf16[512,128]{1,0:T(8,128)(2,1)} %copy-done) | copy-start | bytes 393220

commit v4 on v3

--- a/solution.py
+++ b/solution.py
@@ -19,6 +19,7 @@
 ROWS = 384
 MAIN = 256
 REST = 128
+STEPS = 4
 WIDE = COLS + HALF
 D = 4 * COLS
 VMEM = 40 * 1024 * 1024
@@ -42,14 +43,15 @@
     return lax.broadcasted_iota(jnp.int32, shape, dim)
 
 
-def _routing(ids_t, probs_t):
+def _routing(ids_t, probs_t=None):
     expert = _iota((EXPERTS, BLOCK), 0)
     chosen = jnp.zeros((EXPERTS, BLOCK), F32)
     weight = jnp.zeros((EXPERTS, BLOCK), F32)
     for k in range(TOPK):
         hit = ids_t[k : k + 1, :] == expert
         chosen = jnp.where(hit, 1.0, chosen)
-        weight = jnp.where(hit, probs_t[k : k + 1, :], weight)
+        if probs_t is not None:
+            weight = jnp.where(hit, probs_t[k : k + 1, :], weight)
     earlier = (_iota((BLOCK, BLOCK), 0) < _iota((BLOCK, BLOCK), 1)).astype(F32).astype(BF)
     before = _dot(chosen.astype(BF), earlier)
     code = jnp.where(chosen > 0.5, before, -1.0)
@@ -59,6 +61,8 @@
     j = _iota((MAIN, BLOCK), 0)
     main = jnp.where(place == (j % 8).astype(F32), 1.0, 0.0)
     rest = jnp.where(place == (8 + j % 4).astype(F32), 1.0, 0.0)
+    if probs_t is None:
+        return main, rest, None
     hi = weight.astype(BF)
     left = weight - hi.astype(F32)
     mid = left.astype(BF)
@@ -80,8 +84,8 @@
     return a, b
 
 
-def _pack_rows_kernel(ids_ref, probs_ref, tok_ref, out_ref):
-    main, rest, _ = _routing(ids_ref[...], probs_ref[...])
+def _pack_rows_kernel(ids_ref, tok_ref, out_ref):
+    main, rest, _ = _routing(ids_ref[...])
     a, b = _send(main, rest, tok_ref[...])
     a, b = a.astype(BF), b.astype(BF)
     for y in range(2):
@@ -114,21 +118,28 @@
     return (_iota((MAIN, REST), 0) == (q // 4) * 8 + 4 * h + q % 4).astype(F32).astype(BF)
 
 
-def _unpack(r_ref, x_ref):
-    rest = r_ref[0, :, COLS:]
-    x_ref[:MAIN, :] = r_ref[0, :, :COLS]
-    x_ref[MAIN:, :HALF] = _dot(_fold(0), rest).astype(BF)
-    x_ref[MAIN:, HALF:] = _dot(_fold(1), rest).astype(BF)
+def _unpack(main_ref, rest_ref, x_ref):
+    x_ref[:MAIN, :] = main_ref[0]
+    x_ref[MAIN:, :] = _dot(_fold(pl.program_id(0) % 2), rest_ref[0]).astype(BF)
 
 
 def _pack(value, out_ref):
-    rest = value[MAIN:, :]
-    out_ref[0, :, :COLS] = value[:MAIN, :]
-    out_ref[0, :, COLS:] = (_dot(_fold_t(0), rest[:, :HALF]) + _dot(_fold_t(1), rest[:, HALF:])).astype(BF)
-
-
-def _forward_own_kernel(core_ref, r_ref, wg_ref, wu_ref, x_ref, g_ref, u_ref):
-    _unpack(r_ref, x_ref)
+    h = pl.program_id(0) % 2
+    rest = _dot(_fold_t(h), value[MAIN:, :]).astype(BF)
+
+    @pl.when(h == 0)
+    def _():
+        out_ref[0, :, :HALF] = value[:MAIN, :]
+        out_ref[0, :, COLS:] = rest
+
+    @pl.when(h == 1)
+    def _():
+        out_ref[0, :, HALF:COLS] = value[:MAIN, :]
+        out_ref[0, :, COLS:] += rest
+
+
+def _forward_own_kernel(core_ref, main_ref, rest_ref, wg_ref, wu_ref, x_ref, g_ref, u_ref):
+    _unpack(main_ref, rest_ref, x_ref)
     g = _dot(x_ref[...], wg_ref[...])
     u = _dot(x_ref[...], wu_ref[...])
 
@@ -143,8 +154,8 @@
         u_ref[...] += u
 
 
-def _forward_other_kernel(core_ref, r_ref, wg_ref, wu_ref, g0_ref, u0_ref, x0_ref, x_ref, g_ref, u_ref, h_ref):
-    _unpack(r_ref, x_ref)
+def _forward_other_kernel(core_ref, main_ref, rest_ref, wg_ref, wu_ref, g0_ref, u0_ref, x0_ref, x_ref, g_ref, u_ref, h_ref):
+    _unpack(main_ref, rest_ref, x_ref)
     g = _dot(x_ref[...], wg_ref[...])
     u = _dot(x_ref[...], wu_ref[...])
 
@@ -155,15 +166,17 @@
 
     @pl.when(pl.program_id(0) > 0)
     def _():
-        gate = g_ref[...] + g
-        up = u_ref[...] + u
-        g_ref[...] = gate
-        u_ref[...] = up
+        g_ref[...] += g
+        u_ref[...] += u
+
+    @pl.when(pl.program_id(0) == STEPS - 1)
+    def _():
+        gate, up = g_ref[...], u_ref[...]
         h_ref[...] = (gate * jax.nn.sigmoid(gate) * up).astype(BF)
 
 
-def _backward_own_kernel(core_ref, r_ref, wd_ref, e_ref, a_ref):
-    _unpack(r_ref, e_ref)
+def _backward_own_kernel(core_ref, main_ref, rest_ref, wd_ref, e_ref, a_ref):
+    _unpack(main_ref, rest_ref, e_ref)
     a = _dot_nt(e_ref[...], wd_ref[...])
 
     @pl.when(pl.program_id(0) == 0)
@@ -175,8 +188,8 @@
         a_ref[...] += a
 
 
-def _backward_other_kernel(core_ref, r_ref, wd_ref, a0_ref, g_ref, u_ref, e0_ref, e_ref, d_ref, a_ref):
-    _unpack(r_ref, e_ref)
+def _backward_other_kernel(core_ref, main_ref, rest_ref, wd_ref, a0_ref, g_ref, u_ref, e0_ref, e_ref, d_ref, a_ref):
+    _unpack(main_ref, rest_ref, e_ref)
     a = _dot_nt(e_ref[...], wd_ref[...])
 
     @pl.when(pl.program_id(0) == 0)
@@ -185,7 +198,11 @@
 
     @pl.when(pl.program_id(0) > 0)
     def _():
-        total, gate = a_ref[...] + a, g_ref[...]
+        a_ref[...] += a
+
+    @pl.when(pl.program_id(0) == STEPS - 1)
+    def _():
+        total, gate = a_ref[...], g_ref[...]
         s = jax.nn.sigmoid(gate)
         d_ref[:, :HID] = (total * u_ref[...] * s * (1.0 + gate * (1.0 - s))).astype(BF)
         d_ref[:, HID:] = (total * (gate * s)).astype(BF)
@@ -268,15 +285,20 @@
     return pl.BlockSpec(shape, lambda i, c: (0,) * len(shape))
 
 
+def _piece(i, core):
+    return (2 * (i // 2) + core) * 2 + i % 2
+
+
 def _half_pass(kernel, other, weights, state, out, scratch, flops, moved, name, aliases={}):
-    def group(i, c):
-        return 2 * i + (1 - c[0] if other else c[0])
+    def piece(i, c):
+        return _piece(i, 1 - c[0] if other else c[0])
 
     block = {
-        "row": pl.BlockSpec((COLS, HID), lambda i, c: (group(i, c), 0)),
-        "column": pl.BlockSpec((HID, COLS), lambda i, c: (0, group(i, c))),
-        "received": pl.BlockSpec((1, MAIN, WIDE), lambda i, c: (i, 0, 0)),
-        "slots": pl.BlockSpec((ROWS, COLS), lambda i, c: (0, group(i, c))),
+        "row": pl.BlockSpec((HALF, HID), lambda i, c: (piece(i, c), 0)),
+        "column": pl.BlockSpec((HID, HALF), lambda i, c: (0, piece(i, c))),
+        "main": pl.BlockSpec((1, MAIN, HALF), lambda i, c: (i // 2, 0, i % 2)),
+        "rest": pl.BlockSpec((1, MAIN, HALF), lambda i, c: (i // 2, 0, 2)),
+        "slots": pl.BlockSpec((ROWS, HALF), lambda i, c: (0, piece(i, c))),
         "whole": pl.BlockSpec(memory_space=pl.ANY),
         "hidden": _fixed(ROWS, HID),
         "both": _fixed(ROWS, 2 * HID),
@@ -285,8 +307,8 @@
         kernel,
         grid_spec=pltpu.PrefetchScalarGridSpec(
             num_scalar_prefetch=1,
-            grid=(2,),
-            in_specs=[block["received"]] + [block[k] for k in weights + state],
+            grid=(STEPS,),
+            in_specs=[block[k] for k in ("main", "rest")] + [block[k] for k in weights + state],
             out_specs=[block[k] for k, _ in out],
             scratch_shapes=scratch,
         ),
@@ -309,7 +331,7 @@
         EARLY * 2 * ROWS * D * HID,
         EARLY * 9e6,
         "forward_own",
-    )(core, _hbm(own), _hbm(w_gate), _hbm(w_up))
+    )(core, _hbm(own), _hbm(own), _hbm(w_gate), _hbm(w_up))
 
 
 def _forward_other(core, other, w_gate, w_up, gate, up, x):
@@ -328,8 +350,8 @@
         LATE * 2 * ROWS * D * HID,
         LATE * 9e6,
         "forward_other",
-        {6: 0},
-    )(core, _hbm(other), _hbm(w_gate), _hbm(w_up), gate, up, _hbm(x))
+        {7: 0},
+    )(core, other, other, _hbm(w_gate), _hbm(w_up), gate, up, _hbm(x))
 
 
 def _backward_own(core, own, w_down):
@@ -343,7 +365,7 @@
         EARLY * 2 * ROWS * D * HID,
         EARLY * 9e6,
         "backward_own",
-    )(core, _hbm(own), _hbm(w_down))
+    )(core, _hbm(own), _hbm(own), _hbm(w_down))
 
 
 def _backward_other(core, other, w_down, partial, gate, up, e):
@@ -357,19 +379,19 @@
         LATE * ROWS * D * HID,
         LATE * 6e6,
         "backward_other",
-        {6: 0},
-    )(core, _hbm(other), _hbm(w_down), partial, gate, up, _hbm(e))
+        {7: 0},
+    )(core, other, other, _hbm(w_down), partial, gate, up, _hbm(e))
 
 
 def _result(core, hidden, hidden_p, w_down, w_down_p):
-    weight = pl.BlockSpec((HID, COLS), lambda i, c: (0, 2 * i + c[0]))
+    weight = pl.BlockSpec((HID, HALF), lambda i, c: (0, _piece(i, c[0])))
     return pl.pallas_call(
         _result_kernel,
         grid_spec=pltpu.PrefetchScalarGridSpec(
             num_scalar_prefetch=1,
-            grid=(2,),
+            grid=(STEPS,),
             in_specs=[_fixed(ROWS, HID), _fixed(ROWS, HID), weight, weight],
-            out_specs=pl.BlockSpec((1, MAIN, WIDE), lambda i, c: (i, 0, 0)),
+            out_specs=pl.BlockSpec((1, MAIN, WIDE), lambda i, c: (i // 2, 0, 0)),
         ),
         out_shape=pltpu.HBM((2, MAIN, WIDE), BF),
         compiler_params=_params(),
@@ -379,14 +401,14 @@
 
 
 def _back(core, grads, grads_p, w_gate, w_up, w_gate_p, w_up_p):
-    weight = pl.BlockSpec((COLS, HID), lambda i, c: (2 * i + c[0], 0))
+    weight = pl.BlockSpec((HALF, HID), lambda i, c: (_piece(i, c[0]), 0))
     return pl.pallas_call(
         _back_kernel,
         grid_spec=pltpu.PrefetchScalarGridSpec(
             num_scalar_prefetch=1,
-            grid=(2,),
+            grid=(STEPS,),
             in_specs=[_fixed(ROWS, 2 * HID), _fixed(ROWS, 2 * HID), weight, weight, weight, weight],
-            out_specs=pl.BlockSpec((1, MAIN, WIDE), lambda i, c: (i, 0, 0)),
+            out_specs=pl.BlockSpec((1, MAIN, WIDE), lambda i, c: (i // 2, 0, 0)),
         ),
         out_shape=pltpu.HBM((2, MAIN, WIDE), BF),
         compiler_params=_params(),
@@ -416,7 +438,7 @@
     wg, wu, wd = w_gate[0], w_up[0], w_down[0]
     ids_t, probs_t = expert_ids.T, route_probs.T
 
-    send_x = _local(_pack_rows_kernel, pltpu.HBM((2, MAIN, WIDE), BF), 2e8, 3e6, "pack_rows", _hbm(ids_t), _hbm(probs_t), _hbm(tokens))
+    send_x = _local(_pack_rows_kernel, pltpu.HBM((2, MAIN, WIDE), BF), 2e8, 3e6, "pack_rows", _hbm(ids_t), _hbm(tokens))
     recv_x = _exchange(send_x)
     send_e, pick, weight = _local(
         _pack_grads_kernel,

time: 144 us -> 145 us (level)
  Pallas kernels: 45.7 us -> 50.6 us
  local copies, waits for them, and re-layouts: 3.89 us -> 1.35 us
    unnamed x16 -> x12, local copies, waits for them, and re-layouts: 3.89 us -> 1.35 us
  transfers between devices with their start and end apart: 13 -> 13, of which waited for: 7 -> 7; matrix products, arithmetic and copies ran while one was open for 11% -> 10% of each run, Pallas kernels for 29% -> 32%
where the time goes in v4:
time: 145 us; the launch traced here: 144 us
  Pallas kernels  50.6 us (35%)
  waiting for transfers between devices  40.8 us (28%)
  starting transfers between devices  35.7 us (25%)
  matrix products  15.1 us (10%)
    all_to_all x4, waiting for transfers between devices, _exchange(): lax.all_to_all(chunks, ('yhi', 'expert'), split_axis=0, concat_axis=0, ti...  36.8 us
    all_to_all x4, starting transfers between devices, _exchange(): lax.all_to_all(chunks, ('yhi', 'expert'), split_axis=0, concat_axis=0, ti...  30.7 us
    dot_general x3, matrix products, _dot_tn(): lax.dot_general(a, b, (((0,), (0,)), ((), ())), preferred_element_type=F32)  15.1 us
    pallas_call x4, Pallas kernels, _local(): pl.pallas_call(kernel, out_shape=out_shape, compiler_params=_params(), co...  11 us
    pallas_call x1, Pallas kernels, _back(): pl.pallas_call(_back_kernel, grid_spec=pltpu.PrefetchScalarGridSpec(num_s...  9.1 us
    pallas_call x1, Pallas kernels, _result(): pl.pallas_call(_result_kernel, grid_spec=pltpu.PrefetchScalarGridSpec(num...  6.69 us
    pallas_call x1, Pallas kernels, _forward_own(): _half_pass(_forward_own_kernel, False, ['row', 'row'], [], [('slots', plt...  6.62 us
    pallas_call x1, Pallas kernels, _forward_other(): _half_pass(_forward_other_kernel, True, ['row', 'row'], ['hidden', 'hidde...  6.51 us
  transfers between devices with their start and end apart: 13, of which 7 were waited for; matrix products, arithmetic and copies ran while one was open for 10% of the time, Pallas kernels for 32%

profile of v4, /device:TPU:0, one launch (start us, length us, event | category | flops | bytes accessed | tf_op | source)
XLA Modules:
  0.0 144.2 jit_solution(17240916433857684061)
XLA Ops:
  0.6 3.0 %pack_rows.1 = bf16[2,256,1920]{2,1,0:T(8,128)(2,1)} custom-call(s32[6,128]{1,0:T(8,128)} %bitcast.43, bf16[128,1280]{1,0:T(8,128)(2,1)} %tok_ref.1), custom_call_target="tpu_custom_call" | custom-call | flops 200000000 | bytes 3000000 | tf_op jit(solution)/shard_map/pack_rows/pallas_call | solution.py:421
  3.6 11.5 %all-to-all-start = ((bf16[64,8,1920]{2,1,0:T(8,128)(2,1)}), bf16[64,8,1920]{2,1,0:T(8,128)(2,1)S(1)}, u32[]{:S(2)}, u32[]{:S(2)}) async-start(bf16[64,8,1920]{2,1,0:T(8,128)(2,1)} %bitcast.36), calls=%async_computation | async-start | bytes 3932160 | tf_op jit(solution)/shard_map/all_to_all | solution.py:428
  15.1 0.1 collective-permute-start.2
  15.2 0.5 collective-permute-start.5
  15.7 0.1 collective-permute-start.6
  15.8 3.1 %pack_grads.1 = (bf16[2,256,1920]{2,1,0:T(8,128)(2,1)}, bf16[512,128]{1,0:T(8,128)(2,1)S(1)}, f32[512,128]{1,0:T(8,128)S(1)}) custom-call(s32[6,128]{1,0:T(8,128)} %bitcast.44, f32[6,128]{1,0:T(8,128)} %bitcast.46, bf16[128,1280]{1,0:T(8,128)(2,1)} %cot_ref.3), custom_call_target="tpu_custom_call" | custom-call | flops 200000000 | bytes 3000000 | tf_op jit(solution)/shard_map/pack_grads/pallas_call | solution.py:421
  18.9 0.0 copy-start
  18.9 0.6 copy-done
  19.5 0.0 copy-start.2
  19.5 0.7 copy-done.2
  20.2 22.7 %all-to-all-done = bf16[64,8,1920]{2,1,0:T(8,128)(2,1)S(1)} async-done(((bf16[64,8,1920]{2,1,0:T(8,128)(2,1)}), bf16[64,8,1920]{2,1,0:T(8,128)(2,1)S(1)}, u32[]{:S(2)}, u32[]{:S(2)}) %all-to-all-start) | async-done | bytes 1966112 | tf_op jit(solution)/shard_map/all_to_all | solution.py:428
  42.9 0.0 copy-start.5
  42.9 6.3 %all-to-all-start.1 = ((bf16[64,8,1920]{2,1,0:T(8,128)(2,1)}), bf16[64,8,1920]{2,1,0:T(8,128)(2,1)}, u32[]{:S(2)}, u32[]{:S(2)}) async-start(bf16[64,8,1920]{2,1,0:T(8,128)(2,1)} %bitcast.39), calls=%async_computation.1 | async-start | bytes 3932160 | tf_op jit(solution)/shard_map/all_to_all | solution.py:428
  49.2 0.1 collective-permute-start
  49.3 0.0 copy-done.5
  49.3 6.6 %forward_own.1 = (bf16[384,5120]{1,0:T(8,128)(2,1)}, f32[384,384]{1,0:T(8,128)S(1)}, f32[384,384]{1,0:T(8,128)S(1)}) custom-call(s32[1]{0:T(128)} %bitcast.6.core_ref, bf16[2,256,1920]{2,1,0:T(8,128)(2,1)} %bitcast.41, bf16[2,256,1920]{2,1,0:T(8,128)(2,1)} %bitcast.42, bf16[5120,384]{1,0:T(8,128)(2,1)} %bitcast.24, bf16[5120,384]{1,0:T(8,128)(2,1)} %bitcast.28), custom_call_target="tpu_custom_call" | custom-call | flops 24159191040 | bytes 144000000 | tf_op jit(solution)/shard_map/forward_own/pallas_call | solution.py:324
  55.9 0.0 collective-permute-done.main_ref.rest_ref
  55.9 6.5 %forward_other.1 = (bf16[384,5120]{1,0:T(8,128)(2,1)}, f32[384,384]{1,0:T(8,128)S(1)}, f32[384,384]{1,0:T(8,128)S(1)}, bf16[384,384]{1,0:T(8,128)(2,1)S(1)}) custom-call(s32[1]{0:T(128)} %bitcast.6.core_ref, bf16[2,256,1920]{2,1,0:T(8,128)(2,1)S(1)} %collective-permute-done.main_ref.rest_ref, ...), custom_call_target="tpu_custom_call", output_to_operand_aliasing={{0}: (7, {})} | custom-call | flops 11796480 | bytes 70312 | tf_op jit(solution)/shard_map/forward_other/pallas_call | solution.py:338
  62.4 0.5 collective-permute-start.1
  62.9 0.0 collective-permute-done.2.wdp_ref
  62.9 1.2 collective-permute-done.1.hp_ref
  64.1 6.7 %result.1 = bf16[2,256,1920]{2,1,0:T(8,128)(2,1)} custom-call(s32[1]{0:T(128)} %bitcast.6.core_ref, bf16[384,384]{1,0:T(8,128)(2,1)S(1)} %get-tuple-element.40.h_ref, bf16[384,384]{1,0:T(8,128)(2,1)S(1)} %collective-permute-done.1.hp_ref, bf16[384,5120]{1,0:T(8,128)(2,1)} %bitcast.32, bf16[384,5120]{1,0:T(8,128)(2,1)} %collective-permute-done.2.wdp_ref), custom_call_target="tpu_custom_call" | custom-call | flops 11796480 | bytes 54687 | tf_op jit(solution)/shard_map/result/pallas_call | solution.py:388
  70.8 4.6 %all-to-all-done.1 = bf16[64,8,1920]{2,1,0:T(8,128)(2,1)} async-done(((bf16[64,8,1920]{2,1,0:T(8,128)(2,1)}), bf16[64,8,1920]{2,1,0:T(8,128)(2,1)}, u32[]{:S(2)}, u32[]{:S(2)}) %all-to-all-start.1) | async-done | bytes 1966112 | tf_op jit(solution)/shard_map/all_to_all | solution.py:428
  75.4 6.8 %all-to-all-start.2 = ((bf16[64,8,1920]{2,1,0:T(8,128)(2,1)}), bf16[64,8,1920]{2,1,0:T(8,128)(2,1)}, u32[]{:S(2)}, u32[]{:S(2)}) async-start(bf16[64,8,1920]{2,1,0:T(8,128)(2,1)} %bitcast.35), calls=%async_computation.2 | async-start | bytes 3932160 | tf_op jit(solution)/shard_map/all_to_all | solution.py:428
  82.2 0.1 collective-permute-start.3
  82.3 5.3 %backward_own.1 = (bf16[384,5120]{1,0:T(8,128)(2,1)}, f32[384,384]{1,0:T(8,128)S(1)}) custom-call(s32[1]{0:T(128)} %bitcast.6.core_ref, bf16[2,256,1920]{2,1,0:T(8,128)(2,1)} %bitcast.5.main_ref.rest_ref, bf16[2,256,1920]{2,1,0:T(8,128)(2,1)} %bitcast.5.main_ref.rest_ref, bf16[384,5120]{1,0:T(8,128)(2,1)} %bitcast.33), custom_call_target="tpu_custom_call" | custom-call | flops 24159191040 | bytes 144000000 | tf_op jit(solution)/shard_map/backward_own/pallas_call | solution.py:358
  87.5 0.0 collective-permute-done.3.main_ref.rest_ref
  87.5 5.3 %backward_other.1 = (bf16[384,5120]{1,0:T(8,128)(2,1)}, bf16[384,768]{1,0:T(8,128)(2,1)S(1)}) custom-call(s32[1]{0:T(128)} %bitcast.6.core_ref, bf16[2,256,1920]{2,1,0:T(8,128)(2,1)S(1)} %collective-permute-done.3.main_ref.rest_ref, bf16[2,256,1920]{2,1,0:T(8,128)(2,1)S(1)} %collective-permute-done.3.main_ref.rest_ref, ...), custom_call_target="tpu_custom_call", output_to_operand_aliasing={{0}: (7, {})} | custom-call | flops 5898240 | bytes 46875 | tf_op jit(solution)/shard_map/backward_other/pallas_call | solution.py:372
  92.9 0.5 collective-permute-start.4
  93.3 0.0 collective-permute-done.5.wgp_ref
  93.3 0.0 collective-permute-done.6.wup_ref
  93.3 1.6 %collective-permute-done.4.dp_ref = bf16[384,768]{1,0:T(8,128)(2,1)S(1)} collective-permute-done((bf16[384,768]{1,0:T(8,128)(2,1)S(1)}, bf16[384,768]{1,0:T(8,128)(2,1)S(1)}, u32[]{:S(2)}, u32[]{:S(2)}) %collective-permute-start.4) | collective-permute-done | bytes 589856 | tf_op jit(solution)/shard_map/ppermute | solution.py:433
  95.0 9.1 %back.1 = bf16[2,256,1920]{2,1,0:T(8,128)(2,1)} custom-call(s32[1]{0:T(128)} %bitcast.6.core_ref, bf16[384,768]{1,0:T(8,128)(2,1)S(1)} %get-tuple-element.48.d_ref, bf16[384,768]{1,0:T(8,128)(2,1)S(1)} %collective-permute-done.4.dp_ref, bf16[5120,384]{1,0:T(8,128)(2,1)} %bitcast.26, bf16[5120,384]{1,0:T(8,128)(2,1)} %bitcast.30, ...), custom_call_target="tpu_custom_call" | custom-call | flops 23592960 | bytes 85937 | tf_op jit(solution)/shard_map/back/pallas_call | solution.py:405
  104.1 5.5 %all-to-all-done.2 = bf16[64,8,1920]{2,1,0:T(8,128)(2,1)} async-done(((bf16[64,8,1920]{2,1,0:T(8,128)(2,1)}), bf16[64,8,1920]{2,1,0:T(8,128)(2,1)}, u32[]{:S(2)}, u32[]{:S(2)}) %all-to-all-start.2) | async-done | bytes 1966112 | tf_op jit(solution)/shard_map/all_to_all | solution.py:428
  109.6 6.2 %all-to-all-start.3 = ((bf16[64,8,1920]{2,1,0:T(8,128)(2,1)}), bf16[64,8,1920]{2,1,0:T(8,128)(2,1)S(1)}, u32[]{:S(2)}, u32[]{:S(2)}) async-start(bf16[64,8,1920]{2,1,0:T(8,128)(2,1)} %bitcast.37), calls=%async_computation.3 | async-start | bytes 3932160 | tf_op jit(solution)/shard_map/all_to_all | solution.py:428
  115.8 3.6 %mixed.1 = (bf16[128,1280]{1,0:T(8,128)(2,1)}, f32[6,128]{1,0:T(8,128)S(1)}) custom-call(s32[6,128]{1,0:T(8,128)} %bitcast.45, bf16[512,128]{1,0:T(8,128)(2,1)} %copy-done, f32[512,128]{1,0:T(8,128)} %copy-done.2, bf16[128,1280]{1,0:T(8,128)(2,1)} %cot_ref.3, bf16[2,256,1920]{2,1,0:T(8,128)(2,1)} %bitcast.11.r_ref), custom_call_target="tpu_custom_call" | custom-call | flops 400000000 | bytes 3000000 | tf_op jit(solution)/shard_map/mixed/pallas_call | solution.py:421
  119.4 0.1 collective-permute-start.7
  119.5 1.2 collective-permute-done.7
  120.6 3.2 %collective-permute-start.8 = (f32[6,128]{1,0:T(8,128)S(1)}, f32[6,128]{1,0:T(8,128)S(1)}, u32[]{:S(2)}, u32[]{:S(2)}) collective-permute-start(f32[6,128]{1,0:T(8,128)S(1)} %add.3.inner_ref), channel_id=1, source_target_pairs={{0,2},{2,0},{1,3},{3,1},{4,6},{6,4},{5,7},{7,5},{8,10},{10,8},{9,1... | collective-permute-start | bytes 9224 | tf_op jit(solution)/shard_map/ppermute | solution.py:433
  123.8 0.0 copy-start.4
  123.8 6.8 %convolution_convert_fusion.2 = bf16[5120,384]{1,0:T(8,128)(2,1)} fusion(bf16[384,5120]{1,0:T(8,128)(2,1)} %get-tuple-element.49, bf16[384,768]{1,0:T(8,128)(2,1)S(1)} %get-tuple-element.48.d_ref), kind=kOutput, calls=%fused_computation.2 | convolution fusion | flops 1511915520 | bytes 8159232 | tf_op jit(solution)/shard_map/dot_general | solution.py:39
  130.6 0.0 copy-done.4
  130.6 0.0 copy-start.3
  130.6 4.1 %convolution_convert_fusion.1 = bf16[5120,384]{1,0:T(8,128)(2,1)} fusion(bf16[384,5120]{1,0:T(8,128)(2,1)S(1)} %copy-done.4, bf16[384,768]{1,0:T(8,128)(2,1)S(1)} %get-tuple-element.48.d_ref), kind=kOutput, calls=%fused_computation.1 | convolution fusion | flops 1511915520 | bytes 8159232 | tf_op jit(solution)/shard_map/dot_general | solution.py:39
  134.7 0.0 copy-done.3
  134.7 0.0 copy-start.1
  134.7 4.2 %convolution_convert_fusion = bf16[384,5120]{1,0:T(8,128)(2,1)} fusion(bf16[384,384]{1,0:T(8,128)(2,1)S(1)} %get-tuple-element.40.h_ref, bf16[384,5120]{1,0:T(8,128)(2,1)S(1)} %copy-done.3), kind=kOutput, calls=%fused_computation | convolution fusion | flops 1511915520 | bytes 8159232 | tf_op jit(solution)/shard_map/dot_general | solution.py:39
  138.9 4.0 %all-to-all-done.3 = bf16[64,8,1920]{2,1,0:T(8,128)(2,1)S(1)} async-done(((bf16[64,8,1920]{2,1,0:T(8,128)(2,1)}), bf16[64,8,1920]{2,1,0:T(8,128)(2,1)S(1)}, u32[]{:S(2)}, u32[]{:S(2)}) %all-to-all-start.3) | async-done | bytes 1966112 | tf_op jit(solution)/shard_map/all_to_all | solution.py:428
  142.9 0.0 collective-permute-done.8.far_ref
  142.9 0.0 copy-done.1
  142.9 1.3 grad_tokens.1
  (1 shorter events, 0.0 us)
Async XLA Ops:
  3.6 39.3 %all-to-all-start = ((bf16[64,8,1920]{2,1,0:T(8,128)(2,1)}), bf16[64,8,1920]{2,1,0:T(8,128)(2,1)S(1)}, u32[]{:S(2)}, u32[]{:S(2)}) async-start(bf16[64,8,1920]{2,1,0:T(8,128)(2,1)} %bitcast.36), calls=%async_computation | async-start | bytes 3932160 | tf_op jit(solution)/shard_map/all_to_all | solution.py:428
  15.1 47.7 %collective-permute-start.2 = (bf16[384,5120]{1,0:T(8,128)(2,1)}, bf16[384,5120]{1,0:T(8,128)(2,1)}, u32[]{:S(2)}, u32[]{:S(2)}) collective-permute-start(bf16[384,5120]{1,0:T(8,128)(2,1)} %bitcast.31), channel_id=1, source_target_pairs={{0,1},{1,0},{2,3},{3,2},{4,5},{5,4},{6,7},{7,6},{8,9},{9,8},{10,11... | collective-permute-start | bytes 11796488 | tf_op jit(solution)/shard_map/ppermute | solution.py:433
  15.2 78.1 %collective-permute-start.5 = (bf16[5120,384]{1,0:T(8,128)(2,1)}, bf16[5120,384]{1,0:T(8,128)(2,1)}, u32[]{:S(2)}, u32[]{:S(2)}) collective-permute-start(bf16[5120,384]{1,0:T(8,128)(2,1)} %bitcast.23), channel_id=1, source_target_pairs={{0,1},{1,0},{2,3},{3,2},{4,5},{5,4},{6,7},{7,6},{8,9},{9,8},{10,11... | collective-permute-start | bytes 11796488 | tf_op jit(solution)/shard_map/ppermute | solution.py:433
  15.7 77.6 %collective-permute-start.6 = (bf16[5120,384]{1,0:T(8,128)(2,1)}, bf16[5120,384]{1,0:T(8,128)(2,1)}, u32[]{:S(2)}, u32[]{:S(2)}) collective-permute-start(bf16[5120,384]{1,0:T(8,128)(2,1)} %bitcast.27), channel_id=1, source_target_pairs={{0,1},{1,0},{2,3},{3,2},{4,5},{5,4},{6,7},{7,6},{8,9},{9,8},{10,11... | collective-permute-start | bytes 11796488 | tf_op jit(solution)/shard_map/ppermute | solution.py:433
  18.9 0.6 copy-start
  19.5 0.7 copy-start.2
  42.9 6.4 %copy-start.5 = (bf16[64,8,1920]{2,1,0:T(8,128)(2,1)}, bf16[64,8,1920]{2,1,0:T(8,128)(2,1)S(1)}, u32[]{:S(2)}) copy-start(bf16[64,8,1920]{2,1,0:T(8,128)(2,1)S(1)} %all-to-all-done) | copy-start | bytes 5898244
  42.9 32.5 %all-to-all-start.1 = ((bf16[64,8,1920]{2,1,0:T(8,128)(2,1)}), bf16[64,8,1920]{2,1,0:T(8,128)(2,1)}, u32[]{:S(2)}, u32[]{:S(2)}) async-start(bf16[64,8,1920]{2,1,0:T(8,128)(2,1)} %bitcast.39), calls=%async_computation.1 | async-start | bytes 3932160 | tf_op jit(solution)/shard_map/all_to_all | solution.py:428
  49.2 6.7 %collective-permute-start = (bf16[2,256,1920]{2,1,0:T(8,128)(2,1)S(1)}, bf16[2,256,1920]{2,1,0:T(8,128)(2,1)S(1)}, u32[]{:S(2)}, u32[]{:S(2)}) collective-permute-start(bf16[2,256,1920]{2,1,0:T(8,128)(2,1)S(1)} %bitcast.40), channel_id=1, source_target_pairs={{0,1},{1,0},{2,3},{3,2},{4,5},{5,4},{6,7},{7,6},{8,9},{9,8},{10,11... | collective-permute-start | bytes 5898248 | tf_op jit(solution)/shard_map/ppermute | solution.py:433
  62.4 1.7 %collective-permute-start.1 = (bf16[384,384]{1,0:T(8,128)(2,1)S(1)}, bf16[384,384]{1,0:T(8,128)(2,1)S(1)}, u32[]{:S(2)}, u32[]{:S(2)}) collective-permute-start(bf16[384,384]{1,0:T(8,128)(2,1)S(1)} %get-tuple-element.40.h_ref), channel_id=1, source_target_pairs={{0,1},{1,0},{2,3},{3,2},{4,5},{5,4},{6,7},{7,6},{8,9},{9,8},{10,11... | collective-permute-start | bytes 884744 | tf_op jit(solution)/shard_map/ppermute | solution.py:433
  75.4 34.2 %all-to-all-start.2 = ((bf16[64,8,1920]{2,1,0:T(8,128)(2,1)}), bf16[64,8,1920]{2,1,0:T(8,128)(2,1)}, u32[]{:S(2)}, u32[]{:S(2)}) async-start(bf16[64,8,1920]{2,1,0:T(8,128)(2,1)} %bitcast.35), calls=%async_computation.2 | async-start | bytes 3932160 | tf_op jit(solution)/shard_map/all_to_all | solution.py:428
  82.2 5.4 %collective-permute-start.3 = (bf16[2,256,1920]{2,1,0:T(8,128)(2,1)}, bf16[2,256,1920]{2,1,0:T(8,128)(2,1)S(1)}, u32[]{:S(2)}, u32[]{:S(2)}) collective-permute-start(bf16[2,256,1920]{2,1,0:T(8,128)(2,1)} %bitcast.5.main_ref.rest_ref), channel_id=1, source_target_pairs={{0,1},{1,0},{2,3},{3,2},{4,5},{5,4},{6,7},{7,6},{8,9},{9,8},{10,11... | collective-permute-start | bytes 5898248 | tf_op jit(solution)/shard_map/ppermute | solution.py:433
  92.9 2.1 %collective-permute-start.4 = (bf16[384,768]{1,0:T(8,128)(2,1)S(1)}, bf16[384,768]{1,0:T(8,128)(2,1)S(1)}, u32[]{:S(2)}, u32[]{:S(2)}) collective-permute-start(bf16[384,768]{1,0:T(8,128)(2,1)S(1)} %get-tuple-element.48.d_ref), channel_id=1, source_target_pairs={{0,1},{1,0},{2,3},{3,2},{4,5},{5,4},{6,7},{7,6},{8,9},{9,8},{10,11... | collective-permute-start | bytes 1769480 | tf_op jit(solution)/shard_map/ppermute | solution.py:433
  109.6 33.3 %all-to-all-start.3 = ((bf16[64,8,1920]{2,1,0:T(8,128)(2,1)}), bf16[64,8,1920]{2,1,0:T(8,128)(2,1)S(1)}, u32[]{:S(2)}, u32[]{:S(2)}) async-start(bf16[64,8,1920]{2,1,0:T(8,128)(2,1)} %bitcast.37), calls=%async_computation.3 | async-start | bytes 3932160 | tf_op jit(solution)/shard_map/all_to_all | solution.py:428
  119.4 1.2 collective-permute-start.7
  120.6 22.3 %collective-permute-start.8 = (f32[6,128]{1,0:T(8,128)S(1)}, f32[6,128]{1,0:T(8,128)S(1)}, u32[]{:S(2)}, u32[]{:S(2)}) collective-permute-start(f32[6,128]{1,0:T(8,128)S(1)} %add.3.inner_ref), channel_id=1, source_target_pairs={{0,2},{2,0},{1,3},{3,1},{4,6},{6,4},{5,7},{7,5},{8,10},{10,8},{9,1... | collective-permute-start | bytes 9224 | tf_op jit(solution)/shard_map/ppermute | solution.py:433
  123.8 6.8 %copy-start.4 = (bf16[384,5120]{1,0:T(8,128)(2,1)S(1)}, bf16[384,5120]{1,0:T(8,128)(2,1)}, u32[]{:S(2)}) copy-start(bf16[384,5120]{1,0:T(8,128)(2,1)} %get-tuple-element.49) | copy-start | bytes 11796484
  130.6 4.1 %copy-start.3 = (bf16[384,5120]{1,0:T(8,128)(2,1)S(1)}, bf16[384,5120]{1,0:T(8,128)(2,1)}, u32[]{:S(2)}) copy-start(bf16[384,5120]{1,0:T(8,128)(2,1)} %get-tuple-element.50) | copy-start | bytes 11796484
  134.7 8.2 %copy-start.1 = (bf16[512,128]{1,0:T(8,128)(2,1)S(1)}, bf16[512,128]{1,0:T(8,128)(2,1)}, u32[]{:S(2)}) copy-start(bf16[512,128]{1,0:T(8,128)(2,1)} %copy-done) | copy-start | bytes 393220

commit v5 on v3

--- a/solution.py
+++ b/solution.py
@@ -42,14 +42,15 @@
     return lax.broadcasted_iota(jnp.int32, shape, dim)
 
 
-def _routing(ids_t, probs_t):
+def _routing(ids_t, probs_t=None):
     expert = _iota((EXPERTS, BLOCK), 0)
     chosen = jnp.zeros((EXPERTS, BLOCK), F32)
     weight = jnp.zeros((EXPERTS, BLOCK), F32)
     for k in range(TOPK):
         hit = ids_t[k : k + 1, :] == expert
         chosen = jnp.where(hit, 1.0, chosen)
-        weight = jnp.where(hit, probs_t[k : k + 1, :], weight)
+        if probs_t is not None:
+            weight = jnp.where(hit, probs_t[k : k + 1, :], weight)
     earlier = (_iota((BLOCK, BLOCK), 0) < _iota((BLOCK, BLOCK), 1)).astype(F32).astype(BF)
     before = _dot(chosen.astype(BF), earlier)
     code = jnp.where(chosen > 0.5, before, -1.0)
@@ -59,6 +60,8 @@
     j = _iota((MAIN, BLOCK), 0)
     main = jnp.where(place == (j % 8).astype(F32), 1.0, 0.0)
     rest = jnp.where(place == (8 + j % 4).astype(F32), 1.0, 0.0)
+    if probs_t is None:
+        return main, rest, None
     hi = weight.astype(BF)
     left = weight - hi.astype(F32)
     mid = left.astype(BF)
@@ -80,8 +83,8 @@
     return a, b
 
 
-def _pack_rows_kernel(ids_ref, probs_ref, tok_ref, out_ref):
-    main, rest, _ = _routing(ids_ref[...], probs_ref[...])
+def _pack_rows_kernel(ids_ref, tok_ref, out_ref):
+    main, rest, _ = _routing(ids_ref[...])
     a, b = _send(main, rest, tok_ref[...])
     a, b = a.astype(BF), b.astype(BF)
     for y in range(2):
@@ -200,6 +203,14 @@
     value = _dot_nt(d_ref[:, :HID], wg_ref[...]) + _dot_nt(d_ref[:, HID:], wu_ref[...])
     value += _dot_nt(dp_ref[:, :HID], wgp_ref[...]) + _dot_nt(dp_ref[:, HID:], wup_ref[...])
     _pack(value.astype(BF), out_ref)
+
+
+def _grad_down_kernel(h_ref, e_ref, out_ref, t_ref):
+    @pl.when(pl.program_id(0) == 0)
+    def _():
+        t_ref[...] = h_ref[...].astype(F32).T.astype(BF)
+
+    out_ref[...] = _dot(t_ref[...], e_ref[...]).astype(BF)
 
 
 def _home(pick, r_ref):
@@ -329,7 +340,7 @@
         LATE * 9e6,
         "forward_other",
         {6: 0},
-    )(core, _hbm(other), _hbm(w_gate), _hbm(w_up), gate, up, _hbm(x))
+    )(core, other, _hbm(w_gate), _hbm(w_up), gate, up, _hbm(x))
 
 
 def _backward_own(core, own, w_down):
@@ -358,7 +369,7 @@
         LATE * 6e6,
         "backward_other",
         {6: 0},
-    )(core, _hbm(other), _hbm(w_down), partial, gate, up, _hbm(e))
+    )(core, other, _hbm(w_down), partial, gate, up, _hbm(e))
 
 
 def _result(core, hidden, hidden_p, w_down, w_down_p):
@@ -395,6 +406,21 @@
     )(core, grads, grads_p, _hbm(w_gate), _hbm(w_up), _hbm(w_gate_p), _hbm(w_up_p))
 
 
+def _grad_down(hidden, e):
+    block = pl.BlockSpec((HID, COLS), lambda i: (0, i))
+    return pl.pallas_call(
+        _grad_down_kernel,
+        grid=(4,),
+        in_specs=[pl.BlockSpec((ROWS, HID), lambda i: (0, 0)), pl.BlockSpec((ROWS, COLS), lambda i: (0, i))],
+        out_specs=block,
+        out_shape=_shape((HID, D), BF),
+        scratch_shapes=[pltpu.VMEM((HID, ROWS), BF)],
+        compiler_params=_params(),
+        cost_estimate=_cost(2 * ROWS * D * HID, 8e6),
+        name="grad_down",
+    )(hidden, _hbm(e))
+
+
 def _local(kernel, out_shape, flops, moved, name, *args):
     return pl.pallas_call(
         kernel, out_shape=out_shape, compiler_params=_params(), cost_estimate=_cost(flops, moved), name=name
@@ -416,7 +442,7 @@
     wg, wu, wd = w_gate[0], w_up[0], w_down[0]
     ids_t, probs_t = expert_ids.T, route_probs.T
 
-    send_x = _local(_pack_rows_kernel, pltpu.HBM((2, MAIN, WIDE), BF), 2e8, 3e6, "pack_rows", _hbm(ids_t), _hbm(probs_t), _hbm(tokens))
+    send_x = _local(_pack_rows_kernel, pltpu.HBM((2, MAIN, WIDE), BF), 2e8, 3e6, "pack_rows", _hbm(ids_t), _hbm(tokens))
     recv_x = _exchange(send_x)
     send_e, pick, weight = _local(
         _pack_grads_kernel,
@@ -443,7 +469,7 @@
     send_b = _back(core, grads, _swap(grads), wg, wu, wg_p, wu_p)
     recv_b = _exchange(send_b)
 
-    g_down = _dot_tn(hidden, e).astype(BF)
+    g_down = _grad_down(hidden, e)
     g_gate = _dot_tn(x, grads[:, :HID]).astype(BF)
     g_up = _dot_tn(x, grads[:, HID:]).astype(BF)
 

time: 144 us -> 142 us (0.986)
  Pallas kernels: 45.7 us -> 51.1 us
  matrix products: 15.1 us -> 10.9 us
  local copies, waits for them, and re-layouts: 3.89 us -> 1.36 us
    pallas_call x0 -> x1, Pallas kernels: none -> 6.02 us  [_grad_down(): pl.pallas_call(_grad_down_kernel, grid=(4,), in_specs=[pl.BlockSpec((ROWS...]
    dot_general x3 -> x2, matrix products: 15.1 us -> 10.9 us  [_dot_tn(): lax.dot_general(a, b, (((0,), (0,)), ((), ())), preferred_element_type=F32)]
    unnamed x16 -> x10, local copies, waits for them, and re-layouts: 3.89 us -> 1.36 us
  transfers between devices with their start and end apart: 13 -> 13, of which waited for: 7 -> 7; matrix products, arithmetic and copies ran while one was open for 11% -> 8% of each run, Pallas kernels for 29% -> 33%
where the time goes in v5:
time: 142 us; the launch traced here: 141 us
  Pallas kernels  51.1 us (36%)
  waiting for transfers between devices  41.5 us (29%)
  starting transfers between devices  35.7 us (25%)
  matrix products  10.9 us (8%)
    all_to_all x4, waiting for transfers between devices, _exchange(): lax.all_to_all(chunks, ('yhi', 'expert'), split_axis=0, concat_axis=0, ti...  37.5 us
    all_to_all x4, starting transfers between devices, _exchange(): lax.all_to_all(chunks, ('yhi', 'expert'), split_axis=0, concat_axis=0, ti...  30.7 us
    pallas_call x4, Pallas kernels, _local(): pl.pallas_call(kernel, out_shape=out_shape, compiler_params=_params(), co...  11 us
    dot_general x2, matrix products, _dot_tn(): lax.dot_general(a, b, (((0,), (0,)), ((), ())), preferred_element_type=F32)  10.9 us
    pallas_call x1, Pallas kernels, _back(): pl.pallas_call(_back_kernel, grid_spec=pltpu.PrefetchScalarGridSpec(num_s...  8.67 us
    pallas_call x1, Pallas kernels, _grad_down(): pl.pallas_call(_grad_down_kernel, grid=(4,), in_specs=[pl.BlockSpec((ROWS...  6.02 us
    pallas_call x1, Pallas kernels, _result(): pl.pallas_call(_result_kernel, grid_spec=pltpu.PrefetchScalarGridSpec(num...  5.93 us
    pallas_call x1, Pallas kernels, _forward_own(): _half_pass(_forward_own_kernel, False, ['row', 'row'], [], [('slots', plt...  5.61 us
  transfers between devices with their start and end apart: 13, of which 7 were waited for; matrix products, arithmetic and copies ran while one was open for 8% of the time, Pallas kernels for 33%

profile of v5, /device:TPU:0, one launch (start us, length us, event | category | flops | bytes accessed | tf_op | source)
XLA Modules:
  0.0 141.3 jit_solution(16036427694471310408)
XLA Ops:
  0.6 3.0 %pack_rows.1 = bf16[2,256,1920]{2,1,0:T(8,128)(2,1)} custom-call(s32[6,128]{1,0:T(8,128)} %bitcast.40, bf16[128,1280]{1,0:T(8,128)(2,1)} %tok_ref.1), custom_call_target="tpu_custom_call" | custom-call | flops 200000000 | bytes 3000000 | tf_op jit(solution)/shard_map/pack_rows/pallas_call | solution.py:425
  3.6 11.5 %all-to-all-start = ((bf16[64,8,1920]{2,1,0:T(8,128)(2,1)}), bf16[64,8,1920]{2,1,0:T(8,128)(2,1)S(1)}, u32[]{:S(2)}, u32[]{:S(2)}) async-start(bf16[64,8,1920]{2,1,0:T(8,128)(2,1)} %bitcast.34), calls=%async_computation | async-start | bytes 3932160 | tf_op jit(solution)/shard_map/all_to_all | solution.py:432
  15.1 0.1 collective-permute-start.2
  15.2 0.5 collective-permute-start.5
  15.7 0.1 collective-permute-start.6
  15.8 3.1 %pack_grads.1 = (bf16[2,256,1920]{2,1,0:T(8,128)(2,1)}, bf16[512,128]{1,0:T(8,128)(2,1)S(1)}, f32[512,128]{1,0:T(8,128)S(1)}) custom-call(s32[6,128]{1,0:T(8,128)} %bitcast.41, f32[6,128]{1,0:T(8,128)} %bitcast.43, bf16[128,1280]{1,0:T(8,128)(2,1)} %cot_ref.3), custom_call_target="tpu_custom_call" | custom-call | flops 200000000 | bytes 3000000 | tf_op jit(solution)/shard_map/pack_grads/pallas_call | solution.py:425
  18.9 0.0 copy-start
  18.9 0.6 copy-done
  19.5 0.0 copy-start.2
  19.5 0.7 copy-done.2
  20.2 22.7 %all-to-all-done = bf16[64,8,1920]{2,1,0:T(8,128)(2,1)S(1)} async-done(((bf16[64,8,1920]{2,1,0:T(8,128)(2,1)}), bf16[64,8,1920]{2,1,0:T(8,128)(2,1)S(1)}, u32[]{:S(2)}, u32[]{:S(2)}) %all-to-all-start) | async-done | bytes 1966112 | tf_op jit(solution)/shard_map/all_to_all | solution.py:432
  42.9 0.0 copy-start.4
  42.9 6.3 %all-to-all-start.1 = ((bf16[64,8,1920]{2,1,0:T(8,128)(2,1)}), bf16[64,8,1920]{2,1,0:T(8,128)(2,1)}, u32[]{:S(2)}, u32[]{:S(2)}) async-start(bf16[64,8,1920]{2,1,0:T(8,128)(2,1)} %bitcast.37), calls=%async_computation.1 | async-start | bytes 3932160 | tf_op jit(solution)/shard_map/all_to_all | solution.py:432
  49.2 0.1 collective-permute-start
  49.3 0.0 copy-done.4
  49.3 5.6 %forward_own.1 = (bf16[384,5120]{1,0:T(8,128)(2,1)}, f32[384,384]{1,0:T(8,128)S(1)}, f32[384,384]{1,0:T(8,128)S(1)}) custom-call(s32[1]{0:T(128)} %bitcast.6.core_ref, bf16[2,256,1920]{2,1,0:T(8,128)(2,1)} %bitcast.39, bf16[5120,384]{1,0:T(8,128)(2,1)} %bitcast.22, bf16[5120,384]{1,0:T(8,128)(2,1)} %bitcast.26), custom_call_target="tpu_custom_call" | custom-call | flops 24159191040 | bytes 144000000 | tf_op jit(solution)/shard_map/forward_own/pallas_call | solution.py:313
  54.9 0.0 collective-permute-done.r_ref
  54.9 5.4 %forward_other.1 = (bf16[384,5120]{1,0:T(8,128)(2,1)}, f32[384,384]{1,0:T(8,128)S(1)}, f32[384,384]{1,0:T(8,128)S(1)}, bf16[384,384]{1,0:T(8,128)(2,1)S(1)}) custom-call(s32[1]{0:T(128)} %bitcast.6.core_ref, bf16[2,256,1920]{2,1,0:T(8,128)(2,1)S(1)} %collective-permute-done.r_ref, bf16[5120,384]{1,0:T(8,128)(2,1)} %bitcast.23, ...), custom_call_target="tpu_custom_call", output_to_operand_aliasing={{0}: (6, {})} | custom-call | flops 11796480 | bytes 70312 | tf_op jit(solution)/shard_map/forward_other/pallas_call | solution.py:327
  60.3 0.5 collective-permute-start.1
  60.8 0.0 collective-permute-done.2.wdp_ref
  60.8 1.2 collective-permute-done.1.hp_ref
  62.0 5.9 %result.1 = bf16[2,256,1920]{2,1,0:T(8,128)(2,1)} custom-call(s32[1]{0:T(128)} %bitcast.6.core_ref, bf16[384,384]{1,0:T(8,128)(2,1)S(1)} %get-tuple-element.40.h_ref, bf16[384,384]{1,0:T(8,128)(2,1)S(1)} %collective-permute-done.1.hp_ref, bf16[384,5120]{1,0:T(8,128)(2,1)} %bitcast.30, bf16[384,5120]{1,0:T(8,128)(2,1)} %collective-permute-done.2.wdp_ref), custom_call_target="tpu_custom_call" | custom-call | flops 11796480 | bytes 54687 | tf_op jit(solution)/shard_map/result/pallas_call | solution.py:377
  67.9 7.5 %all-to-all-done.1 = bf16[64,8,1920]{2,1,0:T(8,128)(2,1)} async-done(((bf16[64,8,1920]{2,1,0:T(8,128)(2,1)}), bf16[64,8,1920]{2,1,0:T(8,128)(2,1)}, u32[]{:S(2)}, u32[]{:S(2)}) %all-to-all-start.1) | async-done | bytes 1966112 | tf_op jit(solution)/shard_map/all_to_all | solution.py:432
  75.4 6.8 %all-to-all-start.2 = ((bf16[64,8,1920]{2,1,0:T(8,128)(2,1)}), bf16[64,8,1920]{2,1,0:T(8,128)(2,1)}, u32[]{:S(2)}, u32[]{:S(2)}) async-start(bf16[64,8,1920]{2,1,0:T(8,128)(2,1)} %bitcast.33), calls=%async_computation.2 | async-start | bytes 3932160 | tf_op jit(solution)/shard_map/all_to_all | solution.py:432
  82.2 0.1 collective-permute-start.3
  82.2 4.3 %backward_own.1 = (bf16[384,5120]{1,0:T(8,128)(2,1)}, f32[384,384]{1,0:T(8,128)S(1)}) custom-call(s32[1]{0:T(128)} %bitcast.6.core_ref, bf16[2,256,1920]{2,1,0:T(8,128)(2,1)} %bitcast.5.r_ref, bf16[384,5120]{1,0:T(8,128)(2,1)} %bitcast.31), custom_call_target="tpu_custom_call" | custom-call | flops 24159191040 | bytes 144000000 | tf_op jit(solution)/shard_map/backward_own/pallas_call | solution.py:347
  86.5 0.0 collective-permute-done.3.r_ref
  86.5 4.2 %backward_other.1 = (bf16[384,5120]{1,0:T(8,128)(2,1)}, bf16[384,768]{1,0:T(8,128)(2,1)S(1)}) custom-call(s32[1]{0:T(128)} %bitcast.6.core_ref, bf16[2,256,1920]{2,1,0:T(8,128)(2,1)S(1)} %collective-permute-done.3.r_ref, bf16[384,5120]{1,0:T(8,128)(2,1)} %bitcast.32, f32[384,384]{1,0:T(8,128)S(1)} %get-tuple-element.44.a0_ref, ...), custom_call_target="tpu_custom_call", output_to_operand_aliasing={{0}: (6, {})} | custom-call | flops 5898240 | bytes 46875 | tf_op jit(solution)/shard_map/backward_other/pallas_call | solution.py:361
  90.7 0.5 collective-permute-start.4
  91.2 0.0 collective-permute-done.5.wgp_ref
  91.2 0.0 collective-permute-done.6.wup_ref
  91.2 1.6 %collective-permute-done.4.dp_ref = bf16[384,768]{1,0:T(8,128)(2,1)S(1)} collective-permute-done((bf16[384,768]{1,0:T(8,128)(2,1)S(1)}, bf16[384,768]{1,0:T(8,128)(2,1)S(1)}, u32[]{:S(2)}, u32[]{:S(2)}) %collective-permute-start.4) | collective-permute-done | bytes 589856 | tf_op jit(solution)/shard_map/ppermute | solution.py:437
  92.8 8.7 %back.1 = bf16[2,256,1920]{2,1,0:T(8,128)(2,1)} custom-call(s32[1]{0:T(128)} %bitcast.6.core_ref, bf16[384,768]{1,0:T(8,128)(2,1)S(1)} %get-tuple-element.48.d_ref, bf16[384,768]{1,0:T(8,128)(2,1)S(1)} %collective-permute-done.4.dp_ref, bf16[5120,384]{1,0:T(8,128)(2,1)} %bitcast.24, bf16[5120,384]{1,0:T(8,128)(2,1)} %bitcast.28, ...), custom_call_target="tpu_custom_call" | custom-call | flops 23592960 | bytes 85937 | tf_op jit(solution)/shard_map/back/pallas_call | solution.py:394
  101.5 5.9 %all-to-all-done.2 = bf16[64,8,1920]{2,1,0:T(8,128)(2,1)} async-done(((bf16[64,8,1920]{2,1,0:T(8,128)(2,1)}), bf16[64,8,1920]{2,1,0:T(8,128)(2,1)}, u32[]{:S(2)}, u32[]{:S(2)}) %all-to-all-start.2) | async-done | bytes 1966112 | tf_op jit(solution)/shard_map/all_to_all | solution.py:432
  107.4 6.2 %all-to-all-start.3 = ((bf16[64,8,1920]{2,1,0:T(8,128)(2,1)}), bf16[64,8,1920]{2,1,0:T(8,128)(2,1)S(1)}, u32[]{:S(2)}, u32[]{:S(2)}) async-start(bf16[64,8,1920]{2,1,0:T(8,128)(2,1)} %bitcast.35), calls=%async_computation.3 | async-start | bytes 3932160 | tf_op jit(solution)/shard_map/all_to_all | solution.py:432
  113.6 3.6 %mixed.1 = (bf16[128,1280]{1,0:T(8,128)(2,1)}, f32[6,128]{1,0:T(8,128)S(1)}) custom-call(s32[6,128]{1,0:T(8,128)} %bitcast.42, bf16[512,128]{1,0:T(8,128)(2,1)} %copy-done, f32[512,128]{1,0:T(8,128)} %copy-done.2, bf16[128,1280]{1,0:T(8,128)(2,1)} %cot_ref.3, bf16[2,256,1920]{2,1,0:T(8,128)(2,1)} %bitcast.11.r_ref), custom_call_target="tpu_custom_call" | custom-call | flops 400000000 | bytes 3000000 | tf_op jit(solution)/shard_map/mixed/pallas_call | solution.py:425
  117.2 0.1 collective-permute-start.7
  117.3 1.2 collective-permute-done.7
  118.4 3.2 %collective-permute-start.8 = (f32[6,128]{1,0:T(8,128)S(1)}, f32[6,128]{1,0:T(8,128)S(1)}, u32[]{:S(2)}, u32[]{:S(2)}) collective-permute-start(f32[6,128]{1,0:T(8,128)S(1)} %add.3.inner_ref), channel_id=1, source_target_pairs={{0,2},{2,0},{1,3},{3,1},{4,6},{6,4},{5,7},{7,5},{8,10},{10,8},{9,1... | collective-permute-start | bytes 9224 | tf_op jit(solution)/shard_map/ppermute | solution.py:437
  121.6 0.0 copy-start.3
  121.6 6.8 %convolution_convert_fusion.1 = bf16[5120,384]{1,0:T(8,128)(2,1)} fusion(bf16[384,5120]{1,0:T(8,128)(2,1)} %get-tuple-element.49, bf16[384,768]{1,0:T(8,128)(2,1)S(1)} %get-tuple-element.48.d_ref), kind=kOutput, calls=%fused_computation.1 | convolution fusion | flops 1511915520 | bytes 8159232 | tf_op jit(solution)/shard_map/dot_general | solution.py:38
  128.4 0.0 copy-done.3
  128.4 4.1 %convolution_convert_fusion = bf16[5120,384]{1,0:T(8,128)(2,1)} fusion(bf16[384,5120]{1,0:T(8,128)(2,1)S(1)} %copy-done.3, bf16[384,768]{1,0:T(8,128)(2,1)S(1)} %get-tuple-element.48.d_ref), kind=kOutput, calls=%fused_computation | convolution fusion | flops 1511915520 | bytes 8159232 | tf_op jit(solution)/shard_map/dot_general | solution.py:38
  132.6 0.0 copy-start.1
  132.6 6.0 %grad_down.1 = bf16[384,5120]{1,0:T(8,128)(2,1)} custom-call(bf16[384,384]{1,0:T(8,128)(2,1)S(1)} %get-tuple-element.40.h_ref, bf16[384,5120]{1,0:T(8,128)(2,1)} %get-tuple-element.50.e_ref), custom_call_target="tpu_custom_call" | custom-call | flops 1509949440 | bytes 8000000 | tf_op jit(solution)/shard_map/grad_down/pallas_call | solution.py:411
  138.6 1.4 all-to-all-done.3
  140.0 0.0 collective-permute-done.8.far_ref
  140.0 0.0 copy-done.1
  140.0 1.3 grad_tokens.1
  (1 shorter events, 0.0 us)
Async XLA Ops:
  3.6 39.3 %all-to-all-start = ((bf16[64,8,1920]{2,1,0:T(8,128)(2,1)}), bf16[64,8,1920]{2,1,0:T(8,128)(2,1)S(1)}, u32[]{:S(2)}, u32[]{:S(2)}) async-start(bf16[64,8,1920]{2,1,0:T(8,128)(2,1)} %bitcast.34), calls=%async_computation | async-start | bytes 3932160 | tf_op jit(solution)/shard_map/all_to_all | solution.py:432
  15.1 45.7 %collective-permute-start.2 = (bf16[384,5120]{1,0:T(8,128)(2,1)}, bf16[384,5120]{1,0:T(8,128)(2,1)}, u32[]{:S(2)}, u32[]{:S(2)}) collective-permute-start(bf16[384,5120]{1,0:T(8,128)(2,1)} %bitcast.29), channel_id=1, source_target_pairs={{0,1},{1,0},{2,3},{3,2},{4,5},{5,4},{6,7},{7,6},{8,9},{9,8},{10,11... | collective-permute-start | bytes 11796488 | tf_op jit(solution)/shard_map/ppermute | solution.py:437
  15.2 76.0 %collective-permute-start.5 = (bf16[5120,384]{1,0:T(8,128)(2,1)}, bf16[5120,384]{1,0:T(8,128)(2,1)}, u32[]{:S(2)}, u32[]{:S(2)}) collective-permute-start(bf16[5120,384]{1,0:T(8,128)(2,1)} %bitcast.21), channel_id=1, source_target_pairs={{0,1},{1,0},{2,3},{3,2},{4,5},{5,4},{6,7},{7,6},{8,9},{9,8},{10,11... | collective-permute-start | bytes 11796488 | tf_op jit(solution)/shard_map/ppermute | solution.py:437
  15.7 75.5 %collective-permute-start.6 = (bf16[5120,384]{1,0:T(8,128)(2,1)}, bf16[5120,384]{1,0:T(8,128)(2,1)}, u32[]{:S(2)}, u32[]{:S(2)}) collective-permute-start(bf16[5120,384]{1,0:T(8,128)(2,1)} %bitcast.25), channel_id=1, source_target_pairs={{0,1},{1,0},{2,3},{3,2},{4,5},{5,4},{6,7},{7,6},{8,9},{9,8},{10,11... | collective-permute-start | bytes 11796488 | tf_op jit(solution)/shard_map/ppermute | solution.py:437
  18.9 0.6 copy-start
  19.5 0.7 copy-start.2
  42.9 6.4 %copy-start.4 = (bf16[64,8,1920]{2,1,0:T(8,128)(2,1)}, bf16[64,8,1920]{2,1,0:T(8,128)(2,1)S(1)}, u32[]{:S(2)}) copy-start(bf16[64,8,1920]{2,1,0:T(8,128)(2,1)S(1)} %all-to-all-done) | copy-start | bytes 5898244
  42.9 32.5 %all-to-all-start.1 = ((bf16[64,8,1920]{2,1,0:T(8,128)(2,1)}), bf16[64,8,1920]{2,1,0:T(8,128)(2,1)}, u32[]{:S(2)}, u32[]{:S(2)}) async-start(bf16[64,8,1920]{2,1,0:T(8,128)(2,1)} %bitcast.37), calls=%async_computation.1 | async-start | bytes 3932160 | tf_op jit(solution)/shard_map/all_to_all | solution.py:432
  49.2 5.7 %collective-permute-start = (bf16[2,256,1920]{2,1,0:T(8,128)(2,1)S(1)}, bf16[2,256,1920]{2,1,0:T(8,128)(2,1)S(1)}, u32[]{:S(2)}, u32[]{:S(2)}) collective-permute-start(bf16[2,256,1920]{2,1,0:T(8,128)(2,1)S(1)} %bitcast.38), channel_id=1, source_target_pairs={{0,1},{1,0},{2,3},{3,2},{4,5},{5,4},{6,7},{7,6},{8,9},{9,8},{10,11... | collective-permute-start | bytes 5898248 | tf_op jit(solution)/shard_map/ppermute | solution.py:437
  60.3 1.7 %collective-permute-start.1 = (bf16[384,384]{1,0:T(8,128)(2,1)S(1)}, bf16[384,384]{1,0:T(8,128)(2,1)S(1)}, u32[]{:S(2)}, u32[]{:S(2)}) collective-permute-start(bf16[384,384]{1,0:T(8,128)(2,1)S(1)} %get-tuple-element.40.h_ref), channel_id=1, source_target_pairs={{0,1},{1,0},{2,3},{3,2},{4,5},{5,4},{6,7},{7,6},{8,9},{9,8},{10,11... | collective-permute-start | bytes 884744 | tf_op jit(solution)/shard_map/ppermute | solution.py:437
  75.4 32.0 %all-to-all-start.2 = ((bf16[64,8,1920]{2,1,0:T(8,128)(2,1)}), bf16[64,8,1920]{2,1,0:T(8,128)(2,1)}, u32[]{:S(2)}, u32[]{:S(2)}) async-start(bf16[64,8,1920]{2,1,0:T(8,128)(2,1)} %bitcast.33), calls=%async_computation.2 | async-start | bytes 3932160 | tf_op jit(solution)/shard_map/all_to_all | solution.py:432
  82.2 4.4 %collective-permute-start.3 = (bf16[2,256,1920]{2,1,0:T(8,128)(2,1)}, bf16[2,256,1920]{2,1,0:T(8,128)(2,1)S(1)}, u32[]{:S(2)}, u32[]{:S(2)}) collective-permute-start(bf16[2,256,1920]{2,1,0:T(8,128)(2,1)} %bitcast.5.r_ref), channel_id=1, source_target_pairs={{0,1},{1,0},{2,3},{3,2},{4,5},{5,4},{6,7},{7,6},{8,9},{9,8},{10,11... | collective-permute-start | bytes 5898248 | tf_op jit(solution)/shard_map/ppermute | solution.py:437
  90.7 2.1 %collective-permute-start.4 = (bf16[384,768]{1,0:T(8,128)(2,1)S(1)}, bf16[384,768]{1,0:T(8,128)(2,1)S(1)}, u32[]{:S(2)}, u32[]{:S(2)}) collective-permute-start(bf16[384,768]{1,0:T(8,128)(2,1)S(1)} %get-tuple-element.48.d_ref), channel_id=1, source_target_pairs={{0,1},{1,0},{2,3},{3,2},{4,5},{5,4},{6,7},{7,6},{8,9},{9,8},{10,11... | collective-permute-start | bytes 1769480 | tf_op jit(solution)/shard_map/ppermute | solution.py:437
  107.4 32.6 %all-to-all-start.3 = ((bf16[64,8,1920]{2,1,0:T(8,128)(2,1)}), bf16[64,8,1920]{2,1,0:T(8,128)(2,1)S(1)}, u32[]{:S(2)}, u32[]{:S(2)}) async-start(bf16[64,8,1920]{2,1,0:T(8,128)(2,1)} %bitcast.35), calls=%async_computation.3 | async-start | bytes 3932160 | tf_op jit(solution)/shard_map/all_to_all | solution.py:432
  117.2 1.2 collective-permute-start.7
  118.4 21.5 %collective-permute-start.8 = (f32[6,128]{1,0:T(8,128)S(1)}, f32[6,128]{1,0:T(8,128)S(1)}, u32[]{:S(2)}, u32[]{:S(2)}) collective-permute-start(f32[6,128]{1,0:T(8,128)S(1)} %add.3.inner_ref), channel_id=1, source_target_pairs={{0,2},{2,0},{1,3},{3,1},{4,6},{6,4},{5,7},{7,5},{8,10},{10,8},{9,1... | collective-permute-start | bytes 9224 | tf_op jit(solution)/shard_map/ppermute | solution.py:437
  121.6 6.8 %copy-start.3 = (bf16[384,5120]{1,0:T(8,128)(2,1)S(1)}, bf16[384,5120]{1,0:T(8,128)(2,1)}, u32[]{:S(2)}) copy-start(bf16[384,5120]{1,0:T(8,128)(2,1)} %get-tuple-element.49) | copy-start | bytes 11796484
  132.6 7.4 %copy-start.1 = (bf16[512,128]{1,0:T(8,128)(2,1)S(1)}, bf16[512,128]{1,0:T(8,128)(2,1)}, u32[]{:S(2)}) copy-start(bf16[512,128]{1,0:T(8,128)(2,1)} %copy-done) | copy-start | bytes 393220

commit v6 on v5

--- a/solution.py
+++ b/solution.py
@@ -205,12 +205,10 @@
     _pack(value.astype(BF), out_ref)
 
 
-def _grad_down_kernel(h_ref, e_ref, out_ref, t_ref):
-    @pl.when(pl.program_id(0) == 0)
-    def _():
-        t_ref[...] = h_ref[...].astype(F32).T.astype(BF)
-
-    out_ref[...] = _dot(t_ref[...], e_ref[...]).astype(BF)
+def _grad_in_kernel(x_ref, d_ref, gate_ref, up_ref):
+    x = x_ref[...]
+    gate_ref[...] = _dot_tn(x, d_ref[:, :HID]).astype(BF)
+    up_ref[...] = _dot_tn(x, d_ref[:, HID:]).astype(BF)
 
 
 def _home(pick, r_ref):
@@ -406,19 +404,18 @@
     )(core, grads, grads_p, _hbm(w_gate), _hbm(w_up), _hbm(w_gate_p), _hbm(w_up_p))
 
 
-def _grad_down(hidden, e):
-    block = pl.BlockSpec((HID, COLS), lambda i: (0, i))
+def _grad_in(x, grads):
+    block = pl.BlockSpec((COLS, HID), lambda i: (i, 0))
     return pl.pallas_call(
-        _grad_down_kernel,
+        _grad_in_kernel,
         grid=(4,),
-        in_specs=[pl.BlockSpec((ROWS, HID), lambda i: (0, 0)), pl.BlockSpec((ROWS, COLS), lambda i: (0, i))],
-        out_specs=block,
-        out_shape=_shape((HID, D), BF),
-        scratch_shapes=[pltpu.VMEM((HID, ROWS), BF)],
+        in_specs=[pl.BlockSpec((ROWS, COLS), lambda i: (0, i)), pl.BlockSpec((ROWS, 2 * HID), lambda i: (0, 0))],
+        out_specs=[block, block],
+        out_shape=[_shape((D, HID), BF), _shape((D, HID), BF)],
         compiler_params=_params(),
-        cost_estimate=_cost(2 * ROWS * D * HID, 8e6),
-        name="grad_down",
-    )(hidden, _hbm(e))
+        cost_estimate=_cost(4 * ROWS * D * HID, 13e6),
+        name="grad_in",
+    )(_hbm(x), grads)
 
 
 def _local(kernel, out_shape, flops, moved, name, *args):
@@ -469,9 +466,9 @@
     send_b = _back(core, grads, _swap(grads), wg, wu, wg_p, wu_p)
     recv_b = _exchange(send_b)
 
-    g_down = _grad_down(hidden, e)
-    g_gate = _dot_tn(x, grads[:, :HID]).astype(BF)
-    g_up = _dot_tn(x, grads[:, HID:]).astype(BF)
+    g_gate, g_up = _grad_in(x, grads)
+    hidden, e, g_gate, g_up = lax.optimization_barrier((hidden, e, g_gate, g_up))
+    g_down = _dot_tn(hidden, e).astype(BF)
 
     mixed, inner = _local(
         _mixed_kernel,

time: 142 us -> 142 us (level)
  matrix products: 10.9 us -> 4.17 us
  waiting for transfers between devices: 41.5 us -> 46.2 us
  Pallas kernels: 51.1 us -> 53.2 us
    dot_general x2 -> x1, matrix products: 10.9 us -> 4.17 us  [_dot_tn(): lax.dot_general(a, b, (((0,), (0,)), ((), ())), preferred_element_type=F32)]
    all_to_all x4, waiting for transfers between devices: 37.5 us -> 42.2 us  [_exchange(): lax.all_to_all(chunks, ('yhi', 'expert'), split_axis=0, concat_axis=0, ti...]
    pallas_call x1, Pallas kernels: 6.02 us -> 8.09 us  [_grad_in(): pl.pallas_call(_grad_in_kernel, grid=(4,), in_specs=[pl.BlockSpec((ROWS,...]
  transfers between devices with their start and end apart: 13 -> 13, of which waited for: 7 -> 7; matrix products, arithmetic and copies ran while one was open for 8% -> 3% of each run, Pallas kernels for 33% -> 35%
where the time goes in v6:
time: 142 us; the launch traced here: 141 us
  Pallas kernels  53.2 us (37%)
  waiting for transfers between devices  46.2 us (33%)
  starting transfers between devices  35.7 us (25%)
  matrix products  4.17 us (3%)
    all_to_all x4, waiting for transfers between devices, _exchange(): lax.all_to_all(chunks, ('yhi', 'expert'), split_axis=0, concat_axis=0, ti...  42.2 us
    all_to_all x4, starting transfers between devices, _exchange(): lax.all_to_all(chunks, ('yhi', 'expert'), split_axis=0, concat_axis=0, ti...  30.7 us
    pallas_call x4, Pallas kernels, _local(): pl.pallas_call(kernel, out_shape=out_shape, compiler_params=_params(), co...  11 us
    pallas_call x1, Pallas kernels, _back(): pl.pallas_call(_back_kernel, grid_spec=pltpu.PrefetchScalarGridSpec(num_s...  8.66 us
    pallas_call x1, Pallas kernels, _grad_in(): pl.pallas_call(_grad_in_kernel, grid=(4,), in_specs=[pl.BlockSpec((ROWS,...  8.09 us
    pallas_call x1, Pallas kernels, _result(): pl.pallas_call(_result_kernel, grid_spec=pltpu.PrefetchScalarGridSpec(num...  5.93 us
    pallas_call x1, Pallas kernels, _forward_own(): _half_pass(_forward_own_kernel, False, ['row', 'row'], [], [('slots', plt...  5.61 us
    pallas_call x1, Pallas kernels, _forward_other(): _half_pass(_forward_other_kernel, True, ['row', 'row'], ['hidden', 'hidde...  5.41 us
  transfers between devices with their start and end apart: 13, of which 7 were waited for; matrix products, arithmetic and copies ran while one was open for 3% of the time, Pallas kernels for 35%

profile of v6, /device:TPU:0, one launch (start us, length us, event | category | flops | bytes accessed | tf_op | source)
XLA Modules:
  0.0 141.4 jit_solution(16977270001867599480)
XLA Ops:
  0.6 3.0 %pack_rows.1 = bf16[2,256,1920]{2,1,0:T(8,128)(2,1)} custom-call(s32[6,128]{1,0:T(8,128)} %bitcast.40, bf16[128,1280]{1,0:T(8,128)(2,1)} %tok_ref.1), custom_call_target="tpu_custom_call" | custom-call | flops 200000000 | bytes 3000000 | tf_op jit(solution)/shard_map/pack_rows/pallas_call | solution.py:422
  3.6 11.5 %all-to-all-start = ((bf16[64,8,1920]{2,1,0:T(8,128)(2,1)}), bf16[64,8,1920]{2,1,0:T(8,128)(2,1)S(1)}, u32[]{:S(2)}, u32[]{:S(2)}) async-start(bf16[64,8,1920]{2,1,0:T(8,128)(2,1)} %bitcast.34), calls=%async_computation | async-start | bytes 3932160 | tf_op jit(solution)/shard_map/all_to_all | solution.py:429
  15.1 0.1 collective-permute-start.2
  15.2 0.5 collective-permute-start.5
  15.7 0.1 collective-permute-start.6
  15.8 3.1 %pack_grads.1 = (bf16[2,256,1920]{2,1,0:T(8,128)(2,1)}, bf16[512,128]{1,0:T(8,128)(2,1)S(1)}, f32[512,128]{1,0:T(8,128)S(1)}) custom-call(s32[6,128]{1,0:T(8,128)} %bitcast.41, f32[6,128]{1,0:T(8,128)} %bitcast.43, bf16[128,1280]{1,0:T(8,128)(2,1)} %cot_ref.3), custom_call_target="tpu_custom_call" | custom-call | flops 200000000 | bytes 3000000 | tf_op jit(solution)/shard_map/pack_grads/pallas_call | solution.py:422
  18.9 0.0 copy-start
  18.9 0.6 copy-done
  19.5 0.0 copy-start.2
  19.5 0.7 copy-done.2
  20.2 22.7 %all-to-all-done = bf16[64,8,1920]{2,1,0:T(8,128)(2,1)S(1)} async-done(((bf16[64,8,1920]{2,1,0:T(8,128)(2,1)}), bf16[64,8,1920]{2,1,0:T(8,128)(2,1)S(1)}, u32[]{:S(2)}, u32[]{:S(2)}) %all-to-all-start) | async-done | bytes 1966112 | tf_op jit(solution)/shard_map/all_to_all | solution.py:429
  42.9 0.0 copy-start.4
  42.9 6.3 %all-to-all-start.1 = ((bf16[64,8,1920]{2,1,0:T(8,128)(2,1)}), bf16[64,8,1920]{2,1,0:T(8,128)(2,1)}, u32[]{:S(2)}, u32[]{:S(2)}) async-start(bf16[64,8,1920]{2,1,0:T(8,128)(2,1)} %bitcast.37), calls=%async_computation.1 | async-start | bytes 3932160 | tf_op jit(solution)/shard_map/all_to_all | solution.py:429
  49.2 0.1 collective-permute-start
  49.3 0.0 copy-done.4
  49.3 5.6 %forward_own.1 = (bf16[384,5120]{1,0:T(8,128)(2,1)}, f32[384,384]{1,0:T(8,128)S(1)}, f32[384,384]{1,0:T(8,128)S(1)}) custom-call(s32[1]{0:T(128)} %bitcast.6.core_ref, bf16[2,256,1920]{2,1,0:T(8,128)(2,1)} %bitcast.39, bf16[5120,384]{1,0:T(8,128)(2,1)} %bitcast.22, bf16[5120,384]{1,0:T(8,128)(2,1)} %bitcast.26), custom_call_target="tpu_custom_call" | custom-call | flops 24159191040 | bytes 144000000 | tf_op jit(solution)/shard_map/forward_own/pallas_call | solution.py:311
  54.9 0.0 collective-permute-done.r_ref
  54.9 5.4 %forward_other.1 = (bf16[384,5120]{1,0:T(8,128)(2,1)}, f32[384,384]{1,0:T(8,128)S(1)}, f32[384,384]{1,0:T(8,128)S(1)}, bf16[384,384]{1,0:T(8,128)(2,1)S(1)}) custom-call(s32[1]{0:T(128)} %bitcast.6.core_ref, bf16[2,256,1920]{2,1,0:T(8,128)(2,1)S(1)} %collective-permute-done.r_ref, bf16[5120,384]{1,0:T(8,128)(2,1)} %bitcast.23, ...), custom_call_target="tpu_custom_call", output_to_operand_aliasing={{0}: (6, {})} | custom-call | flops 11796480 | bytes 70312 | tf_op jit(solution)/shard_map/forward_other/pallas_call | solution.py:325
  60.3 0.5 collective-permute-start.1
  60.8 0.0 collective-permute-done.2.wdp_ref
  60.8 1.2 collective-permute-done.1.hp_ref
  62.0 5.9 %result.1 = bf16[2,256,1920]{2,1,0:T(8,128)(2,1)} custom-call(s32[1]{0:T(128)} %bitcast.6.core_ref, bf16[384,384]{1,0:T(8,128)(2,1)S(1)} %get-tuple-element.61.h_ref, bf16[384,384]{1,0:T(8,128)(2,1)S(1)} %collective-permute-done.1.hp_ref, bf16[384,5120]{1,0:T(8,128)(2,1)} %bitcast.30, bf16[384,5120]{1,0:T(8,128)(2,1)} %collective-permute-done.2.wdp_ref), custom_call_target="tpu_custom_call" | custom-call | flops 11796480 | bytes 54687 | tf_op jit(solution)/shard_map/result/pallas_call | solution.py:375
  67.9 7.5 %all-to-all-done.1 = bf16[64,8,1920]{2,1,0:T(8,128)(2,1)} async-done(((bf16[64,8,1920]{2,1,0:T(8,128)(2,1)}), bf16[64,8,1920]{2,1,0:T(8,128)(2,1)}, u32[]{:S(2)}, u32[]{:S(2)}) %all-to-all-start.1) | async-done | bytes 1966112 | tf_op jit(solution)/shard_map/all_to_all | solution.py:429
  75.4 6.8 %all-to-all-start.2 = ((bf16[64,8,1920]{2,1,0:T(8,128)(2,1)}), bf16[64,8,1920]{2,1,0:T(8,128)(2,1)}, u32[]{:S(2)}, u32[]{:S(2)}) async-start(bf16[64,8,1920]{2,1,0:T(8,128)(2,1)} %bitcast.33), calls=%async_computation.2 | async-start | bytes 3932160 | tf_op jit(solution)/shard_map/all_to_all | solution.py:429
  82.2 0.1 collective-permute-start.3
  82.2 4.3 %backward_own.1 = (bf16[384,5120]{1,0:T(8,128)(2,1)}, f32[384,384]{1,0:T(8,128)S(1)}) custom-call(s32[1]{0:T(128)} %bitcast.6.core_ref, bf16[2,256,1920]{2,1,0:T(8,128)(2,1)} %bitcast.5.r_ref, bf16[384,5120]{1,0:T(8,128)(2,1)} %bitcast.31), custom_call_target="tpu_custom_call" | custom-call | flops 24159191040 | bytes 144000000 | tf_op jit(solution)/shard_map/backward_own/pallas_call | solution.py:345
  86.5 0.0 collective-permute-done.3.r_ref
  86.5 4.2 %backward_other.1 = (bf16[384,5120]{1,0:T(8,128)(2,1)}, bf16[384,768]{1,0:T(8,128)(2,1)S(1)}) custom-call(s32[1]{0:T(128)} %bitcast.6.core_ref, bf16[2,256,1920]{2,1,0:T(8,128)(2,1)S(1)} %collective-permute-done.3.r_ref, bf16[384,5120]{1,0:T(8,128)(2,1)} %bitcast.32, f32[384,384]{1,0:T(8,128)S(1)} %get-tuple-element.50.a0_ref, ...), custom_call_target="tpu_custom_call", output_to_operand_aliasing={{0}: (6, {})} | custom-call | flops 5898240 | bytes 46875 | tf_op jit(solution)/shard_map/backward_other/pallas_call | solution.py:359
  90.8 0.5 collective-permute-start.4
  91.2 0.0 collective-permute-done.5.wgp_ref
  91.2 0.0 collective-permute-done.6.wup_ref
  91.3 1.6 %collective-permute-done.4.dp_ref = bf16[384,768]{1,0:T(8,128)(2,1)S(1)} collective-permute-done((bf16[384,768]{1,0:T(8,128)(2,1)S(1)}, bf16[384,768]{1,0:T(8,128)(2,1)S(1)}, u32[]{:S(2)}, u32[]{:S(2)}) %collective-permute-start.4) | collective-permute-done | bytes 589856 | tf_op jit(solution)/shard_map/ppermute | solution.py:434
  92.9 8.7 %back.1 = bf16[2,256,1920]{2,1,0:T(8,128)(2,1)} custom-call(s32[1]{0:T(128)} %bitcast.6.core_ref, bf16[384,768]{1,0:T(8,128)(2,1)S(1)} %get-tuple-element.54.d_ref, bf16[384,768]{1,0:T(8,128)(2,1)S(1)} %collective-permute-done.4.dp_ref, bf16[5120,384]{1,0:T(8,128)(2,1)} %bitcast.24, bf16[5120,384]{1,0:T(8,128)(2,1)} %bitcast.28, ...), custom_call_target="tpu_custom_call" | custom-call | flops 23592960 | bytes 85937 | tf_op jit(solution)/shard_map/back/pallas_call | solution.py:392
  101.5 5.9 %all-to-all-done.2 = bf16[64,8,1920]{2,1,0:T(8,128)(2,1)} async-done(((bf16[64,8,1920]{2,1,0:T(8,128)(2,1)}), bf16[64,8,1920]{2,1,0:T(8,128)(2,1)}, u32[]{:S(2)}, u32[]{:S(2)}) %all-to-all-start.2) | async-done | bytes 1966112 | tf_op jit(solution)/shard_map/all_to_all | solution.py:429
  107.4 6.2 %all-to-all-start.3 = ((bf16[64,8,1920]{2,1,0:T(8,128)(2,1)}), bf16[64,8,1920]{2,1,0:T(8,128)(2,1)S(1)}, u32[]{:S(2)}, u32[]{:S(2)}) async-start(bf16[64,8,1920]{2,1,0:T(8,128)(2,1)} %bitcast.35), calls=%async_computation.3 | async-start | bytes 3932160 | tf_op jit(solution)/shard_map/all_to_all | solution.py:429
  113.6 3.6 %mixed.1 = (bf16[128,1280]{1,0:T(8,128)(2,1)}, f32[6,128]{1,0:T(8,128)S(1)}) custom-call(s32[6,128]{1,0:T(8,128)} %bitcast.42, bf16[512,128]{1,0:T(8,128)(2,1)} %copy-done, f32[512,128]{1,0:T(8,128)} %copy-done.2, bf16[128,1280]{1,0:T(8,128)(2,1)} %cot_ref.3, bf16[2,256,1920]{2,1,0:T(8,128)(2,1)} %bitcast.11.r_ref), custom_call_target="tpu_custom_call" | custom-call | flops 400000000 | bytes 3000000 | tf_op jit(solution)/shard_map/mixed/pallas_call | solution.py:422
  117.2 0.1 collective-permute-start.7
  117.3 1.2 collective-permute-done.7
  118.4 3.2 %collective-permute-start.8 = (f32[6,128]{1,0:T(8,128)S(1)}, f32[6,128]{1,0:T(8,128)S(1)}, u32[]{:S(2)}, u32[]{:S(2)}) collective-permute-start(f32[6,128]{1,0:T(8,128)S(1)} %add.3.inner_ref), channel_id=1, source_target_pairs={{0,2},{2,0},{1,3},{3,1},{4,6},{6,4},{5,7},{7,5},{8,10},{10,8},{9,1... | collective-permute-start | bytes 9224 | tf_op jit(solution)/shard_map/ppermute | solution.py:434
  121.6 0.0 copy-start.3
  121.6 8.1 %grad_in.1 = (bf16[5120,384]{1,0:T(8,128)(2,1)}, bf16[5120,384]{1,0:T(8,128)(2,1)}) custom-call(bf16[384,5120]{1,0:T(8,128)(2,1)} %get-tuple-element.56.x_ref, bf16[384,768]{1,0:T(8,128)(2,1)S(1)} %get-tuple-element.54.d_ref), custom_call_target="tpu_custom_call" | custom-call | flops 3019898880 | bytes 13000000 | tf_op jit(solution)/shard_map/grad_in/pallas_call | solution.py:409
  129.7 0.0 copy-done.3
  129.7 0.0 copy-start.1
  129.7 4.2 %convolution_convert_fusion = bf16[384,5120]{1,0:T(8,128)(2,1)} fusion(bf16[384,384]{1,0:T(8,128)(2,1)S(1)} %get-tuple-element.61.h_ref, bf16[384,5120]{1,0:T(8,128)(2,1)S(1)} %copy-done.3), kind=kOutput, calls=%fused_computation | convolution fusion | flops 1511915520 | bytes 8159232 | tf_op jit(solution)/shard_map/dot_general | solution.py:38
  133.9 6.2 %all-to-all-done.3 = bf16[64,8,1920]{2,1,0:T(8,128)(2,1)S(1)} async-done(((bf16[64,8,1920]{2,1,0:T(8,128)(2,1)}), bf16[64,8,1920]{2,1,0:T(8,128)(2,1)S(1)}, u32[]{:S(2)}, u32[]{:S(2)}) %all-to-all-start.3) | async-done | bytes 1966112 | tf_op jit(solution)/shard_map/all_to_all | solution.py:429
  140.0 0.0 collective-permute-done.8.far_ref
  140.0 0.0 copy-done.1
  140.0 1.4 grad_tokens.1
  (1 shorter events, 0.0 us)
Async XLA Ops:
  3.6 39.3 %all-to-all-start = ((bf16[64,8,1920]{2,1,0:T(8,128)(2,1)}), bf16[64,8,1920]{2,1,0:T(8,128)(2,1)S(1)}, u32[]{:S(2)}, u32[]{:S(2)}) async-start(bf16[64,8,1920]{2,1,0:T(8,128)(2,1)} %bitcast.34), calls=%async_computation | async-start | bytes 3932160 | tf_op jit(solution)/shard_map/all_to_all | solution.py:429
  15.1 45.7 %collective-permute-start.2 = (bf16[384,5120]{1,0:T(8,128)(2,1)}, bf16[384,5120]{1,0:T(8,128)(2,1)}, u32[]{:S(2)}, u32[]{:S(2)}) collective-permute-start(bf16[384,5120]{1,0:T(8,128)(2,1)} %bitcast.29), channel_id=1, source_target_pairs={{0,1},{1,0},{2,3},{3,2},{4,5},{5,4},{6,7},{7,6},{8,9},{9,8},{10,11... | collective-permute-start | bytes 11796488 | tf_op jit(solution)/shard_map/ppermute | solution.py:434
  15.2 76.0 %collective-permute-start.5 = (bf16[5120,384]{1,0:T(8,128)(2,1)}, bf16[5120,384]{1,0:T(8,128)(2,1)}, u32[]{:S(2)}, u32[]{:S(2)}) collective-permute-start(bf16[5120,384]{1,0:T(8,128)(2,1)} %bitcast.21), channel_id=1, source_target_pairs={{0,1},{1,0},{2,3},{3,2},{4,5},{5,4},{6,7},{7,6},{8,9},{9,8},{10,11... | collective-permute-start | bytes 11796488 | tf_op jit(solution)/shard_map/ppermute | solution.py:434
  15.7 75.5 %collective-permute-start.6 = (bf16[5120,384]{1,0:T(8,128)(2,1)}, bf16[5120,384]{1,0:T(8,128)(2,1)}, u32[]{:S(2)}, u32[]{:S(2)}) collective-permute-start(bf16[5120,384]{1,0:T(8,128)(2,1)} %bitcast.25), channel_id=1, source_target_pairs={{0,1},{1,0},{2,3},{3,2},{4,5},{5,4},{6,7},{7,6},{8,9},{9,8},{10,11... | collective-permute-start | bytes 11796488 | tf_op jit(solution)/shard_map/ppermute | solution.py:434
  18.9 0.6 copy-start
  19.5 0.7 copy-start.2
  42.9 6.4 %copy-start.4 = (bf16[64,8,1920]{2,1,0:T(8,128)(2,1)}, bf16[64,8,1920]{2,1,0:T(8,128)(2,1)S(1)}, u32[]{:S(2)}) copy-start(bf16[64,8,1920]{2,1,0:T(8,128)(2,1)S(1)} %all-to-all-done) | copy-start | bytes 5898244
  42.9 32.5 %all-to-all-start.1 = ((bf16[64,8,1920]{2,1,0:T(8,128)(2,1)}), bf16[64,8,1920]{2,1,0:T(8,128)(2,1)}, u32[]{:S(2)}, u32[]{:S(2)}) async-start(bf16[64,8,1920]{2,1,0:T(8,128)(2,1)} %bitcast.37), calls=%async_computation.1 | async-start | bytes 3932160 | tf_op jit(solution)/shard_map/all_to_all | solution.py:429
  49.2 5.7 %collective-permute-start = (bf16[2,256,1920]{2,1,0:T(8,128)(2,1)S(1)}, bf16[2,256,1920]{2,1,0:T(8,128)(2,1)S(1)}, u32[]{:S(2)}, u32[]{:S(2)}) collective-permute-start(bf16[2,256,1920]{2,1,0:T(8,128)(2,1)S(1)} %bitcast.38), channel_id=1, source_target_pairs={{0,1},{1,0},{2,3},{3,2},{4,5},{5,4},{6,7},{7,6},{8,9},{9,8},{10,11... | collective-permute-start | bytes 5898248 | tf_op jit(solution)/shard_map/ppermute | solution.py:434
  60.3 1.7 %collective-permute-start.1 = (bf16[384,384]{1,0:T(8,128)(2,1)S(1)}, bf16[384,384]{1,0:T(8,128)(2,1)S(1)}, u32[]{:S(2)}, u32[]{:S(2)}) collective-permute-start(bf16[384,384]{1,0:T(8,128)(2,1)S(1)} %get-tuple-element.61.h_ref), channel_id=1, source_target_pairs={{0,1},{1,0},{2,3},{3,2},{4,5},{5,4},{6,7},{7,6},{8,9},{9,8},{10,11... | collective-permute-start | bytes 884744 | tf_op jit(solution)/shard_map/ppermute | solution.py:434
  75.4 32.0 %all-to-all-start.2 = ((bf16[64,8,1920]{2,1,0:T(8,128)(2,1)}), bf16[64,8,1920]{2,1,0:T(8,128)(2,1)}, u32[]{:S(2)}, u32[]{:S(2)}) async-start(bf16[64,8,1920]{2,1,0:T(8,128)(2,1)} %bitcast.33), calls=%async_computation.2 | async-start | bytes 3932160 | tf_op jit(solution)/shard_map/all_to_all | solution.py:429
  82.2 4.4 %collective-permute-start.3 = (bf16[2,256,1920]{2,1,0:T(8,128)(2,1)}, bf16[2,256,1920]{2,1,0:T(8,128)(2,1)S(1)}, u32[]{:S(2)}, u32[]{:S(2)}) collective-permute-start(bf16[2,256,1920]{2,1,0:T(8,128)(2,1)} %bitcast.5.r_ref), channel_id=1, source_target_pairs={{0,1},{1,0},{2,3},{3,2},{4,5},{5,4},{6,7},{7,6},{8,9},{9,8},{10,11... | collective-permute-start | bytes 5898248 | tf_op jit(solution)/shard_map/ppermute | solution.py:434
  90.8 2.1 %collective-permute-start.4 = (bf16[384,768]{1,0:T(8,128)(2,1)S(1)}, bf16[384,768]{1,0:T(8,128)(2,1)S(1)}, u32[]{:S(2)}, u32[]{:S(2)}) collective-permute-start(bf16[384,768]{1,0:T(8,128)(2,1)S(1)} %get-tuple-element.54.d_ref), channel_id=1, source_target_pairs={{0,1},{1,0},{2,3},{3,2},{4,5},{5,4},{6,7},{7,6},{8,9},{9,8},{10,11... | collective-permute-start | bytes 1769480 | tf_op jit(solution)/shard_map/ppermute | solution.py:434
  107.4 32.6 %all-to-all-start.3 = ((bf16[64,8,1920]{2,1,0:T(8,128)(2,1)}), bf16[64,8,1920]{2,1,0:T(8,128)(2,1)S(1)}, u32[]{:S(2)}, u32[]{:S(2)}) async-start(bf16[64,8,1920]{2,1,0:T(8,128)(2,1)} %bitcast.35), calls=%async_computation.3 | async-start | bytes 3932160 | tf_op jit(solution)/shard_map/all_to_all | solution.py:429
  117.2 1.2 collective-permute-start.7
  118.4 21.6 %collective-permute-start.8 = (f32[6,128]{1,0:T(8,128)S(1)}, f32[6,128]{1,0:T(8,128)S(1)}, u32[]{:S(2)}, u32[]{:S(2)}) collective-permute-start(f32[6,128]{1,0:T(8,128)S(1)} %add.3.inner_ref), channel_id=1, source_target_pairs={{0,2},{2,0},{1,3},{3,1},{4,6},{6,4},{5,7},{7,5},{8,10},{10,8},{9,1... | collective-permute-start | bytes 9224 | tf_op jit(solution)/shard_map/ppermute | solution.py:434
  121.6 8.1 %copy-start.3 = (bf16[384,5120]{1,0:T(8,128)(2,1)S(1)}, bf16[384,5120]{1,0:T(8,128)(2,1)}, u32[]{:S(2)}) copy-start(bf16[384,5120]{1,0:T(8,128)(2,1)} %get-tuple-element.62) | copy-start | bytes 11796484
  129.7 10.3 %copy-start.1 = (bf16[512,128]{1,0:T(8,128)(2,1)S(1)}, bf16[512,128]{1,0:T(8,128)(2,1)}, u32[]{:S(2)}) copy-start(bf16[512,128]{1,0:T(8,128)(2,1)} %copy-done) | copy-start | bytes 393220

commit v7 on v6

--- a/solution.py
+++ b/solution.py
@@ -200,8 +200,9 @@
 
 
 def _back_kernel(core_ref, d_ref, dp_ref, wg_ref, wu_ref, wgp_ref, wup_ref, out_ref):
-    value = _dot_nt(d_ref[:, :HID], wg_ref[...]) + _dot_nt(d_ref[:, HID:], wu_ref[...])
-    value += _dot_nt(dp_ref[:, :HID], wgp_ref[...]) + _dot_nt(dp_ref[:, HID:], wup_ref[...])
+    both = jnp.concatenate([d_ref[...], dp_ref[...]], axis=1)
+    weights = jnp.concatenate([wg_ref[...], wu_ref[...], wgp_ref[...], wup_ref[...]], axis=1)
+    value = _dot_nt(both, weights)
     _pack(value.astype(BF), out_ref)
 
 

time: 142 us -> 141 us (level)
  transfers between devices with their start and end apart: 13 -> 13, of which waited for: 7 -> 7; matrix products, arithmetic and copies ran while one was open for 3% -> 3% of each run, Pallas kernels for 35% -> 34%
where the time goes in v7:
time: 141 us; the launch traced here: 140 us
  Pallas kernels  52.3 us (37%)
  waiting for transfers between devices  46.2 us (33%)
  starting transfers between devices  35.7 us (25%)
  matrix products  4.17 us (3%)
    all_to_all x4, waiting for transfers between devices, _exchange(): lax.all_to_all(chunks, ('yhi', 'expert'), split_axis=0, concat_axis=0, ti...  42.2 us
    all_to_all x4, starting transfers between devices, _exchange(): lax.all_to_all(chunks, ('yhi', 'expert'), split_axis=0, concat_axis=0, ti...  30.7 us
    pallas_call x4, Pallas kernels, _local(): pl.pallas_call(kernel, out_shape=out_shape, compiler_params=_params(), co...  11 us
    pallas_call x1, Pallas kernels, _grad_in(): pl.pallas_call(_grad_in_kernel, grid=(4,), in_specs=[pl.BlockSpec((ROWS,...  8.09 us
    pallas_call x1, Pallas kernels, _back(): pl.pallas_call(_back_kernel, grid_spec=pltpu.PrefetchScalarGridSpec(num_s...  7.7 us
    pallas_call x1, Pallas kernels, _result(): pl.pallas_call(_result_kernel, grid_spec=pltpu.PrefetchScalarGridSpec(num...  5.93 us
    pallas_call x1, Pallas kernels, _forward_own(): _half_pass(_forward_own_kernel, False, ['row', 'row'], [], [('slots', plt...  5.61 us
    pallas_call x1, Pallas kernels, _forward_other(): _half_pass(_forward_other_kernel, True, ['row', 'row'], ['hidden', 'hidde...  5.41 us
  transfers between devices with their start and end apart: 13, of which 7 were waited for; matrix products, arithmetic and copies ran while one was open for 3% of the time, Pallas kernels for 34%

profile of v7, /device:TPU:0, one launch (start us, length us, event | category | flops | bytes accessed | tf_op | source)
XLA Modules:
  0.0 140.5 jit_solution(1950405368424028165)
XLA Ops:
  0.6 3.0 %pack_rows.1 = bf16[2,256,1920]{2,1,0:T(8,128)(2,1)} custom-call(s32[6,128]{1,0:T(8,128)} %bitcast.40, bf16[128,1280]{1,0:T(8,128)(2,1)} %tok_ref.1), custom_call_target="tpu_custom_call" | custom-call | flops 200000000 | bytes 3000000 | tf_op jit(solution)/shard_map/pack_rows/pallas_call | solution.py:423
  3.6 11.5 %all-to-all-start = ((bf16[64,8,1920]{2,1,0:T(8,128)(2,1)}), bf16[64,8,1920]{2,1,0:T(8,128)(2,1)S(1)}, u32[]{:S(2)}, u32[]{:S(2)}) async-start(bf16[64,8,1920]{2,1,0:T(8,128)(2,1)} %bitcast.34), calls=%async_computation | async-start | bytes 3932160 | tf_op jit(solution)/shard_map/all_to_all | solution.py:430
  15.1 0.1 collective-permute-start.2
  15.2 0.5 collective-permute-start.5
  15.7 0.1 collective-permute-start.6
  15.8 3.1 %pack_grads.1 = (bf16[2,256,1920]{2,1,0:T(8,128)(2,1)}, bf16[512,128]{1,0:T(8,128)(2,1)S(1)}, f32[512,128]{1,0:T(8,128)S(1)}) custom-call(s32[6,128]{1,0:T(8,128)} %bitcast.41, f32[6,128]{1,0:T(8,128)} %bitcast.43, bf16[128,1280]{1,0:T(8,128)(2,1)} %cot_ref.3), custom_call_target="tpu_custom_call" | custom-call | flops 200000000 | bytes 3000000 | tf_op jit(solution)/shard_map/pack_grads/pallas_call | solution.py:423
  18.9 0.0 copy-start
  18.9 0.6 copy-done
  19.5 0.0 copy-start.2
  19.5 0.7 copy-done.2
  20.2 22.7 %all-to-all-done = bf16[64,8,1920]{2,1,0:T(8,128)(2,1)S(1)} async-done(((bf16[64,8,1920]{2,1,0:T(8,128)(2,1)}), bf16[64,8,1920]{2,1,0:T(8,128)(2,1)S(1)}, u32[]{:S(2)}, u32[]{:S(2)}) %all-to-all-start) | async-done | bytes 1966112 | tf_op jit(solution)/shard_map/all_to_all | solution.py:430
  42.9 0.0 copy-start.4
  42.9 6.3 %all-to-all-start.1 = ((bf16[64,8,1920]{2,1,0:T(8,128)(2,1)}), bf16[64,8,1920]{2,1,0:T(8,128)(2,1)}, u32[]{:S(2)}, u32[]{:S(2)}) async-start(bf16[64,8,1920]{2,1,0:T(8,128)(2,1)} %bitcast.37), calls=%async_computation.1 | async-start | bytes 3932160 | tf_op jit(solution)/shard_map/all_to_all | solution.py:430
  49.2 0.1 collective-permute-start
  49.3 0.0 copy-done.4
  49.3 5.6 %forward_own.1 = (bf16[384,5120]{1,0:T(8,128)(2,1)}, f32[384,384]{1,0:T(8,128)S(1)}, f32[384,384]{1,0:T(8,128)S(1)}) custom-call(s32[1]{0:T(128)} %bitcast.6.core_ref, bf16[2,256,1920]{2,1,0:T(8,128)(2,1)} %bitcast.39, bf16[5120,384]{1,0:T(8,128)(2,1)} %bitcast.22, bf16[5120,384]{1,0:T(8,128)(2,1)} %bitcast.26), custom_call_target="tpu_custom_call" | custom-call | flops 24159191040 | bytes 144000000 | tf_op jit(solution)/shard_map/forward_own/pallas_call | solution.py:312
  54.9 0.0 collective-permute-done.r_ref
  54.9 5.4 %forward_other.1 = (bf16[384,5120]{1,0:T(8,128)(2,1)}, f32[384,384]{1,0:T(8,128)S(1)}, f32[384,384]{1,0:T(8,128)S(1)}, bf16[384,384]{1,0:T(8,128)(2,1)S(1)}) custom-call(s32[1]{0:T(128)} %bitcast.6.core_ref, bf16[2,256,1920]{2,1,0:T(8,128)(2,1)S(1)} %collective-permute-done.r_ref, bf16[5120,384]{1,0:T(8,128)(2,1)} %bitcast.23, ...), custom_call_target="tpu_custom_call", output_to_operand_aliasing={{0}: (6, {})} | custom-call | flops 11796480 | bytes 70312 | tf_op jit(solution)/shard_map/forward_other/pallas_call | solution.py:326
  60.3 0.5 collective-permute-start.1
  60.8 0.0 collective-permute-done.2.wdp_ref
  60.8 1.2 collective-permute-done.1.hp_ref
  62.0 5.9 %result.1 = bf16[2,256,1920]{2,1,0:T(8,128)(2,1)} custom-call(s32[1]{0:T(128)} %bitcast.6.core_ref, bf16[384,384]{1,0:T(8,128)(2,1)S(1)} %get-tuple-element.61.h_ref, bf16[384,384]{1,0:T(8,128)(2,1)S(1)} %collective-permute-done.1.hp_ref, bf16[384,5120]{1,0:T(8,128)(2,1)} %bitcast.30, bf16[384,5120]{1,0:T(8,128)(2,1)} %collective-permute-done.2.wdp_ref), custom_call_target="tpu_custom_call" | custom-call | flops 11796480 | bytes 54687 | tf_op jit(solution)/shard_map/result/pallas_call | solution.py:376
  67.9 7.5 %all-to-all-done.1 = bf16[64,8,1920]{2,1,0:T(8,128)(2,1)} async-done(((bf16[64,8,1920]{2,1,0:T(8,128)(2,1)}), bf16[64,8,1920]{2,1,0:T(8,128)(2,1)}, u32[]{:S(2)}, u32[]{:S(2)}) %all-to-all-start.1) | async-done | bytes 1966112 | tf_op jit(solution)/shard_map/all_to_all | solution.py:430
  75.4 6.8 %all-to-all-start.2 = ((bf16[64,8,1920]{2,1,0:T(8,128)(2,1)}), bf16[64,8,1920]{2,1,0:T(8,128)(2,1)}, u32[]{:S(2)}, u32[]{:S(2)}) async-start(bf16[64,8,1920]{2,1,0:T(8,128)(2,1)} %bitcast.33), calls=%async_computation.2 | async-start | bytes 3932160 | tf_op jit(solution)/shard_map/all_to_all | solution.py:430
  82.2 0.1 collective-permute-start.3
  82.2 4.3 %backward_own.1 = (bf16[384,5120]{1,0:T(8,128)(2,1)}, f32[384,384]{1,0:T(8,128)S(1)}) custom-call(s32[1]{0:T(128)} %bitcast.6.core_ref, bf16[2,256,1920]{2,1,0:T(8,128)(2,1)} %bitcast.5.r_ref, bf16[384,5120]{1,0:T(8,128)(2,1)} %bitcast.31), custom_call_target="tpu_custom_call" | custom-call | flops 24159191040 | bytes 144000000 | tf_op jit(solution)/shard_map/backward_own/pallas_call | solution.py:346
  86.5 0.0 collective-permute-done.3.r_ref
  86.5 4.2 %backward_other.1 = (bf16[384,5120]{1,0:T(8,128)(2,1)}, bf16[384,768]{1,0:T(8,128)(2,1)S(1)}) custom-call(s32[1]{0:T(128)} %bitcast.6.core_ref, bf16[2,256,1920]{2,1,0:T(8,128)(2,1)S(1)} %collective-permute-done.3.r_ref, bf16[384,5120]{1,0:T(8,128)(2,1)} %bitcast.32, f32[384,384]{1,0:T(8,128)S(1)} %get-tuple-element.50.a0_ref, ...), custom_call_target="tpu_custom_call", output_to_operand_aliasing={{0}: (6, {})} | custom-call | flops 5898240 | bytes 46875 | tf_op jit(solution)/shard_map/backward_other/pallas_call | solution.py:360
  90.8 0.5 collective-permute-start.4
  91.2 0.0 collective-permute-done.5.wgp_ref
  91.2 0.0 collective-permute-done.6.wup_ref
  91.3 1.6 %collective-permute-done.4.dp_ref = bf16[384,768]{1,0:T(8,128)(2,1)S(1)} collective-permute-done((bf16[384,768]{1,0:T(8,128)(2,1)S(1)}, bf16[384,768]{1,0:T(8,128)(2,1)S(1)}, u32[]{:S(2)}, u32[]{:S(2)}) %collective-permute-start.4) | collective-permute-done | bytes 589856 | tf_op jit(solution)/shard_map/ppermute | solution.py:435
  92.9 7.7 %back.1 = bf16[2,256,1920]{2,1,0:T(8,128)(2,1)} custom-call(s32[1]{0:T(128)} %bitcast.6.core_ref, bf16[384,768]{1,0:T(8,128)(2,1)S(1)} %get-tuple-element.54.d_ref, bf16[384,768]{1,0:T(8,128)(2,1)S(1)} %collective-permute-done.4.dp_ref, bf16[5120,384]{1,0:T(8,128)(2,1)} %bitcast.24, bf16[5120,384]{1,0:T(8,128)(2,1)} %bitcast.28, ...), custom_call_target="tpu_custom_call" | custom-call | flops 23592960 | bytes 85937 | tf_op jit(solution)/shard_map/back/pallas_call | solution.py:393
  100.6 6.8 %all-to-all-done.2 = bf16[64,8,1920]{2,1,0:T(8,128)(2,1)} async-done(((bf16[64,8,1920]{2,1,0:T(8,128)(2,1)}), bf16[64,8,1920]{2,1,0:T(8,128)(2,1)}, u32[]{:S(2)}, u32[]{:S(2)}) %all-to-all-start.2) | async-done | bytes 1966112 | tf_op jit(solution)/shard_map/all_to_all | solution.py:430
  107.4 6.2 %all-to-all-start.3 = ((bf16[64,8,1920]{2,1,0:T(8,128)(2,1)}), bf16[64,8,1920]{2,1,0:T(8,128)(2,1)S(1)}, u32[]{:S(2)}, u32[]{:S(2)}) async-start(bf16[64,8,1920]{2,1,0:T(8,128)(2,1)} %bitcast.35), calls=%async_computation.3 | async-start | bytes 3932160 | tf_op jit(solution)/shard_map/all_to_all | solution.py:430
  113.6 3.6 %mixed.1 = (bf16[128,1280]{1,0:T(8,128)(2,1)}, f32[6,128]{1,0:T(8,128)S(1)}) custom-call(s32[6,128]{1,0:T(8,128)} %bitcast.42, bf16[512,128]{1,0:T(8,128)(2,1)} %copy-done, f32[512,128]{1,0:T(8,128)} %copy-done.2, bf16[128,1280]{1,0:T(8,128)(2,1)} %cot_ref.3, bf16[2,256,1920]{2,1,0:T(8,128)(2,1)} %bitcast.11.r_ref), custom_call_target="tpu_custom_call" | custom-call | flops 400000000 | bytes 3000000 | tf_op jit(solution)/shard_map/mixed/pallas_call | solution.py:423
  117.2 0.1 collective-permute-start.7
  117.3 1.2 collective-permute-done.7
  118.4 3.2 %collective-permute-start.8 = (f32[6,128]{1,0:T(8,128)S(1)}, f32[6,128]{1,0:T(8,128)S(1)}, u32[]{:S(2)}, u32[]{:S(2)}) collective-permute-start(f32[6,128]{1,0:T(8,128)S(1)} %add.3.inner_ref), channel_id=1, source_target_pairs={{0,2},{2,0},{1,3},{3,1},{4,6},{6,4},{5,7},{7,5},{8,10},{10,8},{9,1... | collective-permute-start | bytes 9224 | tf_op jit(solution)/shard_map/ppermute | solution.py:435
  121.6 0.0 copy-start.3
  121.6 8.1 %grad_in.1 = (bf16[5120,384]{1,0:T(8,128)(2,1)}, bf16[5120,384]{1,0:T(8,128)(2,1)}) custom-call(bf16[384,5120]{1,0:T(8,128)(2,1)} %get-tuple-element.56.x_ref, bf16[384,768]{1,0:T(8,128)(2,1)S(1)} %get-tuple-element.54.d_ref), custom_call_target="tpu_custom_call" | custom-call | flops 3019898880 | bytes 13000000 | tf_op jit(solution)/shard_map/grad_in/pallas_call | solution.py:410
  129.7 0.0 copy-done.3
  129.7 0.0 copy-start.1
  129.7 4.2 %convolution_convert_fusion = bf16[384,5120]{1,0:T(8,128)(2,1)} fusion(bf16[384,384]{1,0:T(8,128)(2,1)S(1)} %get-tuple-element.61.h_ref, bf16[384,5120]{1,0:T(8,128)(2,1)S(1)} %copy-done.3), kind=kOutput, calls=%fused_computation | convolution fusion | flops 1511915520 | bytes 8159232 | tf_op jit(solution)/shard_map/dot_general | solution.py:38
  133.9 5.2 %all-to-all-done.3 = bf16[64,8,1920]{2,1,0:T(8,128)(2,1)S(1)} async-done(((bf16[64,8,1920]{2,1,0:T(8,128)(2,1)}), bf16[64,8,1920]{2,1,0:T(8,128)(2,1)S(1)}, u32[]{:S(2)}, u32[]{:S(2)}) %all-to-all-start.3) | async-done | bytes 1966112 | tf_op jit(solution)/shard_map/all_to_all | solution.py:430
  139.1 0.0 collective-permute-done.8.far_ref
  139.1 0.0 copy-done.1
  139.1 1.3 grad_tokens.1
  (1 shorter events, 0.0 us)
Async XLA Ops:
  3.6 39.3 %all-to-all-start = ((bf16[64,8,1920]{2,1,0:T(8,128)(2,1)}), bf16[64,8,1920]{2,1,0:T(8,128)(2,1)S(1)}, u32[]{:S(2)}, u32[]{:S(2)}) async-start(bf16[64,8,1920]{2,1,0:T(8,128)(2,1)} %bitcast.34), calls=%async_computation | async-start | bytes 3932160 | tf_op jit(solution)/shard_map/all_to_all | solution.py:430
  15.1 45.7 %collective-permute-start.2 = (bf16[384,5120]{1,0:T(8,128)(2,1)}, bf16[384,5120]{1,0:T(8,128)(2,1)}, u32[]{:S(2)}, u32[]{:S(2)}) collective-permute-start(bf16[384,5120]{1,0:T(8,128)(2,1)} %bitcast.29), channel_id=1, source_target_pairs={{0,1},{1,0},{2,3},{3,2},{4,5},{5,4},{6,7},{7,6},{8,9},{9,8},{10,11... | collective-permute-start | bytes 11796488 | tf_op jit(solution)/shard_map/ppermute | solution.py:435
  15.2 76.0 %collective-permute-start.5 = (bf16[5120,384]{1,0:T(8,128)(2,1)}, bf16[5120,384]{1,0:T(8,128)(2,1)}, u32[]{:S(2)}, u32[]{:S(2)}) collective-permute-start(bf16[5120,384]{1,0:T(8,128)(2,1)} %bitcast.21), channel_id=1, source_target_pairs={{0,1},{1,0},{2,3},{3,2},{4,5},{5,4},{6,7},{7,6},{8,9},{9,8},{10,11... | collective-permute-start | bytes 11796488 | tf_op jit(solution)/shard_map/ppermute | solution.py:435
  15.7 75.5 %collective-permute-start.6 = (bf16[5120,384]{1,0:T(8,128)(2,1)}, bf16[5120,384]{1,0:T(8,128)(2,1)}, u32[]{:S(2)}, u32[]{:S(2)}) collective-permute-start(bf16[5120,384]{1,0:T(8,128)(2,1)} %bitcast.25), channel_id=1, source_target_pairs={{0,1},{1,0},{2,3},{3,2},{4,5},{5,4},{6,7},{7,6},{8,9},{9,8},{10,11... | collective-permute-start | bytes 11796488 | tf_op jit(solution)/shard_map/ppermute | solution.py:435
  18.9 0.6 copy-start
  19.5 0.7 copy-start.2
  42.9 6.4 %copy-start.4 = (bf16[64,8,1920]{2,1,0:T(8,128)(2,1)}, bf16[64,8,1920]{2,1,0:T(8,128)(2,1)S(1)}, u32[]{:S(2)}) copy-start(bf16[64,8,1920]{2,1,0:T(8,128)(2,1)S(1)} %all-to-all-done) | copy-start | bytes 5898244
  42.9 32.5 %all-to-all-start.1 = ((bf16[64,8,1920]{2,1,0:T(8,128)(2,1)}), bf16[64,8,1920]{2,1,0:T(8,128)(2,1)}, u32[]{:S(2)}, u32[]{:S(2)}) async-start(bf16[64,8,1920]{2,1,0:T(8,128)(2,1)} %bitcast.37), calls=%async_computation.1 | async-start | bytes 3932160 | tf_op jit(solution)/shard_map/all_to_all | solution.py:430
  49.2 5.7 %collective-permute-start = (bf16[2,256,1920]{2,1,0:T(8,128)(2,1)S(1)}, bf16[2,256,1920]{2,1,0:T(8,128)(2,1)S(1)}, u32[]{:S(2)}, u32[]{:S(2)}) collective-permute-start(bf16[2,256,1920]{2,1,0:T(8,128)(2,1)S(1)} %bitcast.38), channel_id=1, source_target_pairs={{0,1},{1,0},{2,3},{3,2},{4,5},{5,4},{6,7},{7,6},{8,9},{9,8},{10,11... | collective-permute-start | bytes 5898248 | tf_op jit(solution)/shard_map/ppermute | solution.py:435
  60.3 1.7 %collective-permute-start.1 = (bf16[384,384]{1,0:T(8,128)(2,1)S(1)}, bf16[384,384]{1,0:T(8,128)(2,1)S(1)}, u32[]{:S(2)}, u32[]{:S(2)}) collective-permute-start(bf16[384,384]{1,0:T(8,128)(2,1)S(1)} %get-tuple-element.61.h_ref), channel_id=1, source_target_pairs={{0,1},{1,0},{2,3},{3,2},{4,5},{5,4},{6,7},{7,6},{8,9},{9,8},{10,11... | collective-permute-start | bytes 884744 | tf_op jit(solution)/shard_map/ppermute | solution.py:435
  75.4 32.0 %all-to-all-start.2 = ((bf16[64,8,1920]{2,1,0:T(8,128)(2,1)}), bf16[64,8,1920]{2,1,0:T(8,128)(2,1)}, u32[]{:S(2)}, u32[]{:S(2)}) async-start(bf16[64,8,1920]{2,1,0:T(8,128)(2,1)} %bitcast.33), calls=%async_computation.2 | async-start | bytes 3932160 | tf_op jit(solution)/shard_map/all_to_all | solution.py:430
  82.2 4.4 %collective-permute-start.3 = (bf16[2,256,1920]{2,1,0:T(8,128)(2,1)}, bf16[2,256,1920]{2,1,0:T(8,128)(2,1)S(1)}, u32[]{:S(2)}, u32[]{:S(2)}) collective-permute-start(bf16[2,256,1920]{2,1,0:T(8,128)(2,1)} %bitcast.5.r_ref), channel_id=1, source_target_pairs={{0,1},{1,0},{2,3},{3,2},{4,5},{5,4},{6,7},{7,6},{8,9},{9,8},{10,11... | collective-permute-start | bytes 5898248 | tf_op jit(solution)/shard_map/ppermute | solution.py:435
  90.8 2.1 %collective-permute-start.4 = (bf16[384,768]{1,0:T(8,128)(2,1)S(1)}, bf16[384,768]{1,0:T(8,128)(2,1)S(1)}, u32[]{:S(2)}, u32[]{:S(2)}) collective-permute-start(bf16[384,768]{1,0:T(8,128)(2,1)S(1)} %get-tuple-element.54.d_ref), channel_id=1, source_target_pairs={{0,1},{1,0},{2,3},{3,2},{4,5},{5,4},{6,7},{7,6},{8,9},{9,8},{10,11... | collective-permute-start | bytes 1769480 | tf_op jit(solution)/shard_map/ppermute | solution.py:435
  107.4 31.7 %all-to-all-start.3 = ((bf16[64,8,1920]{2,1,0:T(8,128)(2,1)}), bf16[64,8,1920]{2,1,0:T(8,128)(2,1)S(1)}, u32[]{:S(2)}, u32[]{:S(2)}) async-start(bf16[64,8,1920]{2,1,0:T(8,128)(2,1)} %bitcast.35), calls=%async_computation.3 | async-start | bytes 3932160 | tf_op jit(solution)/shard_map/all_to_all | solution.py:430
  117.2 1.2 collective-permute-start.7
  118.4 20.7 %collective-permute-start.8 = (f32[6,128]{1,0:T(8,128)S(1)}, f32[6,128]{1,0:T(8,128)S(1)}, u32[]{:S(2)}, u32[]{:S(2)}) collective-permute-start(f32[6,128]{1,0:T(8,128)S(1)} %add.3.inner_ref), channel_id=1, source_target_pairs={{0,2},{2,0},{1,3},{3,1},{4,6},{6,4},{5,7},{7,5},{8,10},{10,8},{9,1... | collective-permute-start | bytes 9224 | tf_op jit(solution)/shard_map/ppermute | solution.py:435
  121.6 8.1 %copy-start.3 = (bf16[384,5120]{1,0:T(8,128)(2,1)S(1)}, bf16[384,5120]{1,0:T(8,128)(2,1)}, u32[]{:S(2)}) copy-start(bf16[384,5120]{1,0:T(8,128)(2,1)} %get-tuple-element.62) | copy-start | bytes 11796484
  129.7 9.4 %copy-start.1 = (bf16[512,128]{1,0:T(8,128)(2,1)S(1)}, bf16[512,128]{1,0:T(8,128)(2,1)}, u32[]{:S(2)}) copy-start(bf16[512,128]{1,0:T(8,128)(2,1)} %copy-done) | copy-start | bytes 393220

commit v8 on v7

--- a/solution.py
+++ b/solution.py
@@ -195,7 +195,8 @@
 
 
 def _result_kernel(core_ref, h_ref, hp_ref, wd_ref, wdp_ref, out_ref):
-    value = _dot(h_ref[...], wd_ref[...]) + _dot(hp_ref[...], wdp_ref[...])
+    both = jnp.concatenate([h_ref[...], hp_ref[...]], axis=1)
+    value = _dot(both, jnp.concatenate([wd_ref[...], wdp_ref[...]], axis=0))
     _pack(value.astype(BF), out_ref)
 
 

time: 141 us -> 141 us (level)
  no operation moved by 1% of the time
where the time goes in v8:
time: 141 us; the launch traced here: 140 us
  Pallas kernels  51.8 us (37%)
  waiting for transfers between devices  46.8 us (33%)
  starting transfers between devices  35.7 us (25%)
  matrix products  4.17 us (3%)
    all_to_all x4, waiting for transfers between devices, _exchange(): lax.all_to_all(chunks, ('yhi', 'expert'), split_axis=0, concat_axis=0, ti...  42.8 us
    all_to_all x4, starting transfers between devices, _exchange(): lax.all_to_all(chunks, ('yhi', 'expert'), split_axis=0, concat_axis=0, ti...  30.7 us
    pallas_call x4, Pallas kernels, _local(): pl.pallas_call(kernel, out_shape=out_shape, compiler_params=_params(), co...  11 us
    pallas_call x1, Pallas kernels, _grad_in(): pl.pallas_call(_grad_in_kernel, grid=(4,), in_specs=[pl.BlockSpec((ROWS,...  8.09 us
    pallas_call x1, Pallas kernels, _back(): pl.pallas_call(_back_kernel, grid_spec=pltpu.PrefetchScalarGridSpec(num_s...  7.7 us
    pallas_call x1, Pallas kernels, _forward_own(): _half_pass(_forward_own_kernel, False, ['row', 'row'], [], [('slots', plt...  5.61 us
    pallas_call x1, Pallas kernels, _result(): pl.pallas_call(_result_kernel, grid_spec=pltpu.PrefetchScalarGridSpec(num...  5.41 us
    pallas_call x1, Pallas kernels, _forward_other(): _half_pass(_forward_other_kernel, True, ['row', 'row'], ['hidden', 'hidde...  5.41 us
  transfers between devices with their start and end apart: 13, of which 7 were waited for; matrix products, arithmetic and copies ran while one was open for 3% of the time, Pallas kernels for 34%

profile of v8, /device:TPU:0, one launch (start us, length us, event | category | flops | bytes accessed | tf_op | source)
XLA Modules:
  0.0 140.5 jit_solution(16744514054835549438)
XLA Ops:
  0.6 3.0 %pack_rows.1 = bf16[2,256,1920]{2,1,0:T(8,128)(2,1)} custom-call(s32[6,128]{1,0:T(8,128)} %bitcast.40, bf16[128,1280]{1,0:T(8,128)(2,1)} %tok_ref.1), custom_call_target="tpu_custom_call" | custom-call | flops 200000000 | bytes 3000000 | tf_op jit(solution)/shard_map/pack_rows/pallas_call | solution.py:424
  3.6 11.5 %all-to-all-start = ((bf16[64,8,1920]{2,1,0:T(8,128)(2,1)}), bf16[64,8,1920]{2,1,0:T(8,128)(2,1)S(1)}, u32[]{:S(2)}, u32[]{:S(2)}) async-start(bf16[64,8,1920]{2,1,0:T(8,128)(2,1)} %bitcast.34), calls=%async_computation | async-start | bytes 3932160 | tf_op jit(solution)/shard_map/all_to_all | solution.py:431
  15.1 0.1 collective-permute-start.2
  15.2 0.5 collective-permute-start.5
  15.7 0.1 collective-permute-start.6
  15.8 3.1 %pack_grads.1 = (bf16[2,256,1920]{2,1,0:T(8,128)(2,1)}, bf16[512,128]{1,0:T(8,128)(2,1)S(1)}, f32[512,128]{1,0:T(8,128)S(1)}) custom-call(s32[6,128]{1,0:T(8,128)} %bitcast.41, f32[6,128]{1,0:T(8,128)} %bitcast.43, bf16[128,1280]{1,0:T(8,128)(2,1)} %cot_ref.3), custom_call_target="tpu_custom_call" | custom-call | flops 200000000 | bytes 3000000 | tf_op jit(solution)/shard_map/pack_grads/pallas_call | solution.py:424
  18.9 0.0 copy-start
  18.9 0.6 copy-done
  19.5 0.0 copy-start.2
  19.5 0.7 copy-done.2
  20.2 22.7 %all-to-all-done = bf16[64,8,1920]{2,1,0:T(8,128)(2,1)S(1)} async-done(((bf16[64,8,1920]{2,1,0:T(8,128)(2,1)}), bf16[64,8,1920]{2,1,0:T(8,128)(2,1)S(1)}, u32[]{:S(2)}, u32[]{:S(2)}) %all-to-all-start) | async-done | bytes 1966112 | tf_op jit(solution)/shard_map/all_to_all | solution.py:431
  42.9 0.0 copy-start.4
  42.9 6.3 %all-to-all-start.1 = ((bf16[64,8,1920]{2,1,0:T(8,128)(2,1)}), bf16[64,8,1920]{2,1,0:T(8,128)(2,1)}, u32[]{:S(2)}, u32[]{:S(2)}) async-start(bf16[64,8,1920]{2,1,0:T(8,128)(2,1)} %bitcast.37), calls=%async_computation.1 | async-start | bytes 3932160 | tf_op jit(solution)/shard_map/all_to_all | solution.py:431
  49.2 0.1 collective-permute-start
  49.3 0.0 copy-done.4
  49.3 5.6 %forward_own.1 = (bf16[384,5120]{1,0:T(8,128)(2,1)}, f32[384,384]{1,0:T(8,128)S(1)}, f32[384,384]{1,0:T(8,128)S(1)}) custom-call(s32[1]{0:T(128)} %bitcast.6.core_ref, bf16[2,256,1920]{2,1,0:T(8,128)(2,1)} %bitcast.39, bf16[5120,384]{1,0:T(8,128)(2,1)} %bitcast.22, bf16[5120,384]{1,0:T(8,128)(2,1)} %bitcast.26), custom_call_target="tpu_custom_call" | custom-call | flops 24159191040 | bytes 144000000 | tf_op jit(solution)/shard_map/forward_own/pallas_call | solution.py:313
  54.9 0.0 collective-permute-done.r_ref
  54.9 5.4 %forward_other.1 = (bf16[384,5120]{1,0:T(8,128)(2,1)}, f32[384,384]{1,0:T(8,128)S(1)}, f32[384,384]{1,0:T(8,128)S(1)}, bf16[384,384]{1,0:T(8,128)(2,1)S(1)}) custom-call(s32[1]{0:T(128)} %bitcast.6.core_ref, bf16[2,256,1920]{2,1,0:T(8,128)(2,1)S(1)} %collective-permute-done.r_ref, bf16[5120,384]{1,0:T(8,128)(2,1)} %bitcast.23, ...), custom_call_target="tpu_custom_call", output_to_operand_aliasing={{0}: (6, {})} | custom-call | flops 11796480 | bytes 70312 | tf_op jit(solution)/shard_map/forward_other/pallas_call | solution.py:327
  60.3 0.5 collective-permute-start.1
  60.8 0.0 collective-permute-done.2.wdp_ref
  60.8 1.2 collective-permute-done.1.hp_ref
  62.0 5.4 %result.1 = bf16[2,256,1920]{2,1,0:T(8,128)(2,1)} custom-call(s32[1]{0:T(128)} %bitcast.6.core_ref, bf16[384,384]{1,0:T(8,128)(2,1)S(1)} %get-tuple-element.61.h_ref, bf16[384,384]{1,0:T(8,128)(2,1)S(1)} %collective-permute-done.1.hp_ref, bf16[384,5120]{1,0:T(8,128)(2,1)} %bitcast.30, bf16[384,5120]{1,0:T(8,128)(2,1)} %collective-permute-done.2.wdp_ref), custom_call_target="tpu_custom_call" | custom-call | flops 11796480 | bytes 54687 | tf_op jit(solution)/shard_map/result/pallas_call | solution.py:377
  67.4 8.0 %all-to-all-done.1 = bf16[64,8,1920]{2,1,0:T(8,128)(2,1)} async-done(((bf16[64,8,1920]{2,1,0:T(8,128)(2,1)}), bf16[64,8,1920]{2,1,0:T(8,128)(2,1)}, u32[]{:S(2)}, u32[]{:S(2)}) %all-to-all-start.1) | async-done | bytes 1966112 | tf_op jit(solution)/shard_map/all_to_all | solution.py:431
  75.4 6.8 %all-to-all-start.2 = ((bf16[64,8,1920]{2,1,0:T(8,128)(2,1)}), bf16[64,8,1920]{2,1,0:T(8,128)(2,1)}, u32[]{:S(2)}, u32[]{:S(2)}) async-start(bf16[64,8,1920]{2,1,0:T(8,128)(2,1)} %bitcast.33), calls=%async_computation.2 | async-start | bytes 3932160 | tf_op jit(solution)/shard_map/all_to_all | solution.py:431
  82.2 0.1 collective-permute-start.3
  82.2 4.3 %backward_own.1 = (bf16[384,5120]{1,0:T(8,128)(2,1)}, f32[384,384]{1,0:T(8,128)S(1)}) custom-call(s32[1]{0:T(128)} %bitcast.6.core_ref, bf16[2,256,1920]{2,1,0:T(8,128)(2,1)} %bitcast.5.r_ref, bf16[384,5120]{1,0:T(8,128)(2,1)} %bitcast.31), custom_call_target="tpu_custom_call" | custom-call | flops 24159191040 | bytes 144000000 | tf_op jit(solution)/shard_map/backward_own/pallas_call | solution.py:347
  86.5 0.0 collective-permute-done.3.r_ref
  86.5 4.2 %backward_other.1 = (bf16[384,5120]{1,0:T(8,128)(2,1)}, bf16[384,768]{1,0:T(8,128)(2,1)S(1)}) custom-call(s32[1]{0:T(128)} %bitcast.6.core_ref, bf16[2,256,1920]{2,1,0:T(8,128)(2,1)S(1)} %collective-permute-done.3.r_ref, bf16[384,5120]{1,0:T(8,128)(2,1)} %bitcast.32, f32[384,384]{1,0:T(8,128)S(1)} %get-tuple-element.50.a0_ref, ...), custom_call_target="tpu_custom_call", output_to_operand_aliasing={{0}: (6, {})} | custom-call | flops 5898240 | bytes 46875 | tf_op jit(solution)/shard_map/backward_other/pallas_call | solution.py:361
  90.8 0.5 collective-permute-start.4
  91.2 0.0 collective-permute-done.5.wgp_ref
  91.2 0.0 collective-permute-done.6.wup_ref
  91.3 1.6 %collective-permute-done.4.dp_ref = bf16[384,768]{1,0:T(8,128)(2,1)S(1)} collective-permute-done((bf16[384,768]{1,0:T(8,128)(2,1)S(1)}, bf16[384,768]{1,0:T(8,128)(2,1)S(1)}, u32[]{:S(2)}, u32[]{:S(2)}) %collective-permute-start.4) | collective-permute-done | bytes 589856 | tf_op jit(solution)/shard_map/ppermute | solution.py:436
  92.9 7.7 %back.1 = bf16[2,256,1920]{2,1,0:T(8,128)(2,1)} custom-call(s32[1]{0:T(128)} %bitcast.6.core_ref, bf16[384,768]{1,0:T(8,128)(2,1)S(1)} %get-tuple-element.54.d_ref, bf16[384,768]{1,0:T(8,128)(2,1)S(1)} %collective-permute-done.4.dp_ref, bf16[5120,384]{1,0:T(8,128)(2,1)} %bitcast.24, bf16[5120,384]{1,0:T(8,128)(2,1)} %bitcast.28, ...), custom_call_target="tpu_custom_call" | custom-call | flops 23592960 | bytes 85937 | tf_op jit(solution)/shard_map/back/pallas_call | solution.py:394
  100.6 6.8 %all-to-all-done.2 = bf16[64,8,1920]{2,1,0:T(8,128)(2,1)} async-done(((bf16[64,8,1920]{2,1,0:T(8,128)(2,1)}), bf16[64,8,1920]{2,1,0:T(8,128)(2,1)}, u32[]{:S(2)}, u32[]{:S(2)}) %all-to-all-start.2) | async-done | bytes 1966112 | tf_op jit(solution)/shard_map/all_to_all | solution.py:431
  107.4 6.2 %all-to-all-start.3 = ((bf16[64,8,1920]{2,1,0:T(8,128)(2,1)}), bf16[64,8,1920]{2,1,0:T(8,128)(2,1)S(1)}, u32[]{:S(2)}, u32[]{:S(2)}) async-start(bf16[64,8,1920]{2,1,0:T(8,128)(2,1)} %bitcast.35), calls=%async_computation.3 | async-start | bytes 3932160 | tf_op jit(solution)/shard_map/all_to_all | solution.py:431
  113.6 3.6 %mixed.1 = (bf16[128,1280]{1,0:T(8,128)(2,1)}, f32[6,128]{1,0:T(8,128)S(1)}) custom-call(s32[6,128]{1,0:T(8,128)} %bitcast.42, bf16[512,128]{1,0:T(8,128)(2,1)} %copy-done, f32[512,128]{1,0:T(8,128)} %copy-done.2, bf16[128,1280]{1,0:T(8,128)(2,1)} %cot_ref.3, bf16[2,256,1920]{2,1,0:T(8,128)(2,1)} %bitcast.11.r_ref), custom_call_target="tpu_custom_call" | custom-call | flops 400000000 | bytes 3000000 | tf_op jit(solution)/shard_map/mixed/pallas_call | solution.py:424
  117.2 0.1 collective-permute-start.7
  117.3 1.2 collective-permute-done.7
  118.4 3.2 %collective-permute-start.8 = (f32[6,128]{1,0:T(8,128)S(1)}, f32[6,128]{1,0:T(8,128)S(1)}, u32[]{:S(2)}, u32[]{:S(2)}) collective-permute-start(f32[6,128]{1,0:T(8,128)S(1)} %add.3.inner_ref), channel_id=1, source_target_pairs={{0,2},{2,0},{1,3},{3,1},{4,6},{6,4},{5,7},{7,5},{8,10},{10,8},{9,1... | collective-permute-start | bytes 9224 | tf_op jit(solution)/shard_map/ppermute | solution.py:436
  121.6 0.0 copy-start.3
  121.6 8.1 %grad_in.1 = (bf16[5120,384]{1,0:T(8,128)(2,1)}, bf16[5120,384]{1,0:T(8,128)(2,1)}) custom-call(bf16[384,5120]{1,0:T(8,128)(2,1)} %get-tuple-element.56.x_ref, bf16[384,768]{1,0:T(8,128)(2,1)S(1)} %get-tuple-element.54.d_ref), custom_call_target="tpu_custom_call" | custom-call | flops 3019898880 | bytes 13000000 | tf_op jit(solution)/shard_map/grad_in/pallas_call | solution.py:411
  129.7 0.0 copy-done.3
  129.7 0.0 copy-start.1
  129.7 4.2 %convolution_convert_fusion = bf16[384,5120]{1,0:T(8,128)(2,1)} fusion(bf16[384,384]{1,0:T(8,128)(2,1)S(1)} %get-tuple-element.61.h_ref, bf16[384,5120]{1,0:T(8,128)(2,1)S(1)} %copy-done.3), kind=kOutput, calls=%fused_computation | convolution fusion | flops 1511915520 | bytes 8159232 | tf_op jit(solution)/shard_map/dot_general | solution.py:38
  133.9 5.2 %all-to-all-done.3 = bf16[64,8,1920]{2,1,0:T(8,128)(2,1)S(1)} async-done(((bf16[64,8,1920]{2,1,0:T(8,128)(2,1)}), bf16[64,8,1920]{2,1,0:T(8,128)(2,1)S(1)}, u32[]{:S(2)}, u32[]{:S(2)}) %all-to-all-start.3) | async-done | bytes 1966112 | tf_op jit(solution)/shard_map/all_to_all | solution.py:431
  139.1 0.0 collective-permute-done.8.far_ref
  139.1 0.0 copy-done.1
  139.1 1.3 grad_tokens.1
  (1 shorter events, 0.0 us)
Async XLA Ops:
  3.6 39.3 %all-to-all-start = ((bf16[64,8,1920]{2,1,0:T(8,128)(2,1)}), bf16[64,8,1920]{2,1,0:T(8,128)(2,1)S(1)}, u32[]{:S(2)}, u32[]{:S(2)}) async-start(bf16[64,8,1920]{2,1,0:T(8,128)(2,1)} %bitcast.34), calls=%async_computation | async-start | bytes 3932160 | tf_op jit(solution)/shard_map/all_to_all | solution.py:431
  15.1 45.7 %collective-permute-start.2 = (bf16[384,5120]{1,0:T(8,128)(2,1)}, bf16[384,5120]{1,0:T(8,128)(2,1)}, u32[]{:S(2)}, u32[]{:S(2)}) collective-permute-start(bf16[384,5120]{1,0:T(8,128)(2,1)} %bitcast.29), channel_id=1, source_target_pairs={{0,1},{1,0},{2,3},{3,2},{4,5},{5,4},{6,7},{7,6},{8,9},{9,8},{10,11... | collective-permute-start | bytes 11796488 | tf_op jit(solution)/shard_map/ppermute | solution.py:436
  15.2 76.0 %collective-permute-start.5 = (bf16[5120,384]{1,0:T(8,128)(2,1)}, bf16[5120,384]{1,0:T(8,128)(2,1)}, u32[]{:S(2)}, u32[]{:S(2)}) collective-permute-start(bf16[5120,384]{1,0:T(8,128)(2,1)} %bitcast.21), channel_id=1, source_target_pairs={{0,1},{1,0},{2,3},{3,2},{4,5},{5,4},{6,7},{7,6},{8,9},{9,8},{10,11... | collective-permute-start | bytes 11796488 | tf_op jit(solution)/shard_map/ppermute | solution.py:436
  15.7 75.5 %collective-permute-start.6 = (bf16[5120,384]{1,0:T(8,128)(2,1)}, bf16[5120,384]{1,0:T(8,128)(2,1)}, u32[]{:S(2)}, u32[]{:S(2)}) collective-permute-start(bf16[5120,384]{1,0:T(8,128)(2,1)} %bitcast.25), channel_id=1, source_target_pairs={{0,1},{1,0},{2,3},{3,2},{4,5},{5,4},{6,7},{7,6},{8,9},{9,8},{10,11... | collective-permute-start | bytes 11796488 | tf_op jit(solution)/shard_map/ppermute | solution.py:436
  18.9 0.6 copy-start
  19.5 0.7 copy-start.2
  42.9 6.4 %copy-start.4 = (bf16[64,8,1920]{2,1,0:T(8,128)(2,1)}, bf16[64,8,1920]{2,1,0:T(8,128)(2,1)S(1)}, u32[]{:S(2)}) copy-start(bf16[64,8,1920]{2,1,0:T(8,128)(2,1)S(1)} %all-to-all-done) | copy-start | bytes 5898244
  42.9 32.5 %all-to-all-start.1 = ((bf16[64,8,1920]{2,1,0:T(8,128)(2,1)}), bf16[64,8,1920]{2,1,0:T(8,128)(2,1)}, u32[]{:S(2)}, u32[]{:S(2)}) async-start(bf16[64,8,1920]{2,1,0:T(8,128)(2,1)} %bitcast.37), calls=%async_computation.1 | async-start | bytes 3932160 | tf_op jit(solution)/shard_map/all_to_all | solution.py:431
  49.2 5.7 %collective-permute-start = (bf16[2,256,1920]{2,1,0:T(8,128)(2,1)S(1)}, bf16[2,256,1920]{2,1,0:T(8,128)(2,1)S(1)}, u32[]{:S(2)}, u32[]{:S(2)}) collective-permute-start(bf16[2,256,1920]{2,1,0:T(8,128)(2,1)S(1)} %bitcast.38), channel_id=1, source_target_pairs={{0,1},{1,0},{2,3},{3,2},{4,5},{5,4},{6,7},{7,6},{8,9},{9,8},{10,11... | collective-permute-start | bytes 5898248 | tf_op jit(solution)/shard_map/ppermute | solution.py:436
  60.3 1.7 %collective-permute-start.1 = (bf16[384,384]{1,0:T(8,128)(2,1)S(1)}, bf16[384,384]{1,0:T(8,128)(2,1)S(1)}, u32[]{:S(2)}, u32[]{:S(2)}) collective-permute-start(bf16[384,384]{1,0:T(8,128)(2,1)S(1)} %get-tuple-element.61.h_ref), channel_id=1, source_target_pairs={{0,1},{1,0},{2,3},{3,2},{4,5},{5,4},{6,7},{7,6},{8,9},{9,8},{10,11... | collective-permute-start | bytes 884744 | tf_op jit(solution)/shard_map/ppermute | solution.py:436
  75.4 32.0 %all-to-all-start.2 = ((bf16[64,8,1920]{2,1,0:T(8,128)(2,1)}), bf16[64,8,1920]{2,1,0:T(8,128)(2,1)}, u32[]{:S(2)}, u32[]{:S(2)}) async-start(bf16[64,8,1920]{2,1,0:T(8,128)(2,1)} %bitcast.33), calls=%async_computation.2 | async-start | bytes 3932160 | tf_op jit(solution)/shard_map/all_to_all | solution.py:431
  82.2 4.4 %collective-permute-start.3 = (bf16[2,256,1920]{2,1,0:T(8,128)(2,1)}, bf16[2,256,1920]{2,1,0:T(8,128)(2,1)S(1)}, u32[]{:S(2)}, u32[]{:S(2)}) collective-permute-start(bf16[2,256,1920]{2,1,0:T(8,128)(2,1)} %bitcast.5.r_ref), channel_id=1, source_target_pairs={{0,1},{1,0},{2,3},{3,2},{4,5},{5,4},{6,7},{7,6},{8,9},{9,8},{10,11... | collective-permute-start | bytes 5898248 | tf_op jit(solution)/shard_map/ppermute | solution.py:436
  90.8 2.1 %collective-permute-start.4 = (bf16[384,768]{1,0:T(8,128)(2,1)S(1)}, bf16[384,768]{1,0:T(8,128)(2,1)S(1)}, u32[]{:S(2)}, u32[]{:S(2)}) collective-permute-start(bf16[384,768]{1,0:T(8,128)(2,1)S(1)} %get-tuple-element.54.d_ref), channel_id=1, source_target_pairs={{0,1},{1,0},{2,3},{3,2},{4,5},{5,4},{6,7},{7,6},{8,9},{9,8},{10,11... | collective-permute-start | bytes 1769480 | tf_op jit(solution)/shard_map/ppermute | solution.py:436
  107.4 31.7 %all-to-all-start.3 = ((bf16[64,8,1920]{2,1,0:T(8,128)(2,1)}), bf16[64,8,1920]{2,1,0:T(8,128)(2,1)S(1)}, u32[]{:S(2)}, u32[]{:S(2)}) async-start(bf16[64,8,1920]{2,1,0:T(8,128)(2,1)} %bitcast.35), calls=%async_computation.3 | async-start | bytes 3932160 | tf_op jit(solution)/shard_map/all_to_all | solution.py:431
  117.2 1.2 collective-permute-start.7
  118.4 20.7 %collective-permute-start.8 = (f32[6,128]{1,0:T(8,128)S(1)}, f32[6,128]{1,0:T(8,128)S(1)}, u32[]{:S(2)}, u32[]{:S(2)}) collective-permute-start(f32[6,128]{1,0:T(8,128)S(1)} %add.3.inner_ref), channel_id=1, source_target_pairs={{0,2},{2,0},{1,3},{3,1},{4,6},{6,4},{5,7},{7,5},{8,10},{10,8},{9,1... | collective-permute-start | bytes 9224 | tf_op jit(solution)/shard_map/ppermute | solution.py:436
  121.6 8.1 %copy-start.3 = (bf16[384,5120]{1,0:T(8,128)(2,1)S(1)}, bf16[384,5120]{1,0:T(8,128)(2,1)}, u32[]{:S(2)}) copy-start(bf16[384,5120]{1,0:T(8,128)(2,1)} %get-tuple-element.62) | copy-start | bytes 11796484
  129.7 9.4 %copy-start.1 = (bf16[512,128]{1,0:T(8,128)(2,1)S(1)}, bf16[512,128]{1,0:T(8,128)(2,1)}, u32[]{:S(2)}) copy-start(bf16[512,128]{1,0:T(8,128)(2,1)} %copy-done) | copy-start | bytes 393220
